TPU v7x, 32 devices: a whole 2x2x4 slice. The times are simulated.
32 devices in a mesh: blk: 8 (over y, x, core), aux: 4 (over z).
Axes of the slice: x: 2, y: 2, z: 4, core: 2. Of those that a mesh axis runs over, the one named last changes fastest.
Arguments:
- occupied_integrals: float32 [8, 128, 3072], P(None, 'blk', 'aux'), may hold values from -6 to 6
- virtual_coefficients: float32 [128, 384], replicated, may hold values from -0.0625 to 0.0625
- shell_size: int32 [16], replicated, may hold values from 1 to 8, as said below
- shell_owner: int32 [16], replicated, may hold values from 0 to 7, as said below
- occ_owner: int32 [8], replicated, may hold values from 0 to 7, each once
- e_occ: float32 [8], replicated, may hold values from -1.5 to -0.4
- e_virt: float32 [384], replicated, may hold values from 0.3 to 2.5
Outputs:
- density: float32 [8, 384, 3072], P('blk', None, 'aux')
Inputs may be any that keep to these rules, and one draw needn't show every extreme that they name: `shell_size`: every shell holds 1 to 8 functions; the shells of one blk index hold at most 16 together, and those of some blk index exactly 16. `shell_owner`: every blk index owns exactly 2 shells. `occ_owner`: each orbital appears once.
All inputs are finite; a program needn't handle non-finite values.
Results may differ from a plain program's by a relative error of at most 0.0003.
Values sent between devices are 32-bit elements; how exact they have to be, the bound alone decides.
No kernel may reach another device: no remote copies, remote signals or barrier semaphores. Data moves between devices by JAX's collectives and lax.ppermute only.
A program may use at most 64 MiB of HBM per device.

v0:
```python
import jax
import jax.numpy as jnp
from jax import lax
from jax.sharding import PartitionSpec as P

STOPS = 3


def shifted(value, axis, steps):
    count = lax.axis_size(axis)
    pairs = [(source, (source + steps) % count) for source in range(count)]
    return lax.ppermute(value, axis, pairs)


def per_device(
    occupied_integrals, virtual_coefficients, shell_size, shell_owner, occ_owner, e_occ, e_virt
):
    blk_count = lax.axis_size("blk")
    occ_total = occupied_integrals.shape[0]
    slot_cap = occupied_integrals.shape[1]
    aux_width = occupied_integrals.shape[2]
    virt_count = virtual_coefficients.shape[1]
    occ_local = occ_total // blk_count
    pair_rows = occ_local * virt_count
    highest = lax.Precision.HIGHEST
    owner_hits = (shell_owner[:, None] == jnp.arange(blk_count, dtype=jnp.int32)[None, :]).astype(
        jnp.int32
    )
    slot_load = jnp.sum(shell_size[:, None] * owner_hits, axis=0)
    live_mask = (jnp.arange(slot_cap, dtype=jnp.int32)[None, :] < slot_load[:, None]).astype(
        jnp.float32
    )
    masked_coef = (
        virtual_coefficients.reshape(blk_count, slot_cap, virt_count) * live_mask[:, :, None]
    )
    grouped = jnp.take(occupied_integrals, occ_owner, axis=0).reshape(
        blk_count, occ_local, slot_cap, aux_width
    )
    owned = jnp.einsum(
        "dnkq,dkv->nvq",
        lax.all_to_all(grouped, "blk", split_axis=0, concat_axis=0, tiled=True),
        masked_coef,
        precision=highest,
    )
    own_block = owned.reshape(pair_rows, aux_width)
    my_index = lax.axis_index("blk")
    block_energy = jnp.take(e_occ, occ_owner).reshape(blk_count, occ_local)
    own_energy = lax.dynamic_index_in_dim(block_energy, my_index, 0, keepdims=False)
    partners = [own_block]
    partner_energies = [own_energy]
    passing = own_block
    for stop in range(1, STOPS):
        passing = shifted(passing, "blk", 1)
        partners.append(passing)
        partner_index = jnp.mod(my_index - stop, blk_count)
        partner_energies.append(
            lax.dynamic_index_in_dim(block_energy, partner_index, 0, keepdims=False)
        )
    density = jnp.zeros((pair_rows, aux_width), jnp.float32)
    for stop in range(STOPS):
        pair_ints = jnp.einsum("rq,cq->rc", own_block, partners[stop], precision=highest)
        pair_ints = pair_ints.reshape(occ_local, virt_count, occ_local, virt_count)
        summed = lax.psum(2.0 * pair_ints - pair_ints.transpose(0, 3, 2, 1), "aux")
        amplitudes = (
            summed
            / (
                own_energy[:, None, None, None]
                + partner_energies[stop][None, None, :, None]
                - e_virt[None, :, None, None]
                - e_virt[None, None, None, :]
            )
        ).reshape(pair_rows, pair_rows)
        density = density + jnp.dot(amplitudes, partners[stop], precision=highest)
    return density.reshape(occ_local, virt_count, aux_width)


def solution(mesh):
    in_specs = (P(None, "blk", "aux"), P(), P(), P(), P(), P(), P())
    out_specs = P("blk", None, "aux")
    return jax.shard_map(
        per_device, mesh=mesh, in_specs=in_specs, out_specs=out_specs, check_vma=False
    )
```

profile of v0, /device:TPU:0, one launch (start us, length us, event | category | flops | bytes accessed | tf_op | source)
XLA Modules:
  0.0 157.3 jit_solution(16350391824992542416)
XLA Ops:
  6.5 0.7 compare_select_fusion
  7.3 0.3 copy-done
  7.5 0.6 gather_fusion
  8.1 0.0 copy-start.7
  8.2 1.3 gather_fusion.1
  9.5 0.8 bitcast_select_fusion
  10.4 5.2 %all-to-all-start = ((f32[8,1,16,768]{3,2,1,0:T(8,128)}), f32[8,1,16,768]{3,2,1,0:T(8,128)S(1)}, u32[]{:S(2)}, u32[]{:S(2)}) async-start(f32[8,1,16,768]{3,2,1,0:T(8,128)} %bitcast_select_fusion), calls=%async_computation | async-start | bytes 786432 | tf_op jit(solution)/shard_map/all_to_all | solution.py:41
  15.5 0.0 all-reduce.3.cloned.1.call-start
  15.6 0.1 select_reduce_fusion
  15.7 0.1 fusion.18
  15.8 0.1 reshape.239
  15.9 0.1 broadcast_multiply_fusion
  16.0 7.9 %all-to-all-done = f32[8,1,16,768]{3,2,1,0:T(8,128)S(1)} async-done(((f32[8,1,16,768]{3,2,1,0:T(8,128)}), f32[8,1,16,768]{3,2,1,0:T(8,128)S(1)}, u32[]{:S(2)}, u32[]{:S(2)}) %all-to-all-start) | async-done | bytes 393248 | tf_op jit(solution)/shard_map/all_to_all | solution.py:41
  23.9 1.1 convolution_bitcast_fusion
  25.0 0.1 collective-permute-start
  25.1 16.5 %collective-permute-done = f32[384,768]{1,0:T(8,128)S(1)} collective-permute-done((f32[384,768]{1,0:T(8,128)S(1)}, f32[384,768]{1,0:T(8,128)S(1)}, u32[]{:S(2)}, u32[]{:S(2)}) %collective-permute-start) | collective-permute-done | bytes 1179680 | tf_op jit(solution)/shard_map/ppermute | solution.py:12
  41.6 2.1 %fusion.20 = f32[384,384]{1,0:T(8,128)S(1)} fusion(f32[384,768]{1,0:T(8,128)S(1)} %convolution_bitcast_fusion), kind=kOutput, calls=%fused_computation.40 | convolution fusion | flops 1358954496 | bytes 1769472 | tf_op jit(solution)/shard_map/rq,cq->rc/dot_general | solution.py:61
  43.7 1.1 copy.17
  44.7 1.9 %bitcast_subtract_fusion.2 = f32[1,384,1,384]{1,3,2,0:T(8,128)} fusion(f32[384,384]{1,0:T(8,128)S(1)} %fusion.20, f32[384,384]{0,1:T(8,128)} %copy.17), kind=kLoop, calls=%fused_computation.8 | loop fusion | flops 294912 | bytes 1769472 | tf_op jit(solution)/shard_map/sub | solution.py:63
  46.7 2.1 %fusion.21 = f32[384,384]{1,0:T(8,128)S(1)} fusion(f32[384,768]{1,0:T(8,128)S(1)} %convolution_bitcast_fusion, f32[384,768]{1,0:T(8,128)S(1)} %collective-permute-done), kind=kOutput, calls=%fused_computation.41 | convolution fusion | flops 1358954496 | bytes 2949120 | tf_op jit(solution)/shard_map/rq,cq->rc/dot_general | solution.py:61
  48.7 1.0 copy.18
  49.8 1.9 %bitcast_subtract_fusion.1 = f32[1,384,1,384]{1,3,2,0:T(8,128)} fusion(f32[384,384]{1,0:T(8,128)S(1)} %fusion.21, f32[384,384]{0,1:T(8,128)} %copy.18), kind=kLoop, calls=%fused_computation.7 | loop fusion | flops 294912 | bytes 1769472 | tf_op jit(solution)/shard_map/sub | solution.py:63
  51.7 6.5 %collective-permute-done.1 = f32[384,768]{1,0:T(8,128)} collective-permute-done((f32[384,768]{1,0:T(8,128)S(1)}, f32[384,768]{1,0:T(8,128)}, u32[]{:S(2)}, u32[]{:S(2)}) %collective-permute-start.1) | collective-permute-done | bytes 1179680 | tf_op jit(solution)/shard_map/ppermute | solution.py:12
  58.2 3.3 %fusion.22 = f32[384,384]{1,0:T(8,128)S(1)} fusion(f32[384,768]{1,0:T(8,128)S(1)} %convolution_bitcast_fusion, f32[384,768]{1,0:T(8,128)} %collective-permute-done.1), kind=kOutput, calls=%fused_computation.42 | convolution fusion | flops 1358954496 | bytes 2949120 | tf_op jit(solution)/shard_map/rq,cq->rc/dot_general | solution.py:61
  61.6 1.0 copy.19
  62.6 1.9 %bitcast_subtract_fusion = f32[1,384,1,384]{1,3,2,0:T(8,128)} fusion(f32[384,384]{1,0:T(8,128)S(1)} %fusion.22, f32[384,384]{0,1:T(8,128)} %copy.19), kind=kLoop, calls=%fused_computation.6 | loop fusion | flops 294912 | bytes 1769472 | tf_op jit(solution)/shard_map/sub | solution.py:63
  64.5 0.0 all-reduce.3.cloned.1.call-update
  64.6 0.7 fusion.19
  68.8 71.6 %all-reduce.3.cloned.1.call-done = (f32[1,384,1,384]{1,3,2,0:T(8,128)}, f32[1,384,1,384]{1,3,2,0:T(8,128)}, f32[1,384,1,384]{1,3,2,0:T(8,128)}) async-done(((f32[1,384,1,384]{1,3,2,0:T(8,128)}, f32[1,384,1,384]{1,3,2,0:T(8,128)}, f32[1,384,1,384]{1,3,2,0:T(8,128)}), (f32[1,384,1,384]{1,3,2,0:T(8,128)}, f32[1,384,1,384]{1,3,2,0:T(8,128)}, f32[1,384,1,384]{1,3,2,0:T(8,128)})) %all-reduce.3.cloned.1.call-update) | async-done | bytes 1769488 | tf_op jit(solution)/shard_map/psum | solution.py:63
  140.4 3.3 %fusion.3 = f32[384,768]{1,0:T(8,128)S(1)} fusion(f32[384,768]{1,0:T(8,128)S(1)} %convolution_bitcast_fusion, f32[1,384,1,384]{1,3,2,0:T(8,128)} %get-tuple-element.5, f32[384]{0:T(512)S(1)} %copy-done.4, f32[384]{0:T(512)S(1)} %get-tuple-element.11), kind=kOutput, calls=%fused_computation.11 | convolution fusion | flops 1359249408 | bytes 2952192 | tf_op jit(solution)/shard_map/dot_general | solution.py:73
  143.7 2.2 %convolution_add_fusion.1 = f32[384,768]{1,0:T(8,128)S(1)} fusion(f32[384,768]{1,0:T(8,128)S(1)} %fusion.3, f32[384,768]{1,0:T(8,128)S(1)} %collective-permute-done, f32[1,384,1,384]{1,3,2,0:T(8,128)S(1)} %copy-done.2, f32[384]{0:T(512)S(1)} %get-tuple-element.12, f32[384]{0:T(512)S(1)} %copy-done.4), kind=kOutput, calls=%fused_computation.3 | convolution fusion | flops 1359544320 | bytes 4131840 | tf_op jit(solution)/shard_map/dot_general | solution.py:73
  146.0 4.5 %fusion = f32[1,384,768]{2,1,0:T(8,128)} fusion(f32[384,768]{1,0:T(8,128)S(1)} %convolution_add_fusion.1, f32[384,768]{1,0:T(8,128)} %collective-permute-done.1, f32[1,384,1,384]{1,3,2,0:T(8,128)S(1)} %copy-done.1, f32[384]{0:T(512)S(1)} %get-tuple-element.10, f32[384]{0:T(512)S(1)} %copy-done.4), kind=kOutput, calls=%fused_computation.4 | convolution fusion | flops 1359544320 | bytes 4131840 | tf_op jit(solution)/shard_map/dot_general | solution.py:73
  (18 shorter events, 0.1 us)
Async XLA Ops:
  6.5 1.0 copy-start
  6.5 3.0 %copy-start.5 = (s32[8]{0:T(128)S(1)}, s32[8]{0:T(128)}, u32[]{:S(2)}) copy-start(s32[8]{0:T(128)} %param.11) | copy-start | bytes 100
  8.1 7.5 %copy-start.6 = (s32[16]{0:T(128)S(1)}, s32[16]{0:T(128)}, u32[]{:S(2)}) copy-start(s32[16]{0:T(128)} %param.9) | copy-start | bytes 196
  8.1 7.5 %copy-start.7 = (s32[16]{0:T(128)S(1)}, s32[16]{0:T(128)}, u32[]{:S(2)}) copy-start(s32[16]{0:T(128)} %param.10) | copy-start | bytes 196
  8.2 7.7 %copy-start.3 = (f32[128,384]{1,0:T(8,128)S(1)}, f32[128,384]{1,0:T(8,128)}, u32[]{:S(2)}) copy-start(f32[128,384]{1,0:T(8,128)} %param.8) | copy-start | bytes 589828
  10.4 13.5 %all-to-all-start = ((f32[8,1,16,768]{3,2,1,0:T(8,128)}), f32[8,1,16,768]{3,2,1,0:T(8,128)S(1)}, u32[]{:S(2)}, u32[]{:S(2)}) async-start(f32[8,1,16,768]{3,2,1,0:T(8,128)} %bitcast_select_fusion), calls=%async_computation | async-start | bytes 786432 | tf_op jit(solution)/shard_map/all_to_all | solution.py:41
  15.5 124.8 %all-reduce.3.cloned.1.call-start = ((), (), s32[]{:S(2)}) async-start(), calls=%async_computation.1 | async-start | bytes 3538944 | tf_op jit(solution)/shard_map/psum | solution.py:63
  25.0 16.6 %collective-permute-start = (f32[384,768]{1,0:T(8,128)S(1)}, f32[384,768]{1,0:T(8,128)S(1)}, u32[]{:S(2)}, u32[]{:S(2)}) collective-permute-start(f32[384,768]{1,0:T(8,128)S(1)} %convolution_bitcast_fusion), channel_id=1, source_target_pairs={{0,4},{4,8},{8,12},{12,16},{16,20},{20,24},{24,28},{28,0},{1,5},{5... | collective-permute-start | bytes 3538952 | tf_op jit(solution)/shard_map/ppermute | solution.py:12
  41.6 16.6 %collective-permute-start.1 = (f32[384,768]{1,0:T(8,128)S(1)}, f32[384,768]{1,0:T(8,128)}, u32[]{:S(2)}, u32[]{:S(2)}) collective-permute-start(f32[384,768]{1,0:T(8,128)S(1)} %collective-permute-done), channel_id=1, source_target_pairs={{0,4},{4,8},{8,12},{12,16},{16,20},{20,24},{24,28},{28,0},{1,5},{5... | collective-permute-start | bytes 3538952 | tf_op jit(solution)/shard_map/ppermute | solution.py:12
  64.5 4.3 %copy-start.4 = (f32[384]{0:T(512)S(1)}, f32[384]{0:T(512)}, u32[]{:S(2)}) copy-start(f32[384]{0:T(512)} %param.13) | copy-start | bytes 4612
  140.4 3.3 %copy-start.2 = (f32[1,384,1,384]{1,3,2,0:T(8,128)S(1)}, f32[1,384,1,384]{1,3,2,0:T(8,128)}, u32[]{:S(2)}) copy-start(f32[1,384,1,384]{1,3,2,0:T(8,128)} %get-tuple-element.6) | copy-start | bytes 1769476
  143.7 2.2 %copy-start.1 = (f32[1,384,1,384]{1,3,2,0:T(8,128)S(1)}, f32[1,384,1,384]{1,3,2,0:T(8,128)}, u32[]{:S(2)}) copy-start(f32[1,384,1,384]{1,3,2,0:T(8,128)} %get-tuple-element.7) | copy-start | bytes 1769476
Sparse Core Ops, SparseCore 0:
  64.7 75.6 all-reduce.2
where the time goes:
time: 158 us; the launch traced here: 157 us
  waiting for transfers between devices  103 us (65%)
  matrix products  18.6 us (12%)
  between operations  17.1 us (11%)
  other arithmetic  7.68 us (5%)
  local copies, waits for them, and re-layouts  6.1 us (4%)
  starting transfers between devices  5.27 us (3%)
    psum x1, waiting for transfers between devices, per_device(): summed = lax.psum(2.0 * pair_ints - pair_ints.transpose(0, 3, 2, 1), 'aux')  71.6 us
    ppermute x2, waiting for transfers between devices, shifted(): return lax.ppermute(value, axis, pairs)  23 us
    dot_general x3, matrix products, per_device(): density = density + jnp.dot(amplitudes, partners[stop], precision=highest)  10 us
    all_to_all x1, waiting for transfers between devices, per_device(): lax.all_to_all(grouped, 'blk', split_axis=0, concat_axis=0, tiled=True)  7.91 us
    dot_general x3, matrix products, per_device(): jnp.einsum('rq,cq->rc', own_block, partners[stop], precision=highest)  7.44 us
    sub x3, other arithmetic, per_device(): summed = lax.psum(2.0 * pair_ints - pair_ints.transpose(0, 3, 2, 1), 'aux')  5.8 us
    all_to_all x1, starting transfers between devices, per_device(): lax.all_to_all(grouped, 'blk', split_axis=0, concat_axis=0, tiled=True)  5.17 us
  transfers between devices with their start and end apart: 4, of which 4 were waited for; matrix products, arithmetic and copies ran while one was open for 7% of the time, Pallas kernels for 0%

commit v1 on v0

--- a/solution.py
+++ b/solution.py
@@ -1,9 +1,15 @@
+import functools
+
 import jax
 import jax.numpy as jnp
 from jax import lax
+from jax.experimental import pallas as pl
+from jax.experimental.pallas import tpu as pltpu
 from jax.sharding import PartitionSpec as P
 
 STOPS = 3
+BF16 = jnp.bfloat16
+F32 = jnp.float32
 
 
 def shifted(value, axis, steps):
@@ -12,7 +18,15 @@
     return lax.ppermute(value, axis, pairs)
 
 
-def per_device(
+def live_slots(shell_size, shell_owner, blk_count, slot_cap):
+    owner_hits = (shell_owner[:, None] == jnp.arange(blk_count, dtype=jnp.int32)[None, :]).astype(
+        jnp.int32
+    )
+    slot_load = jnp.sum(shell_size[:, None] * owner_hits, axis=0)
+    return (jnp.arange(slot_cap, dtype=jnp.int32)[None, :] < slot_load[:, None]).astype(F32)
+
+
+def transformed_first(
     occupied_integrals, virtual_coefficients, shell_size, shell_owner, occ_owner, e_occ, e_virt
 ):
     blk_count = lax.axis_size("blk")
@@ -23,13 +37,7 @@
     occ_local = occ_total // blk_count
     pair_rows = occ_local * virt_count
     highest = lax.Precision.HIGHEST
-    owner_hits = (shell_owner[:, None] == jnp.arange(blk_count, dtype=jnp.int32)[None, :]).astype(
-        jnp.int32
-    )
-    slot_load = jnp.sum(shell_size[:, None] * owner_hits, axis=0)
-    live_mask = (jnp.arange(slot_cap, dtype=jnp.int32)[None, :] < slot_load[:, None]).astype(
-        jnp.float32
-    )
+    live_mask = live_slots(shell_size, shell_owner, blk_count, slot_cap)
     masked_coef = (
         virtual_coefficients.reshape(blk_count, slot_cap, virt_count) * live_mask[:, :, None]
     )
@@ -56,7 +64,7 @@
         partner_energies.append(
             lax.dynamic_index_in_dim(block_energy, partner_index, 0, keepdims=False)
         )
-    density = jnp.zeros((pair_rows, aux_width), jnp.float32)
+    density = jnp.zeros((pair_rows, aux_width), F32)
     for stop in range(STOPS):
         pair_ints = jnp.einsum("rq,cq->rc", own_block, partners[stop], precision=highest)
         pair_ints = pair_ints.reshape(occ_local, virt_count, occ_local, virt_count)
@@ -74,6 +82,194 @@
     return density.reshape(occ_local, virt_count, aux_width)
 
 
+def halves(value):
+    high = value.astype(BF16)
+    return high, (value - high.astype(F32)).astype(BF16)
+
+
+def matmul(a, b):
+    return jnp.dot(a, b, preferred_element_type=F32)
+
+
+def matmul_nt(a, b):
+    return lax.dot_general(a, b, (((1,), (1,)), ((), ())), preferred_element_type=F32)
+
+
+def coefficient_kernel(coef_ref, left_ref, right_ref, back_ref):
+    coef = coef_ref[...]
+    high, low = halves(coef)
+    right_ref[...] = jnp.concatenate([high, low, high], axis=0)
+    turned = coef.T
+    high, low = halves(turned)
+    left_ref[...] = jnp.concatenate([high, high, low], axis=1)
+    back_ref[...] = jnp.concatenate([high, low], axis=1)
+
+
+def overlap_kernel(parts, slot_cap, place_ref, *refs):
+    pieces = refs[: -parts - 3]
+    outs = refs[-parts - 3 : -3]
+    x_high, x_low, total = refs[-3:]
+    first = place_ref[0]
+    for stop in range(STOPS):
+        for index, piece in enumerate(pieces):
+            high, low = halves(piece[first + stop])
+            rows = pl.ds((stop * len(pieces) + index) * slot_cap, slot_cap)
+            x_high[rows, :] = high
+            x_low[rows, :] = low
+    slots = slot_cap * len(pieces)
+    own_high, own_low = x_high[:slots, :], x_low[:slots, :]
+    for stop in range(STOPS):
+        rows = pl.ds(stop * slots, slots)
+        high = x_high[rows, :]
+        gram = (
+            matmul_nt(own_high, high)
+            + matmul_nt(own_high, x_low[rows, :])
+            + matmul_nt(own_low, high)
+        )
+        if stop > 0:
+            gram = 2.0 * gram - gram.T
+        total[:, rows] = gram
+    share = slots // parts
+    for step, out in enumerate(outs):
+        row = pl.multiple_of(lax.rem(place_ref[1] + step, parts) * share, share)
+        out[...] = total[pl.ds(row, share), :]
+
+
+def density_kernel(parts, place_ref, energy_ref, *refs):
+    shares = refs[:parts]
+    e_row, e_col, left, right, back, x_high, x_low, out, total, w_high, w_low = refs[parts:]
+    slots = total.shape[0]
+    share = slots // parts
+    for step, piece in enumerate(shares):
+        row = pl.multiple_of(lax.rem(place_ref[1] + parts - step, parts) * share, share)
+        total[pl.ds(row, share), :] = piece[...]
+    high, low = halves(total[...])
+    half_done = matmul(left[...], jnp.concatenate([high, low, high], axis=0))
+    for stop in range(STOPS):
+        cols = pl.ds(stop * slots, slots)
+        high, low = halves(half_done[:, stop * slots : (stop + 1) * slots])
+        summed = matmul(jnp.concatenate([high, high, low], axis=1), right[...])
+        gap = (energy_ref[0] + energy_ref[stop] - e_col[...]) - e_row[...]
+        high, low = halves(summed / gap)
+        both = matmul(high, back[...])
+        weight = both[:, :slots] + both[:, slots:] + matmul(low, back[:, :slots])
+        w_high[:, cols], w_low[:, cols] = halves(weight)
+    out[...] = (
+        matmul(w_high[...], x_high[...])
+        + matmul(w_high[...], x_low[...])
+        + matmul(w_low[...], x_high[...])
+    )
+
+
+def slots_first(
+    occupied_integrals, virtual_coefficients, shell_size, shell_owner, occ_owner, e_occ, e_virt
+):
+    blk_count = lax.axis_size("blk")
+    parts = lax.axis_size("aux")
+    _, slot_cap, aux_width = occupied_integrals.shape
+    slots, virt_count = virtual_coefficients.shape
+    chips = blk_count // 2
+    my_index = lax.axis_index("blk")
+    my_chip, my_core = my_index // 2, my_index % 2
+    vmem = pl.BlockSpec(memory_space=pltpu.VMEM)
+    smem = pl.BlockSpec(memory_space=pltpu.SMEM)
+
+    def other(chip, step):
+        return chip ^ step if chips & (chips - 1) == 0 else (chip + step) % chips
+
+    def source(chip, step):
+        return chip ^ step if chips & (chips - 1) == 0 else (chip + chips - step) % chips
+
+    window = jnp.arange(STOPS + 1, dtype=jnp.int32)
+
+    def wanted(chip):
+        rows = jnp.mod(2 * chip + 1 - window, blk_count)
+        return jnp.take(occupied_integrals, jnp.take(occ_owner, rows), axis=0)
+
+    pieces, owners = [], []
+    for step in range(chips):
+        piece = wanted(other(my_chip, step))
+        if step > 0:
+            pairs = [
+                (2 * chip + core, 2 * other(chip, step) + core)
+                for chip in range(chips)
+                for core in range(2)
+            ]
+            piece = lax.ppermute(piece, "blk", pairs)
+        swapped = lax.ppermute(piece, "blk", [(i, i ^ 1) for i in range(blk_count)])
+        pieces += [piece, swapped]
+        owner = 2 * source(my_chip, step)
+        owners += [owner + my_core, owner + 1 - my_core]
+    owners = jnp.stack(owners)
+
+    live_mask = live_slots(shell_size, shell_owner, blk_count, slot_cap)
+    coef = virtual_coefficients.reshape(blk_count, slot_cap, virt_count) * live_mask[:, :, None]
+    coef = jnp.take(coef, owners, axis=0).reshape(slots, virt_count)
+    left, right, back = pl.pallas_call(
+        coefficient_kernel,
+        out_shape=[
+            jax.ShapeDtypeStruct((virt_count, 3 * slots), BF16),
+            jax.ShapeDtypeStruct((3 * slots, virt_count), BF16),
+            jax.ShapeDtypeStruct((virt_count, 2 * slots), BF16),
+        ],
+        in_specs=[vmem],
+        out_specs=[vmem] * 3,
+    )(coef)
+
+    stops = jnp.arange(STOPS, dtype=jnp.int32)
+    energies = jnp.take(e_occ, jnp.take(occ_owner, jnp.mod(my_index - stops, blk_count)))
+    place = jnp.stack([1 - my_core, lax.axis_index("aux")]).astype(jnp.int32)
+
+    share = slots // parts
+    *shares, x_high, x_low = pl.pallas_call(
+        functools.partial(overlap_kernel, parts, slot_cap),
+        out_shape=[jax.ShapeDtypeStruct((share, STOPS * slots), F32)] * parts
+        + [jax.ShapeDtypeStruct((STOPS * slots, aux_width), BF16)] * 2,
+        in_specs=[smem] + [vmem] * len(pieces),
+        out_specs=[vmem] * (parts + 2),
+        scratch_shapes=[pltpu.VMEM((slots, STOPS * slots), F32)],
+    )(place, *pieces)
+
+    mine = shares[0]
+    for step in range(1, parts):
+        mine = mine + shifted(shares[step], "aux", step)
+    gathered = [mine] + [shifted(mine, "aux", step) for step in range(1, parts)]
+
+    density = pl.pallas_call(
+        functools.partial(density_kernel, parts),
+        out_shape=jax.ShapeDtypeStruct((virt_count, aux_width), F32),
+        in_specs=[smem, smem] + [vmem] * (parts + 7),
+        out_specs=vmem,
+        scratch_shapes=[
+            pltpu.VMEM((slots, STOPS * slots), F32),
+            pltpu.VMEM((virt_count, STOPS * slots), BF16),
+            pltpu.VMEM((virt_count, STOPS * slots), BF16),
+        ],
+        compiler_params=pltpu.CompilerParams(vmem_limit_bytes=32 * 1024 * 1024),
+    )(
+        place,
+        energies,
+        *gathered,
+        e_virt.reshape(1, virt_count),
+        e_virt.reshape(virt_count, 1),
+        left,
+        right,
+        back,
+        x_high,
+        x_low,
+    )
+    return density.reshape(1, virt_count, aux_width)
+
+
+def per_device(occupied_integrals, virtual_coefficients, *rest):
+    blk_count = lax.axis_size("blk")
+    slots, virt_count = virtual_coefficients.shape
+    paired = blk_count % 2 == 0 and blk_count == occupied_integrals.shape[0]
+    shared = slots % (lax.axis_size("aux") * 16) == 0 and slots <= virt_count
+    run = slots_first if paired and shared else transformed_first
+    return run(occupied_integrals, virtual_coefficients, *rest)
+
+
 def solution(mesh):
     in_specs = (P(None, "blk", "aux"), P(), P(), P(), P(), P(), P())
     out_specs = P("blk", None, "aux")

time: 158 us -> 51.3 us (0.32)
  waiting for transfers between devices: 103 us -> 11.7 us
  matrix products: 18.6 us -> 0 us
  between operations: 17.1 us -> 0.42 us
  Pallas kernels: 0 us -> 9.47 us
  starting transfers between devices: 5.27 us -> 14.5 us
  local copies, waits for them, and re-layouts: 6.1 us -> 11.8 us
  other arithmetic: 7.68 us -> 3.11 us
    psum x1 -> x0, waiting for transfers between devices: 71.6 us -> none  [per_device(): summed = lax.psum(2.0 * pair_ints - pair_ints.transpose(0, 3, 2, 1), 'aux')]
    dot_general x7 -> x0, matrix products: 18.6 us -> none  [the longest x3 10 us: per_device(): density = density + jnp.dot(amplitudes, partners[stop], precision=highest)]
    ppermute x2 -> x6, waiting for transfers between devices: 23 us -> 5.68 us  [shifted(): return lax.ppermute(value, axis, pairs)]
    pallas_call x0 -> x3, Pallas kernels: none -> 9.47 us  [the longest x1 4.5 us: slots_first(): pl.pallas_call(functools.partial(density_kernel, parts), out_shape=jax.Sh...]
    ppermute x2 -> x6, starting transfers between devices: 0.06 us -> 9.25 us  [shifted(): return lax.ppermute(value, axis, pairs)]
    all_to_all x1 -> x0, waiting for transfers between devices: 7.91 us -> none  [per_device(): lax.all_to_all(grouped, 'blk', split_axis=0, concat_axis=0, tiled=True)]
    ppermute x0 -> x7, waiting for transfers between devices: none -> 5.99 us  [the longest x3 4.86 us: slots_first(): piece = lax.ppermute(piece, 'blk', pairs)]
    sub x4 -> x0, other arithmetic: 5.81 us -> none  [the longest x3 5.8 us: per_device(): summed = lax.psum(2.0 * pair_ints - pair_ints.transpose(0, 3, 2, 1), 'aux')]
  transfers between devices with their start and end apart: 4 -> 13, of which waited for: 4 -> 7; matrix products, arithmetic and copies ran while one was open for 7% -> 16% of each run, Pallas kernels for 0% -> 4%
where the time goes in v1:
time: 51.3 us; the launch traced here: 50.9 us
  starting transfers between devices  14.5 us (28%)
  local copies, waits for them, and re-layouts  11.8 us (23%)
  waiting for transfers between devices  11.7 us (23%)
  Pallas kernels  9.47 us (18%)
  other arithmetic  3.11 us (6%)
    ppermute x6, starting transfers between devices, shifted(): return lax.ppermute(value, axis, pairs)  9.25 us
    ppermute x6, waiting for transfers between devices, shifted(): return lax.ppermute(value, axis, pairs)  5.68 us
    gather x8, local copies, waits for them, and re-layouts, wanted(): return jnp.take(occupied_integrals, jnp.take(occ_owner, rows), axis=0)  5.51 us
    ppermute x3, waiting for transfers between devices, slots_first(): piece = lax.ppermute(piece, 'blk', pairs)  4.86 us
    pallas_call x1, Pallas kernels, slots_first(): pl.pallas_call(functools.partial(density_kernel, parts), out_shape=jax.Sh...  4.5 us
    ppermute x3, starting transfers between devices, slots_first(): piece = lax.ppermute(piece, 'blk', pairs)  4.23 us
    unnamed x42, local copies, waits for them, and re-layouts  3.96 us
    pallas_call x1, Pallas kernels, slots_first(): pl.pallas_call(functools.partial(overlap_kernel, parts, slot_cap), out_sh...  3.09 us
  transfers between devices with their start and end apart: 13, of which 7 were waited for; matrix products, arithmetic and copies ran while one was open for 16% of the time, Pallas kernels for 4%

profile of v1, /device:TPU:0, one launch (start us, length us, event | category | flops | bytes accessed | tf_op | source)
XLA Modules:
  0.0 50.9 jit_solution(1112541604888588047)
XLA Ops:
  0.0 1.3 %gather_fusion.3 = s32[4]{0:T(128)S(1)} fusion(s32[8]{0:T(128)} %param.15, s32[1024]{0:T(1024)S(1)} %pad_clamp_fusion.8), kind=kCustom, calls=%fused_computation.clone | custom fusion | bytes 48 | tf_op jit(solution)/shard_map/jit(_take)/gather | solution.py:187
  1.4 0.6 %gather_fusion.4 = f32[4,16,768]{2,1,0:T(8,128)S(1)} fusion(f32[8,16,768]{2,1,0:T(8,128)S(1)} %copy-done, s32[1024]{0:T(1024)S(1)} %pad_clamp_fusion.7), kind=kCustom, calls=%fused_computation.1.clone | custom fusion | bytes 393232 | tf_op jit(solution)/shard_map/jit(_take)/gather | solution.py:187
  2.6 0.6 %gather_fusion.5 = s32[4]{0:T(128)S(1)} fusion(s32[8]{0:T(128)S(1)} %copy-done.7, s32[1024]{0:T(1024)S(1)} %pad_clamp_fusion.6), kind=kCustom, calls=%fused_computation.2.clone | custom fusion | bytes 48 | tf_op jit(solution)/shard_map/jit(_take)/gather | solution.py:187
  3.3 0.6 %gather_fusion.6 = f32[4,16,768]{2,1,0:T(8,128)S(1)} fusion(f32[8,16,768]{2,1,0:T(8,128)S(1)} %copy-done, s32[1024]{0:T(1024)S(1)} %pad_clamp_fusion.5), kind=kCustom, calls=%fused_computation.5.clone | custom fusion | bytes 393232 | tf_op jit(solution)/shard_map/jit(_take)/gather | solution.py:187
  4.0 2.6 %collective-permute-start.1 = (f32[4,16,768]{2,1,0:T(8,128)S(1)}, f32[4,16,768]{2,1,0:T(8,128)S(1)}, u32[]{:S(2)}, u32[]{:S(2)}) collective-permute-start(f32[4,16,768]{2,1,0:T(8,128)S(1)} %broadcast_select_fusion.2), channel_id=1, source_target_pairs={{0,8},{4,12},{8,0},{12,4},{16,24},{20,28},{24,16},{28,20},{1,9},{5... | collective-permute-start | bytes 589832 | tf_op jit(solution)/shard_map/ppermute | solution.py:198
  6.6 0.6 %gather_fusion.7 = s32[4]{0:T(128)S(1)} fusion(s32[8]{0:T(128)S(1)} %copy-done.7, s32[1024]{0:T(1024)S(1)} %pad_clamp_fusion.4), kind=kCustom, calls=%fused_computation.3.clone | custom fusion | bytes 48 | tf_op jit(solution)/shard_map/jit(_take)/gather | solution.py:187
  7.3 0.6 %gather_fusion.8 = f32[4,16,768]{2,1,0:T(8,128)S(1)} fusion(f32[8,16,768]{2,1,0:T(8,128)S(1)} %copy-done, s32[1024]{0:T(1024)S(1)} %pad_clamp_fusion.3), kind=kCustom, calls=%fused_computation.6.clone | custom fusion | bytes 393232 | tf_op jit(solution)/shard_map/jit(_take)/gather | solution.py:187
  8.0 1.6 %collective-permute-start.3 = (f32[4,16,768]{2,1,0:T(8,128)S(1)}, f32[4,16,768]{2,1,0:T(8,128)S(1)}, u32[]{:S(2)}, u32[]{:S(2)}) collective-permute-start(f32[4,16,768]{2,1,0:T(8,128)S(1)} %broadcast_select_fusion.1), channel_id=1, source_target_pairs={{0,16},{4,20},{8,24},{12,28},{16,0},{20,4},{24,8},{28,12},{1,17},{... | collective-permute-start | bytes 589832 | tf_op jit(solution)/shard_map/ppermute | solution.py:198
  9.6 0.6 %gather_fusion.9 = s32[4]{0:T(128)S(1)} fusion(s32[8]{0:T(128)S(1)} %copy-done.7, s32[1024]{0:T(1024)S(1)} %pad_clamp_fusion.2), kind=kCustom, calls=%fused_computation.4.clone | custom fusion | bytes 48 | tf_op jit(solution)/shard_map/jit(_take)/gather | solution.py:187
  10.2 0.6 %gather_fusion.10 = f32[4,16,768]{2,1,0:T(8,128)S(1)} fusion(f32[8,16,768]{2,1,0:T(8,128)S(1)} %copy-done, s32[1024]{0:T(1024)S(1)} %pad_clamp_fusion.1), kind=kCustom, calls=%fused_computation.7.clone | custom fusion | bytes 393232 | tf_op jit(solution)/shard_map/jit(_take)/gather | solution.py:187
  11.4 0.6 %gather_fusion = s32[3]{0:T(128)S(1)} fusion(s32[8]{0:T(128)S(1)} %copy-done.7, s32[1024]{0:T(1024)S(1)} %pad_clamp_fusion.10), kind=kCustom, calls=%fused_computation.8 | custom fusion | bytes 36 | tf_op jit(solution)/shard_map/jit(_take)/gather | solution.py:220
  12.3 0.7 %pad_add_fusion.place_ref = s32[2]{0:T(128)} fusion(s32[1]{0:T(128)} %bitcast.1, s32[1]{0:T(128)} %bitcast), kind=kLoop, calls=%fused_computation.85 | loop fusion | flops 2 | bytes 16 | tf_op jit(solution)/shard_map/stack | solution.py:221
  13.6 0.8 %bitcast_select_fusion.coef_ref = f32[128,384]{1,0:T(8,128)} fusion(f32[8,16,384]{2,1,0:T(8,128)S(1)} %gather_fusion.2, pred[128]{0:T(512)(128)(4,1)S(1)} %broadcast_in_dim.37), kind=kLoop, calls=%fused_computation.11 | loop fusion | flops 49152 | bytes 393344 | tf_op jit(solution)/shard_map/jit(_take)/select_n | solution.py:207
  14.4 4.9 %collective-permute-done.3.refs_4_ = f32[4,16,768]{2,1,0:T(8,128)S(1)} collective-permute-done((f32[4,16,768]{2,1,0:T(8,128)S(1)}, f32[4,16,768]{2,1,0:T(8,128)S(1)}, u32[]{:S(2)}, u32[]{:S(2)}) %collective-permute-start.3) | collective-permute-done | bytes 196640 | tf_op jit(solution)/shard_map/ppermute | solution.py:198
  19.8 0.8 %collective-permute-done.4.refs_5_ = f32[4,16,768]{2,1,0:T(8,128)S(1)} collective-permute-done((f32[4,16,768]{2,1,0:T(8,128)S(1)}, f32[4,16,768]{2,1,0:T(8,128)S(1)}, u32[]{:S(2)}, u32[]{:S(2)}) %collective-permute-start.4) | collective-permute-done | bytes 196640 | tf_op jit(solution)/shard_map/ppermute | solution.py:199
  21.4 0.7 %copy-done.17 = f32[4,16,768]{2,1,0:T(8,128)} copy-done((f32[4,16,768]{2,1,0:T(8,128)}, f32[4,16,768]{2,1,0:T(8,128)S(1)}, u32[]{:S(2)}) %copy-start.17) | copy-done | bytes 196632
  22.0 3.1 %shard_map.73 = (f32[32,384]{1,0:T(8,128)}, f32[32,384]{1,0:T(8,128)}, f32[32,384]{1,0:T(8,128)}, f32[32,384]{1,0:T(8,128)}, bf16[384,768]{1,0:T(8,128)(2,1)}, /*index=5*/bf16[384,768]{1,0:T(8,128)(2,1)}) custom-call(s32[2]{0:T(128)} %pad_add_fusion.place_ref, f32[4,16,768]{2,1,0:T(8,128)} %copy-done.9, f32[4,16,768]{2,1,0:T(8,128)} %copy-done.11, ...), custom_call_target="tpu_custom_call" | custom-call | tf_op jit(solution)/shard_map/pallas_call | solution.py:224
  25.1 1.6 %collective-permute-start.7 = (f32[32,384]{1,0:T(8,128)}, f32[32,384]{1,0:T(8,128)S(1)}, u32[]{:S(2)}, u32[]{:S(2)}) collective-permute-start(f32[32,384]{1,0:T(8,128)} %get-tuple-element.17), channel_id=1, source_target_pairs={{0,1},{1,2},{2,3},{3,0},{4,5},{5,6},{6,7},{7,4},{8,9},{9,10},{10,1... | collective-permute-start | bytes 147464 | tf_op jit(solution)/shard_map/ppermute | solution.py:18
  26.8 2.6 %collective-permute-start.8 = (f32[32,384]{1,0:T(8,128)}, f32[32,384]{1,0:T(8,128)S(1)}, u32[]{:S(2)}, u32[]{:S(2)}) collective-permute-start(f32[32,384]{1,0:T(8,128)} %get-tuple-element.18), channel_id=1, source_target_pairs={{0,2},{1,3},{2,0},{3,1},{4,6},{5,7},{6,4},{7,5},{8,10},{9,11},{10,... | collective-permute-start | bytes 147464 | tf_op jit(solution)/shard_map/ppermute | solution.py:18
  29.4 1.3 %collective-permute-start.9 = (f32[32,384]{1,0:T(8,128)}, f32[32,384]{1,0:T(8,128)S(1)}, u32[]{:S(2)}, u32[]{:S(2)}) collective-permute-start(f32[32,384]{1,0:T(8,128)} %get-tuple-element.19), channel_id=1, source_target_pairs={{0,3},{1,0},{2,1},{3,2},{4,7},{5,4},{6,5},{7,6},{8,11},{9,8},{10,9... | collective-permute-start | bytes 147464 | tf_op jit(solution)/shard_map/ppermute | solution.py:18
  30.7 0.6 %gather_fusion.1 = f32[3]{0:T(128)S(1)} fusion(f32[8]{0:T(128)S(1)} %copy-done.8, s32[1024]{0:T(1024)S(1)} %pad_clamp_fusion.9), kind=kCustom, calls=%fused_computation.9 | custom fusion | bytes 36 | tf_op jit(solution)/shard_map/jit(_take)/gather | solution.py:220
  31.4 2.1 %collective-permute-done.8 = f32[32,384]{1,0:T(8,128)S(1)} collective-permute-done((f32[32,384]{1,0:T(8,128)}, f32[32,384]{1,0:T(8,128)S(1)}, u32[]{:S(2)}, u32[]{:S(2)}) %collective-permute-start.8) | collective-permute-done | bytes 49184 | tf_op jit(solution)/shard_map/ppermute | solution.py:18
  33.8 0.8 %add_add_fusion.refs_0_ = f32[32,384]{1,0:T(8,128)S(1)} fusion(f32[32,384]{1,0:T(8,128)S(1)} %collective-permute-done.9, f32[32,384]{1,0:T(8,128)S(1)} %collective-permute-done.8, f32[32,384]{1,0:T(8,128)} %get-tuple-element.16, f32[32,384]{1,0:T(8,128)S(1)} %collective-permute-done.7), kind=kLoop, calls=%fused_computation.17 | loop fusion | flops 36864 | bytes 245760 | tf_op jit(solution)/shard_map/add | solution.py:235
  34.6 3.0 %collective-permute-start.12 = (f32[32,384]{1,0:T(8,128)S(1)}, f32[32,384]{1,0:T(8,128)S(1)}, u32[]{:S(2)}, u32[]{:S(2)}) collective-permute-start(f32[32,384]{1,0:T(8,128)S(1)} %add_add_fusion.refs_0_), channel_id=1, source_target_pairs={{0,3},{1,0},{2,1},{3,2},{4,7},{5,4},{6,5},{7,6},{8,11},{9,8},{10,9... | collective-permute-start | bytes 147464 | tf_op jit(solution)/shard_map/ppermute | solution.py:18
  37.7 0.6 %collective-permute-start.10 = (f32[32,384]{1,0:T(8,128)S(1)}, f32[32,384]{1,0:T(8,128)S(1)}, u32[]{:S(2)}, u32[]{:S(2)}) collective-permute-start(f32[32,384]{1,0:T(8,128)S(1)} %add_add_fusion.refs_0_), channel_id=1, source_target_pairs={{0,1},{1,2},{2,3},{3,0},{4,5},{5,6},{6,7},{7,4},{8,9},{9,10},{10,1... | collective-permute-start | bytes 147464 | tf_op jit(solution)/shard_map/ppermute | solution.py:18
  38.5 1.9 %shard_map.74 = (bf16[384,384]{1,0:T(8,128)(2,1)}, bf16[384,384]{1,0:T(8,128)(2,1)}, bf16[384,256]{1,0:T(8,128)(2,1)}) custom-call(f32[128,384]{1,0:T(8,128)} %bitcast_select_fusion.coef_ref), custom_call_target="tpu_custom_call" | custom-call | tf_op jit(solution)/shard_map/pallas_call | solution.py:208
  40.4 2.3 %collective-permute-done.11.refs_2_ = f32[32,384]{1,0:T(8,128)S(1)} collective-permute-done((f32[32,384]{1,0:T(8,128)S(1)}, f32[32,384]{1,0:T(8,128)S(1)}, u32[]{:S(2)}, u32[]{:S(2)}) %collective-permute-start.11) | collective-permute-done | bytes 49184 | tf_op jit(solution)/shard_map/ppermute | solution.py:18
  42.7 0.9 %collective-permute-done.10.refs_1_ = f32[32,384]{1,0:T(8,128)S(1)} collective-permute-done((f32[32,384]{1,0:T(8,128)S(1)}, f32[32,384]{1,0:T(8,128)S(1)}, u32[]{:S(2)}, u32[]{:S(2)}) %collective-permute-start.10) | collective-permute-done | bytes 49184 | tf_op jit(solution)/shard_map/ppermute | solution.py:18
  43.6 1.0 %copy-done.3 = bf16[384,384]{1,0:T(8,128)(2,1)S(1)} copy-done((bf16[384,384]{1,0:T(8,128)(2,1)S(1)}, bf16[384,384]{1,0:T(8,128)(2,1)}, u32[]{:S(2)}) %copy-start.3) | copy-done | bytes 294936
  44.5 1.0 %copy-done.4 = bf16[384,384]{1,0:T(8,128)(2,1)S(1)} copy-done((bf16[384,384]{1,0:T(8,128)(2,1)S(1)}, bf16[384,384]{1,0:T(8,128)(2,1)}, u32[]{:S(2)}) %copy-start.4) | copy-done | bytes 294936
  45.5 0.9 %copy-done.5 = bf16[384,256]{1,0:T(8,128)(2,1)S(1)} copy-done((bf16[384,256]{1,0:T(8,128)(2,1)S(1)}, bf16[384,256]{1,0:T(8,128)(2,1)}, u32[]{:S(2)}) %copy-start.5) | copy-done | bytes 196632
  46.4 4.5 %shard_map.75 = f32[384,768]{1,0:T(8,128)} custom-call(s32[2]{0:T(128)S(1)} %copy-done.6, f32[3]{0:T(128)S(1)} %and_select_fusion.9.energy_ref, f32[32,384]{1,0:T(8,128)S(1)} %add_add_fusion.refs_0_, f32[32,384]{1,0:T(8,128)S(1)} %collective-permute-done.10.refs_1_, f32[32,384]{1,0:T(8,128)S(1)} %collective-permute-done.11.refs_2_, ...), custom_call_target="tpu_custom_call" | custom-call | tf_op jit(solution)/shard_map/pallas_call | solution.py:238
  (90 shorter events, 4.1 us)
Async XLA Ops:
  0.0 1.4 %copy-start = (f32[8,16,768]{2,1,0:T(8,128)S(1)}, f32[8,16,768]{2,1,0:T(8,128)}, u32[]{:S(2)}) copy-start(f32[8,16,768]{2,1,0:T(8,128)} %param.11) | copy-start | bytes 1179652
  0.0 2.6 %copy-start.7 = (s32[8]{0:T(128)S(1)}, s32[8]{0:T(128)}, u32[]{:S(2)}) copy-start(s32[8]{0:T(128)} %param.15) | copy-start | bytes 100
  2.1 5.9 %copy-start.9 = (f32[4,16,768]{2,1,0:T(8,128)}, f32[4,16,768]{2,1,0:T(8,128)S(1)}, u32[]{:S(2)}) copy-start(f32[4,16,768]{2,1,0:T(8,128)S(1)} %broadcast_select_fusion.3.refs_0_) | copy-start | bytes 589828
  2.1 17.7 %collective-permute-start = (f32[4,16,768]{2,1,0:T(8,128)S(1)}, f32[4,16,768]{2,1,0:T(8,128)S(1)}, u32[]{:S(2)}, u32[]{:S(2)}) collective-permute-start(f32[4,16,768]{2,1,0:T(8,128)S(1)} %broadcast_select_fusion.3.refs_0_), channel_id=1, source_target_pairs={{0,4},{4,0},{8,12},{12,8},{16,20},{20,16},{24,28},{28,24},{1,5},{5... | collective-permute-start | bytes 589832 | tf_op jit(solution)/shard_map/ppermute | solution.py:199
  4.0 10.4 %collective-permute-start.1 = (f32[4,16,768]{2,1,0:T(8,128)S(1)}, f32[4,16,768]{2,1,0:T(8,128)S(1)}, u32[]{:S(2)}, u32[]{:S(2)}) collective-permute-start(f32[4,16,768]{2,1,0:T(8,128)S(1)} %broadcast_select_fusion.2), channel_id=1, source_target_pairs={{0,8},{4,12},{8,0},{12,4},{16,24},{20,28},{24,16},{28,20},{1,9},{5... | collective-permute-start | bytes 589832 | tf_op jit(solution)/shard_map/ppermute | solution.py:198
  7.8 4.3 %copy-start.19 = (s32[16]{0:T(128)S(1)}, s32[16]{0:T(128)}, u32[]{:S(2)}) copy-start(s32[16]{0:T(128)} %param.13) | copy-start | bytes 196
  7.8 4.3 %copy-start.20 = (s32[16]{0:T(128)S(1)}, s32[16]{0:T(128)}, u32[]{:S(2)}) copy-start(s32[16]{0:T(128)} %param.14) | copy-start | bytes 196
  7.8 5.1 %copy-start.10 = (f32[128,384]{1,0:T(8,128)S(1)}, f32[128,384]{1,0:T(8,128)}, u32[]{:S(2)}) copy-start(f32[128,384]{1,0:T(8,128)} %param.12) | copy-start | bytes 589828
  8.0 11.3 %collective-permute-start.3 = (f32[4,16,768]{2,1,0:T(8,128)S(1)}, f32[4,16,768]{2,1,0:T(8,128)S(1)}, u32[]{:S(2)}, u32[]{:S(2)}) collective-permute-start(f32[4,16,768]{2,1,0:T(8,128)S(1)} %broadcast_select_fusion.1), channel_id=1, source_target_pairs={{0,16},{4,20},{8,24},{12,28},{16,0},{20,4},{24,8},{28,12},{1,17},{... | collective-permute-start | bytes 589832 | tf_op jit(solution)/shard_map/ppermute | solution.py:198
  10.9 8.4 %collective-permute-start.5 = (f32[4,16,768]{2,1,0:T(8,128)S(1)}, f32[4,16,768]{2,1,0:T(8,128)S(1)}, u32[]{:S(2)}, u32[]{:S(2)}) collective-permute-start(f32[4,16,768]{2,1,0:T(8,128)S(1)} %broadcast_select_fusion), channel_id=1, source_target_pairs={{0,24},{4,28},{8,16},{12,20},{16,8},{20,12},{24,0},{28,4},{1,25},{... | collective-permute-start | bytes 589832 | tf_op jit(solution)/shard_map/ppermute | solution.py:198
  13.0 17.7 %copy-start.8 = (f32[8]{0:T(128)S(1)}, f32[8]{0:T(128)}, u32[]{:S(2)}) copy-start(f32[8]{0:T(128)} %param.16) | copy-start | bytes 100
  14.4 6.6 %copy-start.12 = (f32[4,16,768]{2,1,0:T(8,128)}, f32[4,16,768]{2,1,0:T(8,128)S(1)}, u32[]{:S(2)}) copy-start(f32[4,16,768]{2,1,0:T(8,128)S(1)} %collective-permute-done.1.refs_2_) | copy-start | bytes 589828
  14.4 5.4 %collective-permute-start.2 = (f32[4,16,768]{2,1,0:T(8,128)S(1)}, f32[4,16,768]{2,1,0:T(8,128)S(1)}, u32[]{:S(2)}, u32[]{:S(2)}) collective-permute-start(f32[4,16,768]{2,1,0:T(8,128)S(1)} %collective-permute-done.1.refs_2_), channel_id=1, source_target_pairs={{0,4},{4,0},{8,12},{12,8},{16,20},{20,16},{24,28},{28,24},{1,5},{5... | collective-permute-start | bytes 589832 | tf_op jit(solution)/shard_map/ppermute | solution.py:199
  19.2 1.7 %copy-start.13 = (f32[4,16,768]{2,1,0:T(8,128)}, f32[4,16,768]{2,1,0:T(8,128)S(1)}, u32[]{:S(2)}) copy-start(f32[4,16,768]{2,1,0:T(8,128)S(1)} %collective-permute-done.3.refs_4_) | copy-start | bytes 589828
  19.2 1.4 %collective-permute-start.4 = (f32[4,16,768]{2,1,0:T(8,128)S(1)}, f32[4,16,768]{2,1,0:T(8,128)S(1)}, u32[]{:S(2)}, u32[]{:S(2)}) collective-permute-start(f32[4,16,768]{2,1,0:T(8,128)S(1)} %collective-permute-done.3.refs_4_), channel_id=1, source_target_pairs={{0,4},{4,0},{8,12},{12,8},{16,20},{20,16},{24,28},{28,24},{1,5},{5... | collective-permute-start | bytes 589832 | tf_op jit(solution)/shard_map/ppermute | solution.py:199
  19.3 1.7 %copy-start.14 = (f32[4,16,768]{2,1,0:T(8,128)}, f32[4,16,768]{2,1,0:T(8,128)S(1)}, u32[]{:S(2)}) copy-start(f32[4,16,768]{2,1,0:T(8,128)S(1)} %collective-permute-done.5.refs_6_) | copy-start | bytes 589828
  19.3 1.7 %collective-permute-start.6 = (f32[4,16,768]{2,1,0:T(8,128)S(1)}, f32[4,16,768]{2,1,0:T(8,128)S(1)}, u32[]{:S(2)}, u32[]{:S(2)}) collective-permute-start(f32[4,16,768]{2,1,0:T(8,128)S(1)} %collective-permute-done.5.refs_6_), channel_id=1, source_target_pairs={{0,4},{4,0},{8,12},{12,8},{16,20},{20,16},{24,28},{28,24},{1,5},{5... | collective-permute-start | bytes 589832 | tf_op jit(solution)/shard_map/ppermute | solution.py:199
  19.8 18.6 %copy-start.18 = (f32[384]{0:T(512)S(1)}, f32[384]{0:T(512)}, u32[]{:S(2)}) copy-start(f32[384]{0:T(512)} %param.17) | copy-start | bytes 4612
  19.8 23.8 %copy-start.6 = (s32[2]{0:T(128)S(1)}, s32[2]{0:T(128)}, u32[]{:S(2)}) copy-start(s32[2]{0:T(128)} %pad_add_fusion.place_ref) | copy-start | bytes 28
  19.8 1.2 %copy-start.11 = (f32[4,16,768]{2,1,0:T(8,128)}, f32[4,16,768]{2,1,0:T(8,128)S(1)}, u32[]{:S(2)}) copy-start(f32[4,16,768]{2,1,0:T(8,128)S(1)} %collective-permute-done.refs_1_) | copy-start | bytes 589828
  19.8 1.2 %copy-start.15 = (f32[4,16,768]{2,1,0:T(8,128)}, f32[4,16,768]{2,1,0:T(8,128)S(1)}, u32[]{:S(2)}) copy-start(f32[4,16,768]{2,1,0:T(8,128)S(1)} %collective-permute-done.2.refs_3_) | copy-start | bytes 589828
  25.1 18.4 %copy-start.1 = (bf16[384,768]{1,0:T(8,128)(2,1)S(1)}, bf16[384,768]{1,0:T(8,128)(2,1)}, u32[]{:S(2)}) copy-start(bf16[384,768]{1,0:T(8,128)(2,1)} %get-tuple-element.23.refs_9_) | copy-start | bytes 1769476
  25.1 18.4 %copy-start.2 = (bf16[384,768]{1,0:T(8,128)(2,1)S(1)}, bf16[384,768]{1,0:T(8,128)(2,1)}, u32[]{:S(2)}) copy-start(bf16[384,768]{1,0:T(8,128)(2,1)} %get-tuple-element.24.refs_10_) | copy-start | bytes 1769476
  25.1 6.2 %collective-permute-start.7 = (f32[32,384]{1,0:T(8,128)}, f32[32,384]{1,0:T(8,128)S(1)}, u32[]{:S(2)}, u32[]{:S(2)}) collective-permute-start(f32[32,384]{1,0:T(8,128)} %get-tuple-element.17), channel_id=1, source_target_pairs={{0,1},{1,2},{2,3},{3,0},{4,5},{5,6},{6,7},{7,4},{8,9},{9,10},{10,1... | collective-permute-start | bytes 147464 | tf_op jit(solution)/shard_map/ppermute | solution.py:18
  26.8 6.7 %collective-permute-start.8 = (f32[32,384]{1,0:T(8,128)}, f32[32,384]{1,0:T(8,128)S(1)}, u32[]{:S(2)}, u32[]{:S(2)}) collective-permute-start(f32[32,384]{1,0:T(8,128)} %get-tuple-element.18), channel_id=1, source_target_pairs={{0,2},{1,3},{2,0},{3,1},{4,6},{5,7},{6,4},{7,5},{8,10},{9,11},{10,... | collective-permute-start | bytes 147464 | tf_op jit(solution)/shard_map/ppermute | solution.py:18
  29.4 4.5 %collective-permute-start.9 = (f32[32,384]{1,0:T(8,128)}, f32[32,384]{1,0:T(8,128)S(1)}, u32[]{:S(2)}, u32[]{:S(2)}) collective-permute-start(f32[32,384]{1,0:T(8,128)} %get-tuple-element.19), channel_id=1, source_target_pairs={{0,3},{1,0},{2,1},{3,2},{4,7},{5,4},{6,5},{7,6},{8,11},{9,8},{10,9... | collective-permute-start | bytes 147464 | tf_op jit(solution)/shard_map/ppermute | solution.py:18
  34.6 5.7 %collective-permute-start.12 = (f32[32,384]{1,0:T(8,128)S(1)}, f32[32,384]{1,0:T(8,128)S(1)}, u32[]{:S(2)}, u32[]{:S(2)}) collective-permute-start(f32[32,384]{1,0:T(8,128)S(1)} %add_add_fusion.refs_0_), channel_id=1, source_target_pairs={{0,3},{1,0},{2,1},{3,2},{4,7},{5,4},{6,5},{7,6},{8,11},{9,8},{10,9... | collective-permute-start | bytes 147464 | tf_op jit(solution)/shard_map/ppermute | solution.py:18
  37.7 5.0 %collective-permute-start.11 = (f32[32,384]{1,0:T(8,128)S(1)}, f32[32,384]{1,0:T(8,128)S(1)}, u32[]{:S(2)}, u32[]{:S(2)}) collective-permute-start(f32[32,384]{1,0:T(8,128)S(1)} %add_add_fusion.refs_0_), channel_id=1, source_target_pairs={{0,2},{1,3},{2,0},{3,1},{4,6},{5,7},{6,4},{7,5},{8,10},{9,11},{10,... | collective-permute-start | bytes 147464 | tf_op jit(solution)/shard_map/ppermute | solution.py:18
  37.7 5.9 %collective-permute-start.10 = (f32[32,384]{1,0:T(8,128)S(1)}, f32[32,384]{1,0:T(8,128)S(1)}, u32[]{:S(2)}, u32[]{:S(2)}) collective-permute-start(f32[32,384]{1,0:T(8,128)S(1)} %add_add_fusion.refs_0_), channel_id=1, source_target_pairs={{0,1},{1,2},{2,3},{3,0},{4,5},{5,6},{6,7},{7,4},{8,9},{9,10},{10,1... | collective-permute-start | bytes 147464 | tf_op jit(solution)/shard_map/ppermute | solution.py:18
  43.6 1.0 %copy-start.3 = (bf16[384,384]{1,0:T(8,128)(2,1)S(1)}, bf16[384,384]{1,0:T(8,128)(2,1)}, u32[]{:S(2)}) copy-start(bf16[384,384]{1,0:T(8,128)(2,1)} %get-tuple-element.20.refs_6_) | copy-start | bytes 884740
  44.5 1.0 %copy-start.4 = (bf16[384,384]{1,0:T(8,128)(2,1)S(1)}, bf16[384,384]{1,0:T(8,128)(2,1)}, u32[]{:S(2)}) copy-start(bf16[384,384]{1,0:T(8,128)(2,1)} %get-tuple-element.21.refs_7_) | copy-start | bytes 884740
  45.5 0.9 %copy-start.5 = (bf16[384,256]{1,0:T(8,128)(2,1)S(1)}, bf16[384,256]{1,0:T(8,128)(2,1)}, u32[]{:S(2)}) copy-start(bf16[384,256]{1,0:T(8,128)(2,1)} %get-tuple-element.22.refs_8_) | copy-start | bytes 589828
  (2 other events, 1.4 us)

commit v2 on v1

--- a/solution.py
+++ b/solution.py
@@ -10,6 +10,7 @@
 STOPS = 3
 BF16 = jnp.bfloat16
 F32 = jnp.float32
+SELECT_VMEM = 24 * 1024 * 1024
 
 
 def shifted(value, axis, steps):
@@ -95,21 +96,81 @@
     return lax.dot_general(a, b, (((1,), (1,)), ((), ())), preferred_element_type=F32)
 
 
-def coefficient_kernel(coef_ref, left_ref, right_ref, back_ref):
-    coef = coef_ref[...]
+def partner_chip(chip, step, chips):
+    return chip ^ step if chips & (chips - 1) == 0 else lax.rem(chip + step, chips)
+
+
+def source_chip(chip, step, chips):
+    return chip ^ step if chips & (chips - 1) == 0 else lax.rem(chip + chips - step, chips)
+
+
+def select_kernel(blk_count, owner_hbm, x_hbm, *refs):
+    *outs, owner_ref, x_ref, owner_sem, x_sem = refs
+    chips = blk_count // 2
+    my_chip = lax.axis_index("blk") >> 1
+    reads = [
+        pltpu.make_async_copy(owner_hbm, owner_ref, owner_sem),
+        pltpu.make_async_copy(x_hbm, x_ref, x_sem),
+    ]
+    for read in reads:
+        read.start()
+    for read in reads:
+        read.wait()
+    for step, out in enumerate(outs):
+        last = 2 * partner_chip(my_chip, step, chips) + 1
+        for stop in range(STOPS + 1):
+            out[stop] = x_ref[owner_ref[lax.rem(last + blk_count - stop, blk_count)]]
+
+
+def coefficient_kernel(
+    blk_count,
+    size_ref,
+    shell_ref,
+    owner_ref,
+    energy_ref,
+    coef_ref,
+    virt_ref,
+    left_ref,
+    right_ref,
+    back_ref,
+    gap_ref,
+    ordered,
+):
+    slots = coef_ref.shape[0]
+    slot_cap = slots // blk_count
+    me = lax.axis_index("blk")
+    shells = [(size_ref[s], shell_ref[s]) for s in range(size_ref.shape[0])]
+    count = lax.broadcasted_iota(jnp.int32, (slot_cap, coef_ref.shape[1]), 0)
+    for index in range(blk_count):
+        chip = source_chip(me >> 1, index // 2, blk_count // 2)
+        blk = 2 * chip + ((me & 1) ^ (index % 2))
+        load = jnp.int32(0)
+        for size, shell in shells:
+            load = load + jnp.where(shell == blk, size, 0)
+        rows = coef_ref[pl.ds(pl.multiple_of(blk * slot_cap, slot_cap), slot_cap), :]
+        ordered[pl.ds(index * slot_cap, slot_cap), :] = jnp.where(count < load, rows, 0.0)
+    coef = ordered[...]
     high, low = halves(coef)
     right_ref[...] = jnp.concatenate([high, low, high], axis=0)
     turned = coef.T
     high, low = halves(turned)
     left_ref[...] = jnp.concatenate([high, high, low], axis=1)
     back_ref[...] = jnp.concatenate([high, low], axis=1)
-
-
-def overlap_kernel(parts, slot_cap, place_ref, *refs):
+    row = virt_ref[...]
+    virt_count = row.shape[1]
+    column = jnp.broadcast_to(row, (8, virt_count)).T[:, :1]
+    own = energy_ref[owner_ref[me]]
+    for stop in range(STOPS):
+        both = own + energy_ref[owner_ref[lax.rem(me + blk_count - stop, blk_count)]]
+        gap_ref[pl.ds(stop * virt_count, virt_count), :] = 1.0 / ((both - column) - row)
+
+
+def overlap_kernel(parts, slot_cap, *refs):
     pieces = refs[: -parts - 3]
     outs = refs[-parts - 3 : -3]
     x_high, x_low, total = refs[-3:]
-    first = place_ref[0]
+    first = 1 - (lax.axis_index("blk") & 1)
+    here = lax.axis_index("aux")
     for stop in range(STOPS):
         for index, piece in enumerate(pieces):
             high, low = halves(piece[first + stop])
@@ -131,34 +192,45 @@
         total[:, rows] = gram
     share = slots // parts
     for step, out in enumerate(outs):
-        row = pl.multiple_of(lax.rem(place_ref[1] + step, parts) * share, share)
+        row = pl.multiple_of(lax.rem(here + step, parts) * share, share)
         out[...] = total[pl.ds(row, share), :]
 
 
-def density_kernel(parts, place_ref, energy_ref, *refs):
+def density_kernel(parts, *refs):
     shares = refs[:parts]
-    e_row, e_col, left, right, back, x_high, x_low, out, total, w_high, w_low = refs[parts:]
+    left, right, back, gap, x_high, x_low, out, total, w_high, w_low, density, sems = refs[parts:]
+    here = lax.axis_index("aux")
     slots = total.shape[0]
     share = slots // parts
+    virt_count = out.shape[0]
     for step, piece in enumerate(shares):
-        row = pl.multiple_of(lax.rem(place_ref[1] + parts - step, parts) * share, share)
+        row = pl.multiple_of(lax.rem(here + parts - step, parts) * share, share)
         total[pl.ds(row, share), :] = piece[...]
     high, low = halves(total[...])
     half_done = matmul(left[...], jnp.concatenate([high, low, high], axis=0))
-    for stop in range(STOPS):
-        cols = pl.ds(stop * slots, slots)
-        high, low = halves(half_done[:, stop * slots : (stop + 1) * slots])
-        summed = matmul(jnp.concatenate([high, high, low], axis=1), right[...])
-        gap = (energy_ref[0] + energy_ref[stop] - e_col[...]) - e_row[...]
-        high, low = halves(summed / gap)
-        both = matmul(high, back[...])
-        weight = both[:, :slots] + both[:, slots:] + matmul(low, back[:, :slots])
-        w_high[:, cols], w_low[:, cols] = halves(weight)
-    out[...] = (
-        matmul(w_high[...], x_high[...])
-        + matmul(w_high[...], x_low[...])
-        + matmul(w_low[...], x_high[...])
-    )
+    half_done = jnp.concatenate(
+        [half_done[:, stop * slots : (stop + 1) * slots] for stop in range(STOPS)], axis=0
+    )
+    high, low = halves(half_done)
+    summed = matmul(jnp.concatenate([high, high, low], axis=1), right[...])
+    high, low = halves(summed * gap[...])
+    both = matmul(high, back[...])
+    weight = both[:, :slots] + both[:, slots:] + matmul(low, back[:, :slots])
+    for stop in range(STOPS):
+        rows = slice(stop * virt_count, (stop + 1) * virt_count)
+        cols = slice(stop * slots, (stop + 1) * slots)
+        w_high[:, cols], w_low[:, cols] = halves(weight[rows])
+    copies = []
+    for index in range(sems.shape[0]):
+        band = virt_count // sems.shape[0]
+        rows = pl.ds(index * band, band)
+        high, low = w_high[rows, :], w_low[rows, :]
+        x_all = jnp.concatenate([x_high[...], x_high[...], x_low[...]], axis=0)
+        density[rows, :] = matmul(jnp.concatenate([high, low, high], axis=1), x_all)
+        copies.append(pltpu.make_async_copy(density.at[rows], out.at[rows], sems.at[index]))
+        copies[-1].start()
+    for copy in copies:
+        copy.wait()
 
 
 def slots_first(
@@ -169,95 +241,87 @@
     _, slot_cap, aux_width = occupied_integrals.shape
     slots, virt_count = virtual_coefficients.shape
     chips = blk_count // 2
-    my_index = lax.axis_index("blk")
-    my_chip, my_core = my_index // 2, my_index % 2
     vmem = pl.BlockSpec(memory_space=pltpu.VMEM)
     smem = pl.BlockSpec(memory_space=pltpu.SMEM)
-
-    def other(chip, step):
-        return chip ^ step if chips & (chips - 1) == 0 else (chip + step) % chips
-
-    def source(chip, step):
-        return chip ^ step if chips & (chips - 1) == 0 else (chip + chips - step) % chips
-
-    window = jnp.arange(STOPS + 1, dtype=jnp.int32)
-
-    def wanted(chip):
-        rows = jnp.mod(2 * chip + 1 - window, blk_count)
-        return jnp.take(occupied_integrals, jnp.take(occ_owner, rows), axis=0)
-
-    pieces, owners = [], []
-    for step in range(chips):
-        piece = wanted(other(my_chip, step))
+    params = pltpu.CompilerParams(vmem_limit_bytes=24 * 1024 * 1024)
+
+    sent = pl.pallas_call(
+        functools.partial(select_kernel, blk_count),
+        out_shape=[jax.ShapeDtypeStruct((STOPS + 1, slot_cap, aux_width), F32)] * chips,
+        in_specs=[pl.BlockSpec(memory_space=pltpu.HBM)] * 2,
+        out_specs=[vmem] * chips,
+        scratch_shapes=[
+            pltpu.SMEM(occ_owner.shape, jnp.int32),
+            pltpu.VMEM(occupied_integrals.shape, F32),
+            pltpu.SemaphoreType.DMA,
+            pltpu.SemaphoreType.DMA,
+        ],
+        compiler_params=pltpu.CompilerParams(vmem_limit_bytes=SELECT_VMEM),
+    )(occ_owner, occupied_integrals)
+
+    pieces = []
+    for step, piece in enumerate(sent):
         if step > 0:
             pairs = [
-                (2 * chip + core, 2 * other(chip, step) + core)
+                (2 * chip + core, 2 * int(partner_chip(chip, step, chips)) + core)
                 for chip in range(chips)
                 for core in range(2)
             ]
             piece = lax.ppermute(piece, "blk", pairs)
-        swapped = lax.ppermute(piece, "blk", [(i, i ^ 1) for i in range(blk_count)])
-        pieces += [piece, swapped]
-        owner = 2 * source(my_chip, step)
-        owners += [owner + my_core, owner + 1 - my_core]
-    owners = jnp.stack(owners)
-
-    live_mask = live_slots(shell_size, shell_owner, blk_count, slot_cap)
-    coef = virtual_coefficients.reshape(blk_count, slot_cap, virt_count) * live_mask[:, :, None]
-    coef = jnp.take(coef, owners, axis=0).reshape(slots, virt_count)
-    left, right, back = pl.pallas_call(
-        coefficient_kernel,
+        pieces += [piece, lax.ppermute(piece, "blk", [(i, i ^ 1) for i in range(blk_count)])]
+
+    left, right, back, gap = pl.pallas_call(
+        functools.partial(coefficient_kernel, blk_count),
         out_shape=[
             jax.ShapeDtypeStruct((virt_count, 3 * slots), BF16),
             jax.ShapeDtypeStruct((3 * slots, virt_count), BF16),
             jax.ShapeDtypeStruct((virt_count, 2 * slots), BF16),
+            jax.ShapeDtypeStruct((STOPS * virt_count, virt_count), F32),
         ],
-        in_specs=[vmem],
-        out_specs=[vmem] * 3,
-    )(coef)
-
-    stops = jnp.arange(STOPS, dtype=jnp.int32)
-    energies = jnp.take(e_occ, jnp.take(occ_owner, jnp.mod(my_index - stops, blk_count)))
-    place = jnp.stack([1 - my_core, lax.axis_index("aux")]).astype(jnp.int32)
+        in_specs=[smem] * 4 + [vmem] * 2,
+        out_specs=[vmem] * 4,
+        scratch_shapes=[pltpu.VMEM((slots, virt_count), F32)],
+        compiler_params=params,
+    )(
+        shell_size,
+        shell_owner,
+        occ_owner,
+        e_occ,
+        virtual_coefficients,
+        e_virt.reshape(1, virt_count),
+    )
 
     share = slots // parts
     *shares, x_high, x_low = pl.pallas_call(
         functools.partial(overlap_kernel, parts, slot_cap),
         out_shape=[jax.ShapeDtypeStruct((share, STOPS * slots), F32)] * parts
         + [jax.ShapeDtypeStruct((STOPS * slots, aux_width), BF16)] * 2,
-        in_specs=[smem] + [vmem] * len(pieces),
+        in_specs=[vmem] * len(pieces),
         out_specs=[vmem] * (parts + 2),
         scratch_shapes=[pltpu.VMEM((slots, STOPS * slots), F32)],
-    )(place, *pieces)
+        compiler_params=params,
+    )(*pieces)
 
     mine = shares[0]
     for step in range(1, parts):
         mine = mine + shifted(shares[step], "aux", step)
     gathered = [mine] + [shifted(mine, "aux", step) for step in range(1, parts)]
 
+    bands = 3 if virt_count % 48 == 0 else 1
     density = pl.pallas_call(
         functools.partial(density_kernel, parts),
         out_shape=jax.ShapeDtypeStruct((virt_count, aux_width), F32),
-        in_specs=[smem, smem] + [vmem] * (parts + 7),
-        out_specs=vmem,
+        in_specs=[vmem] * (parts + 6),
+        out_specs=pl.BlockSpec(memory_space=pl.ANY),
         scratch_shapes=[
             pltpu.VMEM((slots, STOPS * slots), F32),
             pltpu.VMEM((virt_count, STOPS * slots), BF16),
             pltpu.VMEM((virt_count, STOPS * slots), BF16),
+            pltpu.VMEM((virt_count, aux_width), F32),
+            pltpu.SemaphoreType.DMA((bands,)),
         ],
-        compiler_params=pltpu.CompilerParams(vmem_limit_bytes=32 * 1024 * 1024),
-    )(
-        place,
-        energies,
-        *gathered,
-        e_virt.reshape(1, virt_count),
-        e_virt.reshape(virt_count, 1),
-        left,
-        right,
-        back,
-        x_high,
-        x_low,
-    )
+        compiler_params=params,
+    )(*gathered, left, right, back, gap, x_high, x_low)
     return density.reshape(1, virt_count, aux_width)
 
 

time: 51.3 us -> 39.1 us (0.76)
  local copies, waits for them, and re-layouts: 11.8 us -> 1.68 us
  waiting for transfers between devices: 11.7 us -> 17.2 us
  Pallas kernels: 9.47 us -> 5.75 us
  other arithmetic: 3.11 us -> 0.02 us
    gather x11 -> x0, local copies, waits for them, and re-layouts: 7.35 us -> none  [the longest x8 5.51 us: wanted(): return jnp.take(occupied_integrals, jnp.take(occ_owner, rows), axis=0)]
    ppermute x3, waiting for transfers between devices: 4.86 us -> 9.03 us  [slots_first(): piece = lax.ppermute(piece, 'blk', pairs)]
    pallas_call x1, Pallas kernels: 3.09 us -> 0.75 us  [slots_first(): pl.pallas_call(functools.partial(overlap_kernel, parts, slot_cap), out_sh...]
    unnamed x42 -> x16, local copies, waits for them, and re-layouts: 3.96 us -> 1.67 us
    pallas_call x1, Pallas kernels: 4.5 us -> 3.17 us  [slots_first(): pl.pallas_call(functools.partial(density_kernel, parts), out_shape=jax.Sh...]
    ppermute x6, waiting for transfers between devices: 5.68 us -> 6.93 us  [shifted(): return lax.ppermute(value, axis, pairs)]
    select_n x13 -> x0, other arithmetic: 1.19 us -> none  [the longest x2 0.76 us: slots_first(): coef = jnp.take(coef, owners, axis=0).reshape(slots, virt_count)]
    add x1, other arithmetic: 0.81 us -> 0.02 us  [slots_first(): mine = mine + shifted(shares[step], 'aux', step)]
  transfers between devices with their start and end apart: 13 -> 13, of which waited for: 7 -> 9; matrix products, arithmetic and copies ran while one was open for 16% -> 0% of each run, Pallas kernels for 4% -> 3%
where the time goes in v2:
time: 39.1 us; the launch traced here: 39 us
  waiting for transfers between devices  17.2 us (44%)
  starting transfers between devices  14.2 us (36%)
  Pallas kernels  5.75 us (15%)
  local copies, waits for them, and re-layouts  1.68 us (4%)
    ppermute x6, starting transfers between devices, shifted(): return lax.ppermute(value, axis, pairs)  9.19 us
    ppermute x3, waiting for transfers between devices, slots_first(): piece = lax.ppermute(piece, 'blk', pairs)  9.03 us
    ppermute x6, waiting for transfers between devices, shifted(): return lax.ppermute(value, axis, pairs)  6.93 us
    ppermute x3, starting transfers between devices, slots_first(): piece = lax.ppermute(piece, 'blk', pairs)  4.54 us
    pallas_call x1, Pallas kernels, slots_first(): pl.pallas_call(functools.partial(density_kernel, parts), out_shape=jax.Sh...  3.17 us
    unnamed x16, local copies, waits for them, and re-layouts  1.67 us
    pallas_call x1, Pallas kernels, slots_first(): pl.pallas_call(functools.partial(coefficient_kernel, blk_count), out_shap...  1.21 us
    ppermute x4, waiting for transfers between devices, slots_first(): lax.ppermute(piece, 'blk', [(i, i ^ 1) for i in range(blk_count)])  1.21 us
  transfers between devices with their start and end apart: 13, of which 9 were waited for; matrix products, arithmetic and copies ran while one was open for 0% of the time, Pallas kernels for 3%

profile of v2, /device:TPU:0, one launch (start us, length us, event | category | flops | bytes accessed | tf_op | source)
XLA Modules:
  0.0 39.0 jit_solution(8865017792812845920)
XLA Ops:
  0.0 1.0 %copy-done = f32[8,16,768]{2,1,0:T(8,128)S(1)} copy-done((f32[8,16,768]{2,1,0:T(8,128)S(1)}, f32[8,16,768]{2,1,0:T(8,128)}, u32[]{:S(2)}) %copy-start) | copy-done | bytes 393240
  1.0 0.7 %copy-done.2 = s32[8]{0:T(128)S(1)} copy-done((s32[8]{0:T(128)S(1)}, s32[8]{0:T(128)}, u32[]{:S(2)}) %copy-start.2) | copy-done | bytes 56
  1.7 0.6 %shard_map.73 = (f32[4,16,768]{2,1,0:T(8,128)S(1)}, f32[4,16,768]{2,1,0:T(8,128)S(1)}, f32[4,16,768]{2,1,0:T(8,128)S(1)}, f32[4,16,768]{2,1,0:T(8,128)S(1)}) custom-call(s32[8]{0:T(128)S(1)} %copy-done.2, f32[8,16,768]{2,1,0:T(8,128)S(1)} %copy-done), custom_call_target="tpu_custom_call" | custom-call | tf_op jit(solution)/shard_map/pallas_call | solution.py:248
  2.3 3.0 %collective-permute-start.1 = (f32[4,16,768]{2,1,0:T(8,128)S(1)}, f32[4,16,768]{2,1,0:T(8,128)S(1)}, u32[]{:S(2)}, u32[]{:S(2)}) collective-permute-start(f32[4,16,768]{2,1,0:T(8,128)S(1)} %get-tuple-element.20), channel_id=1, source_target_pairs={{0,8},{4,12},{8,0},{12,4},{16,24},{20,28},{24,16},{28,20},{1,9},{5... | collective-permute-start | bytes 589832 | tf_op jit(solution)/shard_map/ppermute | solution.py:270
  5.3 1.5 %collective-permute-start.3 = (f32[4,16,768]{2,1,0:T(8,128)S(1)}, f32[4,16,768]{2,1,0:T(8,128)S(1)}, u32[]{:S(2)}, u32[]{:S(2)}) collective-permute-start(f32[4,16,768]{2,1,0:T(8,128)S(1)} %get-tuple-element.21), channel_id=1, source_target_pairs={{0,16},{4,20},{8,24},{12,28},{16,0},{20,4},{24,8},{28,12},{1,17},{... | collective-permute-start | bytes 589832 | tf_op jit(solution)/shard_map/ppermute | solution.py:270
  6.8 0.0 collective-permute-start.5
  6.9 0.0 collective-permute-start
  6.9 4.2 %collective-permute-done.1.refs_2_ = f32[4,16,768]{2,1,0:T(8,128)S(1)} collective-permute-done((f32[4,16,768]{2,1,0:T(8,128)S(1)}, f32[4,16,768]{2,1,0:T(8,128)S(1)}, u32[]{:S(2)}, u32[]{:S(2)}) %collective-permute-start.1) | collective-permute-done | bytes 196640 | tf_op jit(solution)/shard_map/ppermute | solution.py:270
  11.0 0.0 collective-permute-start.2
  11.0 4.8 %collective-permute-done.3.refs_4_ = f32[4,16,768]{2,1,0:T(8,128)S(1)} collective-permute-done((f32[4,16,768]{2,1,0:T(8,128)S(1)}, f32[4,16,768]{2,1,0:T(8,128)S(1)}, u32[]{:S(2)}, u32[]{:S(2)}) %collective-permute-start.3) | collective-permute-done | bytes 196640 | tf_op jit(solution)/shard_map/ppermute | solution.py:270
  15.9 0.0 collective-permute-start.4
  15.9 0.0 collective-permute-done.5.refs_6_
  15.9 0.5 %collective-permute-start.6 = (f32[4,16,768]{2,1,0:T(8,128)S(1)}, f32[4,16,768]{2,1,0:T(8,128)S(1)}, u32[]{:S(2)}, u32[]{:S(2)}) collective-permute-start(f32[4,16,768]{2,1,0:T(8,128)S(1)} %collective-permute-done.5.refs_6_), channel_id=1, source_target_pairs={{0,4},{4,0},{8,12},{12,8},{16,20},{20,16},{24,28},{28,24},{1,5},{5... | collective-permute-start | bytes 589832 | tf_op jit(solution)/shard_map/ppermute | solution.py:271
  16.4 0.0 collective-permute-done.refs_1_
  16.4 0.0 collective-permute-done.2.refs_3_
  16.4 0.9 %collective-permute-done.4.refs_5_ = f32[4,16,768]{2,1,0:T(8,128)S(1)} collective-permute-done((f32[4,16,768]{2,1,0:T(8,128)S(1)}, f32[4,16,768]{2,1,0:T(8,128)S(1)}, u32[]{:S(2)}, u32[]{:S(2)}) %collective-permute-start.4) | collective-permute-done | bytes 196640 | tf_op jit(solution)/shard_map/ppermute | solution.py:271
  17.3 0.3 collective-permute-done.6.refs_7_
  17.6 0.8 %shard_map.74 = (f32[32,384]{1,0:T(8,128)S(1)}, f32[32,384]{1,0:T(8,128)S(1)}, f32[32,384]{1,0:T(8,128)S(1)}, f32[32,384]{1,0:T(8,128)S(1)}, bf16[384,768]{1,0:T(8,128)(2,1)S(1)}, /*index=5*/bf16[384,768]{1,0:T(8,128)(2,1)S(1)}) custom-call(f32[4,16,768]{2,1,0:T(8,128)S(1)} %get-tuple-element.19.refs_0_, f32[4,16,768]{2,1,0:T(8,128)S(1)} %collective-permute-done.refs_1_, ...), custom_call_target="tpu_custom_call" | custom-call | tf_op jit(solution)/shard_map/pallas_call | solution.py:295
  18.4 1.6 %collective-permute-start.7 = (f32[32,384]{1,0:T(8,128)S(1)}, f32[32,384]{1,0:T(8,128)S(1)}, u32[]{:S(2)}, u32[]{:S(2)}) collective-permute-start(f32[32,384]{1,0:T(8,128)S(1)} %get-tuple-element.24), channel_id=1, source_target_pairs={{0,1},{1,2},{2,3},{3,0},{4,5},{5,6},{6,7},{7,4},{8,9},{9,10},{10,1... | collective-permute-start | bytes 147464 | tf_op jit(solution)/shard_map/ppermute | solution.py:19
  20.0 2.6 %collective-permute-start.8 = (f32[32,384]{1,0:T(8,128)S(1)}, f32[32,384]{1,0:T(8,128)S(1)}, u32[]{:S(2)}, u32[]{:S(2)}) collective-permute-start(f32[32,384]{1,0:T(8,128)S(1)} %get-tuple-element.25), channel_id=1, source_target_pairs={{0,2},{1,3},{2,0},{3,1},{4,6},{5,7},{6,4},{7,5},{8,10},{9,11},{10,... | collective-permute-start | bytes 147464 | tf_op jit(solution)/shard_map/ppermute | solution.py:19
  22.6 1.3 %collective-permute-start.9 = (f32[32,384]{1,0:T(8,128)S(1)}, f32[32,384]{1,0:T(8,128)S(1)}, u32[]{:S(2)}, u32[]{:S(2)}) collective-permute-start(f32[32,384]{1,0:T(8,128)S(1)} %get-tuple-element.26), channel_id=1, source_target_pairs={{0,3},{1,0},{2,1},{3,2},{4,7},{5,4},{6,5},{7,6},{8,11},{9,8},{10,9... | collective-permute-start | bytes 147464 | tf_op jit(solution)/shard_map/ppermute | solution.py:19
  23.9 0.4 collective-permute-done.7
  24.3 2.2 %collective-permute-done.8 = f32[32,384]{1,0:T(8,128)S(1)} collective-permute-done((f32[32,384]{1,0:T(8,128)S(1)}, f32[32,384]{1,0:T(8,128)S(1)}, u32[]{:S(2)}, u32[]{:S(2)}) %collective-permute-start.8) | collective-permute-done | bytes 49184 | tf_op jit(solution)/shard_map/ppermute | solution.py:19
  26.6 0.3 collective-permute-done.9
  26.9 3.0 %collective-permute-start.12 = (f32[32,384]{1,0:T(8,128)S(1)}, f32[32,384]{1,0:T(8,128)S(1)}, u32[]{:S(2)}, u32[]{:S(2)}) collective-permute-start(f32[32,384]{1,0:T(8,128)S(1)} %add_add_fusion.refs_0_), channel_id=1, source_target_pairs={{0,3},{1,0},{2,1},{3,2},{4,7},{5,4},{6,5},{7,6},{8,11},{9,8},{10,9... | collective-permute-start | bytes 147464 | tf_op jit(solution)/shard_map/ppermute | solution.py:19
  29.9 0.0 collective-permute-start.11
  29.9 0.6 %collective-permute-start.10 = (f32[32,384]{1,0:T(8,128)S(1)}, f32[32,384]{1,0:T(8,128)S(1)}, u32[]{:S(2)}, u32[]{:S(2)}) collective-permute-start(f32[32,384]{1,0:T(8,128)S(1)} %add_add_fusion.refs_0_), channel_id=1, source_target_pairs={{0,1},{1,2},{2,3},{3,0},{4,5},{5,6},{6,7},{7,4},{8,9},{9,10},{10,1... | collective-permute-start | bytes 147464 | tf_op jit(solution)/shard_map/ppermute | solution.py:19
  30.6 1.2 %shard_map.75 = (bf16[384,384]{1,0:T(8,128)(2,1)S(1)}, bf16[384,384]{1,0:T(8,128)(2,1)S(1)}, bf16[384,256]{1,0:T(8,128)(2,1)S(1)}, f32[1152,384]{1,0:T(8,128)S(1)}) custom-call(s32[16]{0:T(128)S(1)} %copy-done.4, s32[16]{0:T(128)S(1)} %copy-done.5, s32[8]{0:T(128)S(1)} %copy-done.3, f32[8]{0:T(128)S(1)} %copy-done.6, f32[128,384]{1,0:T(8,128)S(1)} %copy-done.1, ...), custom_call_target="tpu_custom_call" | custom-call | tf_op jit(solution)/shard_map/pallas_call | solution.py:273
  31.8 0.0 collective-permute-done.12.refs_3_
  31.8 3.1 %collective-permute-done.11.refs_2_ = f32[32,384]{1,0:T(8,128)S(1)} collective-permute-done((f32[32,384]{1,0:T(8,128)S(1)}, f32[32,384]{1,0:T(8,128)S(1)}, u32[]{:S(2)}, u32[]{:S(2)}) %collective-permute-start.11) | collective-permute-done | bytes 49184 | tf_op jit(solution)/shard_map/ppermute | solution.py:19
  34.9 0.9 %collective-permute-done.10.refs_1_ = f32[32,384]{1,0:T(8,128)S(1)} collective-permute-done((f32[32,384]{1,0:T(8,128)S(1)}, f32[32,384]{1,0:T(8,128)S(1)}, u32[]{:S(2)}, u32[]{:S(2)}) %collective-permute-start.10) | collective-permute-done | bytes 49184 | tf_op jit(solution)/shard_map/ppermute | solution.py:19
  35.8 3.2 %shard_map.76 = f32[384,768]{1,0:T(8,128)} custom-call(f32[32,384]{1,0:T(8,128)S(1)} %add_add_fusion.refs_0_, f32[32,384]{1,0:T(8,128)S(1)} %collective-permute-done.10.refs_1_, f32[32,384]{1,0:T(8,128)S(1)} %collective-permute-done.11.refs_2_, f32[32,384]{1,0:T(8,128)S(1)} %collective-permute-done.12.refs_3_, ...), custom_call_target="tpu_custom_call" | custom-call | tf_op jit(solution)/shard_map/pallas_call | solution.py:311
  (16 shorter events, 0.0 us)
Async XLA Ops:
  0.0 1.0 %copy-start = (f32[8,16,768]{2,1,0:T(8,128)S(1)}, f32[8,16,768]{2,1,0:T(8,128)}, u32[]{:S(2)}) copy-start(f32[8,16,768]{2,1,0:T(8,128)} %x_hbm.1) | copy-start | bytes 1179652
  1.0 0.7 %copy-start.2 = (s32[8]{0:T(128)S(1)}, s32[8]{0:T(128)}, u32[]{:S(2)}) copy-start(s32[8]{0:T(128)} %owner_ref.1) | copy-start | bytes 100
  1.7 28.9 %copy-start.7 = (f32[384]{0:T(512)S(1)}, f32[384]{0:T(512)}, u32[]{:S(2)}) copy-start(f32[384]{0:T(512)} %param.13) | copy-start | bytes 4612
  1.7 28.9 %copy-start.1 = (f32[128,384]{1,0:T(8,128)S(1)}, f32[128,384]{1,0:T(8,128)}, u32[]{:S(2)}) copy-start(f32[128,384]{1,0:T(8,128)} %coef_ref.1) | copy-start | bytes 589828
  1.7 28.9 %copy-start.3 = (s32[8]{0:T(128)S(1)}, s32[8]{0:T(128)}, u32[]{:S(2)}) copy-start(s32[8]{0:T(128)} %owner_ref.1) | copy-start | bytes 100
  1.7 28.9 %copy-start.4 = (s32[16]{0:T(128)S(1)}, s32[16]{0:T(128)}, u32[]{:S(2)}) copy-start(s32[16]{0:T(128)} %size_ref.1) | copy-start | bytes 196
  1.7 28.9 %copy-start.5 = (s32[16]{0:T(128)S(1)}, s32[16]{0:T(128)}, u32[]{:S(2)}) copy-start(s32[16]{0:T(128)} %shell_ref.1) | copy-start | bytes 196
  1.7 28.9 %copy-start.6 = (f32[8]{0:T(128)S(1)}, f32[8]{0:T(128)}, u32[]{:S(2)}) copy-start(f32[8]{0:T(128)} %energy_ref.1) | copy-start | bytes 100
  2.3 8.7 %collective-permute-start.1 = (f32[4,16,768]{2,1,0:T(8,128)S(1)}, f32[4,16,768]{2,1,0:T(8,128)S(1)}, u32[]{:S(2)}, u32[]{:S(2)}) collective-permute-start(f32[4,16,768]{2,1,0:T(8,128)S(1)} %get-tuple-element.20), channel_id=1, source_target_pairs={{0,8},{4,12},{8,0},{12,4},{16,24},{20,28},{24,16},{28,20},{1,9},{5... | collective-permute-start | bytes 589832 | tf_op jit(solution)/shard_map/ppermute | solution.py:270
  5.3 10.6 %collective-permute-start.3 = (f32[4,16,768]{2,1,0:T(8,128)S(1)}, f32[4,16,768]{2,1,0:T(8,128)S(1)}, u32[]{:S(2)}, u32[]{:S(2)}) collective-permute-start(f32[4,16,768]{2,1,0:T(8,128)S(1)} %get-tuple-element.21), channel_id=1, source_target_pairs={{0,16},{4,20},{8,24},{12,28},{16,0},{20,4},{24,8},{28,12},{1,17},{... | collective-permute-start | bytes 589832 | tf_op jit(solution)/shard_map/ppermute | solution.py:270
  6.8 9.1 %collective-permute-start.5 = (f32[4,16,768]{2,1,0:T(8,128)S(1)}, f32[4,16,768]{2,1,0:T(8,128)S(1)}, u32[]{:S(2)}, u32[]{:S(2)}) collective-permute-start(f32[4,16,768]{2,1,0:T(8,128)S(1)} %get-tuple-element.22), channel_id=1, source_target_pairs={{0,24},{4,28},{8,16},{12,20},{16,8},{20,12},{24,0},{28,4},{1,25},{... | collective-permute-start | bytes 589832 | tf_op jit(solution)/shard_map/ppermute | solution.py:270
  6.9 9.6 %collective-permute-start = (f32[4,16,768]{2,1,0:T(8,128)S(1)}, f32[4,16,768]{2,1,0:T(8,128)S(1)}, u32[]{:S(2)}, u32[]{:S(2)}) collective-permute-start(f32[4,16,768]{2,1,0:T(8,128)S(1)} %get-tuple-element.19.refs_0_), channel_id=1, source_target_pairs={{0,4},{4,0},{8,12},{12,8},{16,20},{20,16},{24,28},{28,24},{1,5},{5... | collective-permute-start | bytes 589832 | tf_op jit(solution)/shard_map/ppermute | solution.py:271
  11.0 5.4 %collective-permute-start.2 = (f32[4,16,768]{2,1,0:T(8,128)S(1)}, f32[4,16,768]{2,1,0:T(8,128)S(1)}, u32[]{:S(2)}, u32[]{:S(2)}) collective-permute-start(f32[4,16,768]{2,1,0:T(8,128)S(1)} %collective-permute-done.1.refs_2_), channel_id=1, source_target_pairs={{0,4},{4,0},{8,12},{12,8},{16,20},{20,16},{24,28},{28,24},{1,5},{5... | collective-permute-start | bytes 589832 | tf_op jit(solution)/shard_map/ppermute | solution.py:271
  15.9 1.4 %collective-permute-start.4 = (f32[4,16,768]{2,1,0:T(8,128)S(1)}, f32[4,16,768]{2,1,0:T(8,128)S(1)}, u32[]{:S(2)}, u32[]{:S(2)}) collective-permute-start(f32[4,16,768]{2,1,0:T(8,128)S(1)} %collective-permute-done.3.refs_4_), channel_id=1, source_target_pairs={{0,4},{4,0},{8,12},{12,8},{16,20},{20,16},{24,28},{28,24},{1,5},{5... | collective-permute-start | bytes 589832 | tf_op jit(solution)/shard_map/ppermute | solution.py:271
  15.9 1.7 %collective-permute-start.6 = (f32[4,16,768]{2,1,0:T(8,128)S(1)}, f32[4,16,768]{2,1,0:T(8,128)S(1)}, u32[]{:S(2)}, u32[]{:S(2)}) collective-permute-start(f32[4,16,768]{2,1,0:T(8,128)S(1)} %collective-permute-done.5.refs_6_), channel_id=1, source_target_pairs={{0,4},{4,0},{8,12},{12,8},{16,20},{20,16},{24,28},{28,24},{1,5},{5... | collective-permute-start | bytes 589832 | tf_op jit(solution)/shard_map/ppermute | solution.py:271
  18.4 5.9 %collective-permute-start.7 = (f32[32,384]{1,0:T(8,128)S(1)}, f32[32,384]{1,0:T(8,128)S(1)}, u32[]{:S(2)}, u32[]{:S(2)}) collective-permute-start(f32[32,384]{1,0:T(8,128)S(1)} %get-tuple-element.24), channel_id=1, source_target_pairs={{0,1},{1,2},{2,3},{3,0},{4,5},{5,6},{6,7},{7,4},{8,9},{9,10},{10,1... | collective-permute-start | bytes 147464 | tf_op jit(solution)/shard_map/ppermute | solution.py:19
  20.0 6.6 %collective-permute-start.8 = (f32[32,384]{1,0:T(8,128)S(1)}, f32[32,384]{1,0:T(8,128)S(1)}, u32[]{:S(2)}, u32[]{:S(2)}) collective-permute-start(f32[32,384]{1,0:T(8,128)S(1)} %get-tuple-element.25), channel_id=1, source_target_pairs={{0,2},{1,3},{2,0},{3,1},{4,6},{5,7},{6,4},{7,5},{8,10},{9,11},{10,... | collective-permute-start | bytes 147464 | tf_op jit(solution)/shard_map/ppermute | solution.py:19
  22.6 4.3 %collective-permute-start.9 = (f32[32,384]{1,0:T(8,128)S(1)}, f32[32,384]{1,0:T(8,128)S(1)}, u32[]{:S(2)}, u32[]{:S(2)}) collective-permute-start(f32[32,384]{1,0:T(8,128)S(1)} %get-tuple-element.26), channel_id=1, source_target_pairs={{0,3},{1,0},{2,1},{3,2},{4,7},{5,4},{6,5},{7,6},{8,11},{9,8},{10,9... | collective-permute-start | bytes 147464 | tf_op jit(solution)/shard_map/ppermute | solution.py:19
  26.9 4.9 %collective-permute-start.12 = (f32[32,384]{1,0:T(8,128)S(1)}, f32[32,384]{1,0:T(8,128)S(1)}, u32[]{:S(2)}, u32[]{:S(2)}) collective-permute-start(f32[32,384]{1,0:T(8,128)S(1)} %add_add_fusion.refs_0_), channel_id=1, source_target_pairs={{0,3},{1,0},{2,1},{3,2},{4,7},{5,4},{6,5},{7,6},{8,11},{9,8},{10,9... | collective-permute-start | bytes 147464 | tf_op jit(solution)/shard_map/ppermute | solution.py:19
  29.9 5.0 %collective-permute-start.11 = (f32[32,384]{1,0:T(8,128)S(1)}, f32[32,384]{1,0:T(8,128)S(1)}, u32[]{:S(2)}, u32[]{:S(2)}) collective-permute-start(f32[32,384]{1,0:T(8,128)S(1)} %add_add_fusion.refs_0_), channel_id=1, source_target_pairs={{0,2},{1,3},{2,0},{3,1},{4,6},{5,7},{6,4},{7,5},{8,10},{9,11},{10,... | collective-permute-start | bytes 147464 | tf_op jit(solution)/shard_map/ppermute | solution.py:19
  29.9 5.9 %collective-permute-start.10 = (f32[32,384]{1,0:T(8,128)S(1)}, f32[32,384]{1,0:T(8,128)S(1)}, u32[]{:S(2)}, u32[]{:S(2)}) collective-permute-start(f32[32,384]{1,0:T(8,128)S(1)} %add_add_fusion.refs_0_), channel_id=1, source_target_pairs={{0,1},{1,2},{2,3},{3,0},{4,5},{5,6},{6,7},{7,4},{8,9},{9,10},{10,1... | collective-permute-start | bytes 147464 | tf_op jit(solution)/shard_map/ppermute | solution.py:19

commit v3 on v2

--- a/solution.py
+++ b/solution.py
@@ -10,13 +10,16 @@
 STOPS = 3
 BF16 = jnp.bfloat16
 F32 = jnp.float32
-SELECT_VMEM = 24 * 1024 * 1024
 
 
 def shifted(value, axis, steps):
     count = lax.axis_size(axis)
     pairs = [(source, (source + steps) % count) for source in range(count)]
     return lax.ppermute(value, axis, pairs)
+
+
+def swapped(value, axis, step):
+    return lax.ppermute(value, axis, [(i, i ^ step) for i in range(lax.axis_size(axis))])
 
 
 def live_slots(shell_size, shell_owner, blk_count, slot_cap):
@@ -165,14 +168,12 @@
         gap_ref[pl.ds(stop * virt_count, virt_count), :] = 1.0 / ((both - column) - row)
 
 
-def overlap_kernel(parts, slot_cap, *refs):
-    pieces = refs[: -parts - 3]
-    outs = refs[-parts - 3 : -3]
-    x_high, x_low, total = refs[-3:]
+def overlap_kernel(slot_cap, places, *refs):
+    *pieces, keep, give, x_high, x_low, total = refs
     first = 1 - (lax.axis_index("blk") & 1)
     here = lax.axis_index("aux")
     for stop in range(STOPS):
-        for index, piece in enumerate(pieces):
+        for index, piece in zip(places, pieces):
             high, low = halves(piece[first + stop])
             rows = pl.ds((stop * len(pieces) + index) * slot_cap, slot_cap)
             x_high[rows, :] = high
@@ -190,22 +191,25 @@
         if stop > 0:
             gram = 2.0 * gram - gram.T
         total[:, rows] = gram
-    share = slots // parts
-    for step, out in enumerate(outs):
-        row = pl.multiple_of(lax.rem(here + step, parts) * share, share)
-        out[...] = total[pl.ds(row, share), :]
-
-
-def density_kernel(parts, *refs):
+    half = slots // 2
+    mine = here & 1
+    keep[...] = total[pl.ds(pl.multiple_of(mine * half, half), half), :]
+    give[...] = total[pl.ds(pl.multiple_of((1 - mine) * half, half), half), :]
+
+
+def density_kernel(steps, *refs):
+    parts = len(steps)
     shares = refs[:parts]
     left, right, back, gap, x_high, x_low, out, total, w_high, w_low, density, sems = refs[parts:]
     here = lax.axis_index("aux")
     slots = total.shape[0]
-    share = slots // parts
+    half = slots // 2
     virt_count = out.shape[0]
-    for step, piece in enumerate(shares):
-        row = pl.multiple_of(lax.rem(here + parts - step, parts) * share, share)
-        total[pl.ds(row, share), :] = piece[...]
+    for other in range(2):
+        row = pl.multiple_of((here & 1 ^ other) * half, half)
+        total[pl.ds(row, half), :] = sum(
+            piece[...] for step, piece in zip(steps, shares) if step & 1 == other
+        )
     high, low = halves(total[...])
     half_done = matmul(left[...], jnp.concatenate([high, low, high], axis=0))
     half_done = jnp.concatenate(
@@ -256,8 +260,8 @@
             pltpu.SemaphoreType.DMA,
             pltpu.SemaphoreType.DMA,
         ],
-        compiler_params=pltpu.CompilerParams(vmem_limit_bytes=SELECT_VMEM),
-    )(occ_owner, occupied_integrals)
+        compiler_params=params,
+    )(*[pltpu.with_memory_space_constraint(a, pltpu.HBM) for a in (occ_owner, occupied_integrals)])
 
     pieces = []
     for step, piece in enumerate(sent):
@@ -268,7 +272,7 @@
                 for core in range(2)
             ]
             piece = lax.ppermute(piece, "blk", pairs)
-        pieces += [piece, lax.ppermute(piece, "blk", [(i, i ^ 1) for i in range(blk_count)])]
+        pieces += [piece, swapped(piece, "blk", 1)]
 
     left, right, back, gap = pl.pallas_call(
         functools.partial(coefficient_kernel, blk_count),
@@ -291,25 +295,24 @@
         e_virt.reshape(1, virt_count),
     )
 
-    share = slots // parts
-    *shares, x_high, x_low = pl.pallas_call(
-        functools.partial(overlap_kernel, parts, slot_cap),
-        out_shape=[jax.ShapeDtypeStruct((share, STOPS * slots), F32)] * parts
+    places = [2 * step + core for step in reversed(range(chips)) for core in range(2)]
+    keep, give, x_high, x_low = pl.pallas_call(
+        functools.partial(overlap_kernel, slot_cap, places),
+        out_shape=[jax.ShapeDtypeStruct((slots // 2, STOPS * slots), F32)] * 2
         + [jax.ShapeDtypeStruct((STOPS * slots, aux_width), BF16)] * 2,
         in_specs=[vmem] * len(pieces),
-        out_specs=[vmem] * (parts + 2),
+        out_specs=[vmem] * 4,
         scratch_shapes=[pltpu.VMEM((slots, STOPS * slots), F32)],
         compiler_params=params,
-    )(*pieces)
-
-    mine = shares[0]
-    for step in range(1, parts):
-        mine = mine + shifted(shares[step], "aux", step)
-    gathered = [mine] + [shifted(mine, "aux", step) for step in range(1, parts)]
+    )(*[pieces[place] for place in places])
+
+    mine = keep + swapped(give, "aux", 1)
+    steps = [0, *range(1, parts, 2), *range(2, parts, 2)]
+    gathered = [swapped(mine, "aux", step) if step else mine for step in steps]
 
     bands = 3 if virt_count % 48 == 0 else 1
     density = pl.pallas_call(
-        functools.partial(density_kernel, parts),
+        functools.partial(density_kernel, steps),
         out_shape=jax.ShapeDtypeStruct((virt_count, aux_width), F32),
         in_specs=[vmem] * (parts + 6),
         out_specs=pl.BlockSpec(memory_space=pl.ANY),
@@ -329,7 +332,8 @@
     blk_count = lax.axis_size("blk")
     slots, virt_count = virtual_coefficients.shape
     paired = blk_count % 2 == 0 and blk_count == occupied_integrals.shape[0]
-    shared = slots % (lax.axis_size("aux") * 16) == 0 and slots <= virt_count
+    parts = lax.axis_size("aux")
+    shared = parts > 1 and parts & (parts - 1) == 0 and slots % 32 == 0 and slots <= virt_count
     run = slots_first if paired and shared else transformed_first
     return run(occupied_integrals, virtual_coefficients, *rest)
 

time: 39.1 us -> 35.7 us (0.913)
  starting transfers between devices: 14.2 us -> 11.1 us
  local copies, waits for them, and re-layouts: 1.68 us -> 0.02 us
  waiting for transfers between devices: 17.2 us -> 18 us
  Pallas kernels: 5.75 us -> 6.32 us
    ppermute x10 -> x8, starting transfers between devices: 9.71 us -> 6.46 us  [swapped(): lax.ppermute(value, axis, [(i, i ^ step) for i in range(lax.axis_size(axi...]
    unnamed x16 -> x12, local copies, waits for them, and re-layouts: 1.67 us -> 0.02 us
    ppermute x10 -> x8, waiting for transfers between devices: 8.13 us -> 9.29 us  [swapped(): lax.ppermute(value, axis, [(i, i ^ step) for i in range(lax.axis_size(axi...]
    pallas_call x1, Pallas kernels: 0.62 us -> 1.17 us  [slots_first(): pl.pallas_call(functools.partial(select_kernel, blk_count), out_shape=[ja...]
  transfers between devices with their start and end apart: 13 -> 11, of which waited for: 9 -> 8; matrix products, arithmetic and copies ran while one was open for 0% -> 0% of each run, Pallas kernels for 3% -> 3%
where the time goes in v3:
time: 35.7 us; the launch traced here: 35.5 us
  waiting for transfers between devices  18 us (50%)
  starting transfers between devices  11.1 us (31%)
  Pallas kernels  6.32 us (18%)
    ppermute x8, waiting for transfers between devices, swapped(): lax.ppermute(value, axis, [(i, i ^ step) for i in range(lax.axis_size(axi...  9.29 us
    ppermute x3, waiting for transfers between devices, slots_first(): piece = lax.ppermute(piece, 'blk', pairs)  8.74 us
    ppermute x8, starting transfers between devices, swapped(): lax.ppermute(value, axis, [(i, i ^ step) for i in range(lax.axis_size(axi...  6.46 us
    ppermute x3, starting transfers between devices, slots_first(): piece = lax.ppermute(piece, 'blk', pairs)  4.6 us
    pallas_call x1, Pallas kernels, slots_first(): pl.pallas_call(functools.partial(density_kernel, steps), out_shape=jax.Sh...  3.17 us
    pallas_call x1, Pallas kernels, slots_first(): pl.pallas_call(functools.partial(coefficient_kernel, blk_count), out_shap...  1.21 us
    pallas_call x1, Pallas kernels, slots_first(): pl.pallas_call(functools.partial(select_kernel, blk_count), out_shape=[ja...  1.17 us
    pallas_call x1, Pallas kernels, slots_first(): pl.pallas_call(functools.partial(overlap_kernel, slot_cap, places), out_s...  0.76 us
  transfers between devices with their start and end apart: 11, of which 8 were waited for; matrix products, arithmetic and copies ran while one was open for 0% of the time, Pallas kernels for 3%

profile of v3, /device:TPU:0, one launch (start us, length us, event | category | flops | bytes accessed | tf_op | source)
XLA Modules:
  0.0 35.5 jit_solution(4363524164450179255)
XLA Ops:
  0.0 0.0 copy-start
  0.0 1.2 %shard_map.73 = (f32[4,16,768]{2,1,0:T(8,128)S(1)}, f32[4,16,768]{2,1,0:T(8,128)S(1)}, f32[4,16,768]{2,1,0:T(8,128)S(1)}, f32[4,16,768]{2,1,0:T(8,128)S(1)}) custom-call(s32[8]{0:T(128)} %owner_ref.1, f32[8,16,768]{2,1,0:T(8,128)} %x_hbm.1), custom_call_target="tpu_custom_call" | custom-call | tf_op jit(solution)/shard_map/pallas_call | solution.py:252
  1.2 4.0 %collective-permute-start = (f32[4,16,768]{2,1,0:T(8,128)S(1)}, f32[4,16,768]{2,1,0:T(8,128)S(1)}, u32[]{:S(2)}, u32[]{:S(2)}) collective-permute-start(f32[4,16,768]{2,1,0:T(8,128)S(1)} %get-tuple-element.17), channel_id=1, source_target_pairs={{0,24},{4,28},{8,16},{12,20},{16,8},{20,12},{24,0},{28,4},{1,25},{... | collective-permute-start | bytes 589832 | tf_op jit(solution)/shard_map/ppermute | solution.py:274
  5.2 0.5 %collective-permute-start.2 = (f32[4,16,768]{2,1,0:T(8,128)S(1)}, f32[4,16,768]{2,1,0:T(8,128)S(1)}, u32[]{:S(2)}, u32[]{:S(2)}) collective-permute-start(f32[4,16,768]{2,1,0:T(8,128)S(1)} %get-tuple-element.18), channel_id=1, source_target_pairs={{0,16},{4,20},{8,24},{12,28},{16,0},{20,4},{24,8},{28,12},{1,17},{... | collective-permute-start | bytes 589832 | tf_op jit(solution)/shard_map/ppermute | solution.py:274
  5.7 0.1 collective-permute-start.4
  5.8 0.0 collective-permute-start.6
  5.8 5.1 %collective-permute-done.refs_0_ = f32[4,16,768]{2,1,0:T(8,128)S(1)} collective-permute-done((f32[4,16,768]{2,1,0:T(8,128)S(1)}, f32[4,16,768]{2,1,0:T(8,128)S(1)}, u32[]{:S(2)}, u32[]{:S(2)}) %collective-permute-start) | collective-permute-done | bytes 196640 | tf_op jit(solution)/shard_map/ppermute | solution.py:274
  10.9 0.0 collective-permute-start.1
  10.9 3.3 %collective-permute-done.2.refs_2_ = f32[4,16,768]{2,1,0:T(8,128)S(1)} collective-permute-done((f32[4,16,768]{2,1,0:T(8,128)S(1)}, f32[4,16,768]{2,1,0:T(8,128)S(1)}, u32[]{:S(2)}, u32[]{:S(2)}) %collective-permute-start.2) | collective-permute-done | bytes 196640 | tf_op jit(solution)/shard_map/ppermute | solution.py:274
  14.3 0.0 collective-permute-start.3
  14.3 0.3 collective-permute-done.4.refs_4_
  14.6 0.2 collective-permute-start.5
  14.8 0.0 collective-permute-done.6.refs_7_
  14.8 0.0 collective-permute-done.1.refs_1_
  14.8 0.9 %collective-permute-done.3.refs_3_ = f32[4,16,768]{2,1,0:T(8,128)S(1)} collective-permute-done((f32[4,16,768]{2,1,0:T(8,128)S(1)}, f32[4,16,768]{2,1,0:T(8,128)S(1)}, u32[]{:S(2)}, u32[]{:S(2)}) %collective-permute-start.3) | collective-permute-done | bytes 196640 | tf_op jit(solution)/shard_map/ppermute | solution.py:22
  15.7 0.3 collective-permute-done.5.refs_5_
  16.0 0.8 %shard_map.74 = (f32[64,384]{1,0:T(8,128)S(1)}, f32[64,384]{1,0:T(8,128)S(1)}, bf16[384,768]{1,0:T(8,128)(2,1)S(1)}, bf16[384,768]{1,0:T(8,128)(2,1)S(1)}) custom-call(f32[4,16,768]{2,1,0:T(8,128)S(1)} %collective-permute-done.refs_0_, f32[4,16,768]{2,1,0:T(8,128)S(1)} %collective-permute-done.1.refs_1_, f32[4,16,768]{2,1,0:T(8,128)S(1)} %collective-permute-done.2.refs_2_, ...), custom_call_target="tpu_custom_call" | custom-call | tf_op jit(solution)/shard_map/pallas_call | solution.py:299
  16.8 1.8 %collective-permute-start.7 = (f32[64,384]{1,0:T(8,128)S(1)}, f32[64,384]{1,0:T(8,128)S(1)}, u32[]{:S(2)}, u32[]{:S(2)}) collective-permute-start(f32[64,384]{1,0:T(8,128)S(1)} %get-tuple-element.22), channel_id=1, source_target_pairs={{0,1},{1,0},{2,3},{3,2},{4,5},{5,4},{6,7},{7,6},{8,9},{9,8},{10,11... | collective-permute-start | bytes 294920 | tf_op jit(solution)/shard_map/ppermute | solution.py:22
  18.6 3.2 %collective-permute-done.7 = f32[64,384]{1,0:T(8,128)S(1)} collective-permute-done((f32[64,384]{1,0:T(8,128)S(1)}, f32[64,384]{1,0:T(8,128)S(1)}, u32[]{:S(2)}, u32[]{:S(2)}) %collective-permute-start.7) | collective-permute-done | bytes 98336 | tf_op jit(solution)/shard_map/ppermute | solution.py:22
  21.8 2.8 %collective-permute-start.10 = (f32[64,384]{1,0:T(8,128)S(1)}, f32[64,384]{1,0:T(8,128)S(1)}, u32[]{:S(2)}, u32[]{:S(2)}) collective-permute-start(f32[64,384]{1,0:T(8,128)S(1)} %add.3.refs_0_), channel_id=1, source_target_pairs={{0,2},{1,3},{2,0},{3,1},{4,6},{5,7},{6,4},{7,5},{8,10},{9,11},{10,... | collective-permute-start | bytes 294920 | tf_op jit(solution)/shard_map/ppermute | solution.py:22
  24.6 1.3 %collective-permute-start.9 = (f32[64,384]{1,0:T(8,128)S(1)}, f32[64,384]{1,0:T(8,128)S(1)}, u32[]{:S(2)}, u32[]{:S(2)}) collective-permute-start(f32[64,384]{1,0:T(8,128)S(1)} %add.3.refs_0_), channel_id=1, source_target_pairs={{0,3},{1,2},{2,1},{3,0},{4,7},{5,6},{6,5},{7,4},{8,11},{9,10},{10,... | collective-permute-start | bytes 294920 | tf_op jit(solution)/shard_map/ppermute | solution.py:22
  26.0 0.2 collective-permute-start.8
  26.2 0.0 copy-done.5
  26.2 0.0 copy-done.4
  26.2 0.0 copy-done.3
  26.2 0.0 copy-done.2
  26.2 0.0 copy-done
  26.3 1.2 %shard_map.75 = (bf16[384,384]{1,0:T(8,128)(2,1)S(1)}, bf16[384,384]{1,0:T(8,128)(2,1)S(1)}, bf16[384,256]{1,0:T(8,128)(2,1)S(1)}, f32[1152,384]{1,0:T(8,128)S(1)}) custom-call(s32[16]{0:T(128)S(1)} %copy-done.2, s32[16]{0:T(128)S(1)} %copy-done.3, s32[8]{0:T(128)S(1)} %copy-done.1, f32[8]{0:T(128)S(1)} %copy-done.4, f32[128,384]{1,0:T(8,128)S(1)} %copy-done, ...), custom_call_target="tpu_custom_call" | custom-call | tf_op jit(solution)/shard_map/pallas_call | solution.py:277
  27.5 4.4 %collective-permute-done.10.refs_3_ = f32[64,384]{1,0:T(8,128)S(1)} collective-permute-done((f32[64,384]{1,0:T(8,128)S(1)}, f32[64,384]{1,0:T(8,128)S(1)}, u32[]{:S(2)}, u32[]{:S(2)}) %collective-permute-start.10) | collective-permute-done | bytes 98336 | tf_op jit(solution)/shard_map/ppermute | solution.py:22
  31.9 0.0 collective-permute-done.9.refs_2_
  31.9 0.4 %collective-permute-done.8.refs_1_ = f32[64,384]{1,0:T(8,128)S(1)} collective-permute-done((f32[64,384]{1,0:T(8,128)S(1)}, f32[64,384]{1,0:T(8,128)S(1)}, u32[]{:S(2)}, u32[]{:S(2)}) %collective-permute-start.8) | collective-permute-done | bytes 98336 | tf_op jit(solution)/shard_map/ppermute | solution.py:22
  32.3 3.2 %shard_map.76 = f32[384,768]{1,0:T(8,128)} custom-call(f32[64,384]{1,0:T(8,128)S(1)} %add.3.refs_0_, f32[64,384]{1,0:T(8,128)S(1)} %collective-permute-done.8.refs_1_, f32[64,384]{1,0:T(8,128)S(1)} %collective-permute-done.9.refs_2_, f32[64,384]{1,0:T(8,128)S(1)} %collective-permute-done.10.refs_3_, bf16[384,384]{1,0:T(8,128)(2,1)S(1)} %get-tuple-element.23.refs_4_, ...), custom_call_target="tpu_custom_call" | custom-call | tf_op jit(solution)/shard_map/pallas_call | solution.py:314
  (8 shorter events, 0.0 us)
Async XLA Ops:
  0.0 26.2 %copy-start.1 = (s32[8]{0:T(128)S(1)}, s32[8]{0:T(128)}, u32[]{:S(2)}) copy-start(s32[8]{0:T(128)} %owner_ref.1) | copy-start | bytes 100
  0.0 26.2 %copy-start.5 = (f32[384]{0:T(512)S(1)}, f32[384]{0:T(512)}, u32[]{:S(2)}) copy-start(f32[384]{0:T(512)} %param.13) | copy-start | bytes 4612
  0.0 26.2 %copy-start.4 = (f32[8]{0:T(128)S(1)}, f32[8]{0:T(128)}, u32[]{:S(2)}) copy-start(f32[8]{0:T(128)} %energy_ref.1) | copy-start | bytes 100
  0.0 26.2 %copy-start.3 = (s32[16]{0:T(128)S(1)}, s32[16]{0:T(128)}, u32[]{:S(2)}) copy-start(s32[16]{0:T(128)} %shell_ref.1) | copy-start | bytes 196
  0.0 26.2 %copy-start.2 = (s32[16]{0:T(128)S(1)}, s32[16]{0:T(128)}, u32[]{:S(2)}) copy-start(s32[16]{0:T(128)} %size_ref.1) | copy-start | bytes 196
  0.0 26.2 %copy-start = (f32[128,384]{1,0:T(8,128)S(1)}, f32[128,384]{1,0:T(8,128)}, u32[]{:S(2)}) copy-start(f32[128,384]{1,0:T(8,128)} %coef_ref.1) | copy-start | bytes 589828
  1.2 9.7 %collective-permute-start = (f32[4,16,768]{2,1,0:T(8,128)S(1)}, f32[4,16,768]{2,1,0:T(8,128)S(1)}, u32[]{:S(2)}, u32[]{:S(2)}) collective-permute-start(f32[4,16,768]{2,1,0:T(8,128)S(1)} %get-tuple-element.17), channel_id=1, source_target_pairs={{0,24},{4,28},{8,16},{12,20},{16,8},{20,12},{24,0},{28,4},{1,25},{... | collective-permute-start | bytes 589832 | tf_op jit(solution)/shard_map/ppermute | solution.py:274
  5.2 9.1 %collective-permute-start.2 = (f32[4,16,768]{2,1,0:T(8,128)S(1)}, f32[4,16,768]{2,1,0:T(8,128)S(1)}, u32[]{:S(2)}, u32[]{:S(2)}) collective-permute-start(f32[4,16,768]{2,1,0:T(8,128)S(1)} %get-tuple-element.18), channel_id=1, source_target_pairs={{0,16},{4,20},{8,24},{12,28},{16,0},{20,4},{24,8},{28,12},{1,17},{... | collective-permute-start | bytes 589832 | tf_op jit(solution)/shard_map/ppermute | solution.py:274
  5.7 8.9 %collective-permute-start.4 = (f32[4,16,768]{2,1,0:T(8,128)S(1)}, f32[4,16,768]{2,1,0:T(8,128)S(1)}, u32[]{:S(2)}, u32[]{:S(2)}) collective-permute-start(f32[4,16,768]{2,1,0:T(8,128)S(1)} %get-tuple-element.19), channel_id=1, source_target_pairs={{0,8},{4,12},{8,0},{12,4},{16,24},{20,28},{24,16},{28,20},{1,9},{5... | collective-permute-start | bytes 589832 | tf_op jit(solution)/shard_map/ppermute | solution.py:274
  5.8 9.0 %collective-permute-start.6 = (f32[4,16,768]{2,1,0:T(8,128)S(1)}, f32[4,16,768]{2,1,0:T(8,128)S(1)}, u32[]{:S(2)}, u32[]{:S(2)}) collective-permute-start(f32[4,16,768]{2,1,0:T(8,128)S(1)} %get-tuple-element.20.refs_6_), channel_id=1, source_target_pairs={{0,4},{4,0},{8,12},{12,8},{16,20},{20,16},{24,28},{28,24},{1,5},{5... | collective-permute-start | bytes 589832 | tf_op jit(solution)/shard_map/ppermute | solution.py:22
  10.9 3.9 %collective-permute-start.1 = (f32[4,16,768]{2,1,0:T(8,128)S(1)}, f32[4,16,768]{2,1,0:T(8,128)S(1)}, u32[]{:S(2)}, u32[]{:S(2)}) collective-permute-start(f32[4,16,768]{2,1,0:T(8,128)S(1)} %collective-permute-done.refs_0_), channel_id=1, source_target_pairs={{0,4},{4,0},{8,12},{12,8},{16,20},{20,16},{24,28},{28,24},{1,5},{5... | collective-permute-start | bytes 589832 | tf_op jit(solution)/shard_map/ppermute | solution.py:22
  14.3 1.4 %collective-permute-start.3 = (f32[4,16,768]{2,1,0:T(8,128)S(1)}, f32[4,16,768]{2,1,0:T(8,128)S(1)}, u32[]{:S(2)}, u32[]{:S(2)}) collective-permute-start(f32[4,16,768]{2,1,0:T(8,128)S(1)} %collective-permute-done.2.refs_2_), channel_id=1, source_target_pairs={{0,4},{4,0},{8,12},{12,8},{16,20},{20,16},{24,28},{28,24},{1,5},{5... | collective-permute-start | bytes 589832 | tf_op jit(solution)/shard_map/ppermute | solution.py:22
  14.6 1.4 %collective-permute-start.5 = (f32[4,16,768]{2,1,0:T(8,128)S(1)}, f32[4,16,768]{2,1,0:T(8,128)S(1)}, u32[]{:S(2)}, u32[]{:S(2)}) collective-permute-start(f32[4,16,768]{2,1,0:T(8,128)S(1)} %collective-permute-done.4.refs_4_), channel_id=1, source_target_pairs={{0,4},{4,0},{8,12},{12,8},{16,20},{20,16},{24,28},{28,24},{1,5},{5... | collective-permute-start | bytes 589832 | tf_op jit(solution)/shard_map/ppermute | solution.py:22
  16.8 5.0 %collective-permute-start.7 = (f32[64,384]{1,0:T(8,128)S(1)}, f32[64,384]{1,0:T(8,128)S(1)}, u32[]{:S(2)}, u32[]{:S(2)}) collective-permute-start(f32[64,384]{1,0:T(8,128)S(1)} %get-tuple-element.22), channel_id=1, source_target_pairs={{0,1},{1,0},{2,3},{3,2},{4,5},{5,4},{6,7},{7,6},{8,9},{9,8},{10,11... | collective-permute-start | bytes 294920 | tf_op jit(solution)/shard_map/ppermute | solution.py:22
  21.8 10.1 %collective-permute-start.10 = (f32[64,384]{1,0:T(8,128)S(1)}, f32[64,384]{1,0:T(8,128)S(1)}, u32[]{:S(2)}, u32[]{:S(2)}) collective-permute-start(f32[64,384]{1,0:T(8,128)S(1)} %add.3.refs_0_), channel_id=1, source_target_pairs={{0,2},{1,3},{2,0},{3,1},{4,6},{5,7},{6,4},{7,5},{8,10},{9,11},{10,... | collective-permute-start | bytes 294920 | tf_op jit(solution)/shard_map/ppermute | solution.py:22
  24.6 7.3 %collective-permute-start.9 = (f32[64,384]{1,0:T(8,128)S(1)}, f32[64,384]{1,0:T(8,128)S(1)}, u32[]{:S(2)}, u32[]{:S(2)}) collective-permute-start(f32[64,384]{1,0:T(8,128)S(1)} %add.3.refs_0_), channel_id=1, source_target_pairs={{0,3},{1,2},{2,1},{3,0},{4,7},{5,6},{6,5},{7,4},{8,11},{9,10},{10,... | collective-permute-start | bytes 294920 | tf_op jit(solution)/shard_map/ppermute | solution.py:22
  26.0 6.4 %collective-permute-start.8 = (f32[64,384]{1,0:T(8,128)S(1)}, f32[64,384]{1,0:T(8,128)S(1)}, u32[]{:S(2)}, u32[]{:S(2)}) collective-permute-start(f32[64,384]{1,0:T(8,128)S(1)} %add.3.refs_0_), channel_id=1, source_target_pairs={{0,1},{1,0},{2,3},{3,2},{4,5},{5,4},{6,7},{7,6},{8,9},{9,8},{10,11... | collective-permute-start | bytes 294920 | tf_op jit(solution)/shard_map/ppermute | solution.py:22

commit v4 on v3

--- a/solution.py
+++ b/solution.py
@@ -169,7 +169,7 @@
 
 
 def overlap_kernel(slot_cap, places, *refs):
-    *pieces, keep, give, x_high, x_low, total = refs
+    *pieces, keep, give, x_high, x_low, total, folded = refs
     first = 1 - (lax.axis_index("blk") & 1)
     here = lax.axis_index("aux")
     for stop in range(STOPS):
@@ -179,37 +179,63 @@
             x_high[rows, :] = high
             x_low[rows, :] = low
     slots = slot_cap * len(pieces)
-    own_high, own_low = x_high[:slots, :], x_low[:slots, :]
-    for stop in range(STOPS):
-        rows = pl.ds(stop * slots, slots)
-        high = x_high[rows, :]
-        gram = (
-            matmul_nt(own_high, high)
-            + matmul_nt(own_high, x_low[rows, :])
-            + matmul_nt(own_low, high)
-        )
-        if stop > 0:
-            gram = 2.0 * gram - gram.T
-        total[:, rows] = gram
-    half = slots // 2
-    mine = here & 1
-    keep[...] = total[pl.ds(pl.multiple_of(mine * half, half), half), :]
-    give[...] = total[pl.ds(pl.multiple_of((1 - mine) * half, half), half), :]
+    own = jnp.concatenate([x_high[:slots, :], x_low[:slots, :]], axis=0)
+    both = matmul_nt(own, x_high[...])
+    gram = both[:slots] + both[slots:] + matmul_nt(x_high[:slots, :], x_low[...])
+    half, band, thin = slots // 2, slots // 4, slots // 8
+    for stop in range(1, STOPS):
+        square = gram[:, stop * slots : (stop + 1) * slots]
+        total[stop - 1] = 2.0 * square - square.T
+    square = gram[:, :slots]
+    lanes = lax.broadcasted_iota(jnp.int32, (band, slots), 1)
+    folded[:band, :] = square[:band]
+    folded[band:half, :] = jnp.where(
+        lanes < band, pltpu.roll(square[half + band :], band, 1), square[band:half]
+    )
+    folded[half:, :] = jnp.where(
+        lanes[:thin] < half,
+        pltpu.roll(square[half + thin : half + band], half, 1),
+        square[half : half + thin],
+    )
+    rest = folded.shape[0] // 2
+    for out, part in ((keep, here & 1), (give, 1 - (here & 1))):
+        rows = pl.ds(pl.multiple_of(part * half, half), half)
+        for stop in range(STOPS - 1):
+            out[pl.ds(stop * half, half), :] = total[stop, rows, :]
+        out[pl.ds((STOPS - 1) * half, rest), :] = folded[
+            pl.ds(pl.multiple_of(part * rest, 8), rest), :
+        ]
 
 
 def density_kernel(steps, *refs):
     parts = len(steps)
     shares = refs[:parts]
-    left, right, back, gap, x_high, x_low, out, total, w_high, w_low, density, sems = refs[parts:]
+    left, right, back, gap, x_high, x_low, out, total, folded, w_high, w_low, density, sems = refs[parts:]
     here = lax.axis_index("aux")
     slots = total.shape[0]
     half = slots // 2
     virt_count = out.shape[0]
+    band, rest = slots // 4, folded.shape[0] // 2
     for other in range(2):
-        row = pl.multiple_of((here & 1 ^ other) * half, half)
-        total[pl.ds(row, half), :] = sum(
-            piece[...] for step, piece in zip(steps, shares) if step & 1 == other
-        )
+        part = here & 1 ^ other
+        rows = pl.ds(pl.multiple_of(part * half, half), half)
+        share = sum(piece[...] for step, piece in zip(steps, shares) if step & 1 == other)
+        for stop in range(1, STOPS):
+            total[rows, stop * slots : (stop + 1) * slots] = share[(stop - 1) * half : stop * half]
+        folded[pl.ds(pl.multiple_of(part * rest, 8), rest), :] = share[(STOPS - 1) * half :]
+    last = folded[half:, :]
+    upper = jnp.concatenate(
+        [
+            folded[:half, :],
+            last,
+            pltpu.roll(last, half, 1),
+            pltpu.roll(folded[band:half, :], slots - band, 1),
+        ],
+        axis=0,
+    )
+    row_band = lax.broadcasted_iota(jnp.int32, (slots, slots), 0) // band
+    lane_band = lax.broadcasted_iota(jnp.int32, (slots, slots), 1) // band
+    total[:, :slots] = jnp.where(lane_band >= row_band, upper, upper.T)
     high, low = halves(total[...])
     half_done = matmul(left[...], jnp.concatenate([high, low, high], axis=0))
     half_done = jnp.concatenate(
@@ -295,14 +321,18 @@
         e_virt.reshape(1, virt_count),
     )
 
+    fold = 5 * slots // 8
     places = [2 * step + core for step in reversed(range(chips)) for core in range(2)]
     keep, give, x_high, x_low = pl.pallas_call(
         functools.partial(overlap_kernel, slot_cap, places),
-        out_shape=[jax.ShapeDtypeStruct((slots // 2, STOPS * slots), F32)] * 2
+        out_shape=[jax.ShapeDtypeStruct(((STOPS - 1) * slots // 2 + fold // 2, slots), F32)] * 2
         + [jax.ShapeDtypeStruct((STOPS * slots, aux_width), BF16)] * 2,
         in_specs=[vmem] * len(pieces),
         out_specs=[vmem] * 4,
-        scratch_shapes=[pltpu.VMEM((slots, STOPS * slots), F32)],
+        scratch_shapes=[
+            pltpu.VMEM((STOPS - 1, slots, slots), F32),
+            pltpu.VMEM((fold, slots), F32),
+        ],
         compiler_params=params,
     )(*[pieces[place] for place in places])
 
@@ -318,6 +348,7 @@
         out_specs=pl.BlockSpec(memory_space=pl.ANY),
         scratch_shapes=[
             pltpu.VMEM((slots, STOPS * slots), F32),
+            pltpu.VMEM((fold, slots), F32),
             pltpu.VMEM((virt_count, STOPS * slots), BF16),
             pltpu.VMEM((virt_count, STOPS * slots), BF16),
             pltpu.VMEM((virt_count, aux_width), F32),
@@ -333,7 +364,7 @@
     slots, virt_count = virtual_coefficients.shape
     paired = blk_count % 2 == 0 and blk_count == occupied_integrals.shape[0]
     parts = lax.axis_size("aux")
-    shared = parts > 1 and parts & (parts - 1) == 0 and slots % 32 == 0 and slots <= virt_count
+    shared = parts > 1 and parts & (parts - 1) == 0 and slots % 128 == 0 and slots <= virt_count
     run = slots_first if paired and shared else transformed_first
     return run(occupied_integrals, virtual_coefficients, *rest)
 

time: 35.7 us -> 34.7 us (0.972)
  waiting for transfers between devices: 18 us -> 17.1 us
    ppermute x8, waiting for transfers between devices: 9.29 us -> 8.33 us  [swapped(): lax.ppermute(value, axis, [(i, i ^ step) for i in range(lax.axis_size(axi...]
  transfers between devices with their start and end apart: 11 -> 11, of which waited for: 8 -> 9; matrix products, arithmetic and copies ran while one was open for 0% -> 0% of each run, Pallas kernels for 3% -> 3%
where the time goes in v4:
time: 34.7 us; the launch traced here: 34.6 us
  waiting for transfers between devices  17.1 us (49%)
  starting transfers between devices  11.1 us (32%)
  Pallas kernels  6.35 us (18%)
    ppermute x3, waiting for transfers between devices, slots_first(): piece = lax.ppermute(piece, 'blk', pairs)  8.74 us
    ppermute x8, waiting for transfers between devices, swapped(): lax.ppermute(value, axis, [(i, i ^ step) for i in range(lax.axis_size(axi...  8.33 us
    ppermute x8, starting transfers between devices, swapped(): lax.ppermute(value, axis, [(i, i ^ step) for i in range(lax.axis_size(axi...  6.46 us
    ppermute x3, starting transfers between devices, slots_first(): piece = lax.ppermute(piece, 'blk', pairs)  4.6 us
    pallas_call x1, Pallas kernels, slots_first(): pl.pallas_call(functools.partial(density_kernel, steps), out_shape=jax.Sh...  3.29 us
    pallas_call x1, Pallas kernels, slots_first(): pl.pallas_call(functools.partial(coefficient_kernel, blk_count), out_shap...  1.21 us
    pallas_call x1, Pallas kernels, slots_first(): pl.pallas_call(functools.partial(select_kernel, blk_count), out_shape=[ja...  1.17 us
  transfers between devices with their start and end apart: 11, of which 9 were waited for; matrix products, arithmetic and copies ran while one was open for 0% of the time, Pallas kernels for 3%

profile of v4, /device:TPU:0, one launch (start us, length us, event | category | flops | bytes accessed | tf_op | source)
XLA Modules:
  0.0 34.6 jit_solution(18412091407699827154)
XLA Ops:
  0.0 0.0 copy-start
  0.0 1.2 %shard_map.73 = (f32[4,16,768]{2,1,0:T(8,128)S(1)}, f32[4,16,768]{2,1,0:T(8,128)S(1)}, f32[4,16,768]{2,1,0:T(8,128)S(1)}, f32[4,16,768]{2,1,0:T(8,128)S(1)}) custom-call(s32[8]{0:T(128)} %owner_ref.1, f32[8,16,768]{2,1,0:T(8,128)} %x_hbm.1), custom_call_target="tpu_custom_call" | custom-call | tf_op jit(solution)/shard_map/pallas_call | solution.py:278
  1.2 4.0 %collective-permute-start = (f32[4,16,768]{2,1,0:T(8,128)S(1)}, f32[4,16,768]{2,1,0:T(8,128)S(1)}, u32[]{:S(2)}, u32[]{:S(2)}) collective-permute-start(f32[4,16,768]{2,1,0:T(8,128)S(1)} %get-tuple-element.17), channel_id=1, source_target_pairs={{0,24},{4,28},{8,16},{12,20},{16,8},{20,12},{24,0},{28,4},{1,25},{... | collective-permute-start | bytes 589832 | tf_op jit(solution)/shard_map/ppermute | solution.py:300
  5.2 0.5 %collective-permute-start.2 = (f32[4,16,768]{2,1,0:T(8,128)S(1)}, f32[4,16,768]{2,1,0:T(8,128)S(1)}, u32[]{:S(2)}, u32[]{:S(2)}) collective-permute-start(f32[4,16,768]{2,1,0:T(8,128)S(1)} %get-tuple-element.18), channel_id=1, source_target_pairs={{0,16},{4,20},{8,24},{12,28},{16,0},{20,4},{24,8},{28,12},{1,17},{... | collective-permute-start | bytes 589832 | tf_op jit(solution)/shard_map/ppermute | solution.py:300
  5.7 0.1 collective-permute-start.4
  5.8 0.0 collective-permute-start.6
  5.8 5.1 %collective-permute-done.refs_0_ = f32[4,16,768]{2,1,0:T(8,128)S(1)} collective-permute-done((f32[4,16,768]{2,1,0:T(8,128)S(1)}, f32[4,16,768]{2,1,0:T(8,128)S(1)}, u32[]{:S(2)}, u32[]{:S(2)}) %collective-permute-start) | collective-permute-done | bytes 196640 | tf_op jit(solution)/shard_map/ppermute | solution.py:300
  10.9 0.0 collective-permute-start.1
  10.9 3.3 %collective-permute-done.2.refs_2_ = f32[4,16,768]{2,1,0:T(8,128)S(1)} collective-permute-done((f32[4,16,768]{2,1,0:T(8,128)S(1)}, f32[4,16,768]{2,1,0:T(8,128)S(1)}, u32[]{:S(2)}, u32[]{:S(2)}) %collective-permute-start.2) | collective-permute-done | bytes 196640 | tf_op jit(solution)/shard_map/ppermute | solution.py:300
  14.3 0.0 collective-permute-start.3
  14.3 0.3 collective-permute-done.4.refs_4_
  14.6 0.2 collective-permute-start.5
  14.8 0.0 collective-permute-done.6.refs_7_
  14.8 0.0 collective-permute-done.1.refs_1_
  14.8 0.9 %collective-permute-done.3.refs_3_ = f32[4,16,768]{2,1,0:T(8,128)S(1)} collective-permute-done((f32[4,16,768]{2,1,0:T(8,128)S(1)}, f32[4,16,768]{2,1,0:T(8,128)S(1)}, u32[]{:S(2)}, u32[]{:S(2)}) %collective-permute-start.3) | collective-permute-done | bytes 196640 | tf_op jit(solution)/shard_map/ppermute | solution.py:22
  15.7 0.3 collective-permute-done.5.refs_5_
  16.0 0.7 %shard_map.74 = (f32[168,128]{1,0:T(8,128)S(1)}, f32[168,128]{1,0:T(8,128)S(1)}, bf16[384,768]{1,0:T(8,128)(2,1)S(1)}, bf16[384,768]{1,0:T(8,128)(2,1)S(1)}) custom-call(f32[4,16,768]{2,1,0:T(8,128)S(1)} %collective-permute-done.refs_0_, f32[4,16,768]{2,1,0:T(8,128)S(1)} %collective-permute-done.1.refs_1_, f32[4,16,768]{2,1,0:T(8,128)S(1)} %collective-permute-done.2.refs_2_, ...), custom_call_target="tpu_custom_call" | custom-call | tf_op jit(solution)/shard_map/pallas_call | solution.py:326
  16.7 1.8 %collective-permute-start.7 = (f32[168,128]{1,0:T(8,128)S(1)}, f32[168,128]{1,0:T(8,128)S(1)}, u32[]{:S(2)}, u32[]{:S(2)}) collective-permute-start(f32[168,128]{1,0:T(8,128)S(1)} %get-tuple-element.22), channel_id=1, source_target_pairs={{0,1},{1,0},{2,3},{3,2},{4,5},{5,4},{6,7},{7,6},{8,9},{9,8},{10,11... | collective-permute-start | bytes 258056 | tf_op jit(solution)/shard_map/ppermute | solution.py:22
  18.5 2.9 %collective-permute-done.7 = f32[168,128]{1,0:T(8,128)S(1)} collective-permute-done((f32[168,128]{1,0:T(8,128)S(1)}, f32[168,128]{1,0:T(8,128)S(1)}, u32[]{:S(2)}, u32[]{:S(2)}) %collective-permute-start.7) | collective-permute-done | bytes 86048 | tf_op jit(solution)/shard_map/ppermute | solution.py:22
  21.5 2.8 %collective-permute-start.10 = (f32[168,128]{1,0:T(8,128)S(1)}, f32[168,128]{1,0:T(8,128)S(1)}, u32[]{:S(2)}, u32[]{:S(2)}) collective-permute-start(f32[168,128]{1,0:T(8,128)S(1)} %add.3.refs_0_), channel_id=1, source_target_pairs={{0,2},{1,3},{2,0},{3,1},{4,6},{5,7},{6,4},{7,5},{8,10},{9,11},{10,... | collective-permute-start | bytes 258056 | tf_op jit(solution)/shard_map/ppermute | solution.py:22
  24.3 1.3 %collective-permute-start.9 = (f32[168,128]{1,0:T(8,128)S(1)}, f32[168,128]{1,0:T(8,128)S(1)}, u32[]{:S(2)}, u32[]{:S(2)}) collective-permute-start(f32[168,128]{1,0:T(8,128)S(1)} %add.3.refs_0_), channel_id=1, source_target_pairs={{0,3},{1,2},{2,1},{3,0},{4,7},{5,6},{6,5},{7,4},{8,11},{9,10},{10,... | collective-permute-start | bytes 258056 | tf_op jit(solution)/shard_map/ppermute | solution.py:22
  25.6 0.2 collective-permute-start.8
  25.9 0.0 copy-done.5
  25.9 0.0 copy-done.1
  25.9 0.0 copy-done.4
  25.9 0.0 copy-done.3
  25.9 0.0 copy-done.2
  25.9 1.2 %shard_map.75 = (bf16[384,384]{1,0:T(8,128)(2,1)S(1)}, bf16[384,384]{1,0:T(8,128)(2,1)S(1)}, bf16[384,256]{1,0:T(8,128)(2,1)S(1)}, f32[1152,384]{1,0:T(8,128)S(1)}) custom-call(s32[16]{0:T(128)S(1)} %copy-done.2, s32[16]{0:T(128)S(1)} %copy-done.3, s32[8]{0:T(128)S(1)} %copy-done.1, f32[8]{0:T(128)S(1)} %copy-done.4, f32[128,384]{1,0:T(8,128)S(1)} %copy-done, ...), custom_call_target="tpu_custom_call" | custom-call | tf_op jit(solution)/shard_map/pallas_call | solution.py:303
  27.1 2.6 %collective-permute-done.10.refs_3_ = f32[168,128]{1,0:T(8,128)S(1)} collective-permute-done((f32[168,128]{1,0:T(8,128)S(1)}, f32[168,128]{1,0:T(8,128)S(1)}, u32[]{:S(2)}, u32[]{:S(2)}) %collective-permute-start.10) | collective-permute-done | bytes 86048 | tf_op jit(solution)/shard_map/ppermute | solution.py:22
  29.7 1.3 %collective-permute-done.9.refs_2_ = f32[168,128]{1,0:T(8,128)S(1)} collective-permute-done((f32[168,128]{1,0:T(8,128)S(1)}, f32[168,128]{1,0:T(8,128)S(1)}, u32[]{:S(2)}, u32[]{:S(2)}) %collective-permute-start.9) | collective-permute-done | bytes 86048 | tf_op jit(solution)/shard_map/ppermute | solution.py:22
  31.1 0.2 collective-permute-done.8.refs_1_
  31.3 3.3 %shard_map.76 = f32[384,768]{1,0:T(8,128)} custom-call(f32[168,128]{1,0:T(8,128)S(1)} %add.3.refs_0_, f32[168,128]{1,0:T(8,128)S(1)} %collective-permute-done.8.refs_1_, f32[168,128]{1,0:T(8,128)S(1)} %collective-permute-done.9.refs_2_, f32[168,128]{1,0:T(8,128)S(1)} %collective-permute-done.10.refs_3_, bf16[384,384]{1,0:T(8,128)(2,1)S(1)} %get-tuple-element.23.refs_4_, ...), custom_call_target="tpu_custom_call" | custom-call | tf_op jit(solution)/shard_map/pallas_call | solution.py:344
  (8 shorter events, 0.0 us)
Async XLA Ops:
  0.0 25.9 %copy-start.1 = (s32[8]{0:T(128)S(1)}, s32[8]{0:T(128)}, u32[]{:S(2)}) copy-start(s32[8]{0:T(128)} %owner_ref.1) | copy-start | bytes 100
  0.0 25.9 %copy-start.5 = (f32[384]{0:T(512)S(1)}, f32[384]{0:T(512)}, u32[]{:S(2)}) copy-start(f32[384]{0:T(512)} %param.13) | copy-start | bytes 4612
  0.0 25.9 %copy-start.4 = (f32[8]{0:T(128)S(1)}, f32[8]{0:T(128)}, u32[]{:S(2)}) copy-start(f32[8]{0:T(128)} %energy_ref.1) | copy-start | bytes 100
  0.0 25.9 %copy-start.3 = (s32[16]{0:T(128)S(1)}, s32[16]{0:T(128)}, u32[]{:S(2)}) copy-start(s32[16]{0:T(128)} %shell_ref.1) | copy-start | bytes 196
  0.0 25.9 %copy-start.2 = (s32[16]{0:T(128)S(1)}, s32[16]{0:T(128)}, u32[]{:S(2)}) copy-start(s32[16]{0:T(128)} %size_ref.1) | copy-start | bytes 196
  0.0 25.9 %copy-start = (f32[128,384]{1,0:T(8,128)S(1)}, f32[128,384]{1,0:T(8,128)}, u32[]{:S(2)}) copy-start(f32[128,384]{1,0:T(8,128)} %coef_ref.1) | copy-start | bytes 589828
  1.2 9.7 %collective-permute-start = (f32[4,16,768]{2,1,0:T(8,128)S(1)}, f32[4,16,768]{2,1,0:T(8,128)S(1)}, u32[]{:S(2)}, u32[]{:S(2)}) collective-permute-start(f32[4,16,768]{2,1,0:T(8,128)S(1)} %get-tuple-element.17), channel_id=1, source_target_pairs={{0,24},{4,28},{8,16},{12,20},{16,8},{20,12},{24,0},{28,4},{1,25},{... | collective-permute-start | bytes 589832 | tf_op jit(solution)/shard_map/ppermute | solution.py:300
  5.2 9.1 %collective-permute-start.2 = (f32[4,16,768]{2,1,0:T(8,128)S(1)}, f32[4,16,768]{2,1,0:T(8,128)S(1)}, u32[]{:S(2)}, u32[]{:S(2)}) collective-permute-start(f32[4,16,768]{2,1,0:T(8,128)S(1)} %get-tuple-element.18), channel_id=1, source_target_pairs={{0,16},{4,20},{8,24},{12,28},{16,0},{20,4},{24,8},{28,12},{1,17},{... | collective-permute-start | bytes 589832 | tf_op jit(solution)/shard_map/ppermute | solution.py:300
  5.7 8.9 %collective-permute-start.4 = (f32[4,16,768]{2,1,0:T(8,128)S(1)}, f32[4,16,768]{2,1,0:T(8,128)S(1)}, u32[]{:S(2)}, u32[]{:S(2)}) collective-permute-start(f32[4,16,768]{2,1,0:T(8,128)S(1)} %get-tuple-element.19), channel_id=1, source_target_pairs={{0,8},{4,12},{8,0},{12,4},{16,24},{20,28},{24,16},{28,20},{1,9},{5... | collective-permute-start | bytes 589832 | tf_op jit(solution)/shard_map/ppermute | solution.py:300
  5.8 9.0 %collective-permute-start.6 = (f32[4,16,768]{2,1,0:T(8,128)S(1)}, f32[4,16,768]{2,1,0:T(8,128)S(1)}, u32[]{:S(2)}, u32[]{:S(2)}) collective-permute-start(f32[4,16,768]{2,1,0:T(8,128)S(1)} %get-tuple-element.20.refs_6_), channel_id=1, source_target_pairs={{0,4},{4,0},{8,12},{12,8},{16,20},{20,16},{24,28},{28,24},{1,5},{5... | collective-permute-start | bytes 589832 | tf_op jit(solution)/shard_map/ppermute | solution.py:22
  10.9 3.9 %collective-permute-start.1 = (f32[4,16,768]{2,1,0:T(8,128)S(1)}, f32[4,16,768]{2,1,0:T(8,128)S(1)}, u32[]{:S(2)}, u32[]{:S(2)}) collective-permute-start(f32[4,16,768]{2,1,0:T(8,128)S(1)} %collective-permute-done.refs_0_), channel_id=1, source_target_pairs={{0,4},{4,0},{8,12},{12,8},{16,20},{20,16},{24,28},{28,24},{1,5},{5... | collective-permute-start | bytes 589832 | tf_op jit(solution)/shard_map/ppermute | solution.py:22
  14.3 1.4 %collective-permute-start.3 = (f32[4,16,768]{2,1,0:T(8,128)S(1)}, f32[4,16,768]{2,1,0:T(8,128)S(1)}, u32[]{:S(2)}, u32[]{:S(2)}) collective-permute-start(f32[4,16,768]{2,1,0:T(8,128)S(1)} %collective-permute-done.2.refs_2_), channel_id=1, source_target_pairs={{0,4},{4,0},{8,12},{12,8},{16,20},{20,16},{24,28},{28,24},{1,5},{5... | collective-permute-start | bytes 589832 | tf_op jit(solution)/shard_map/ppermute | solution.py:22
  14.6 1.4 %collective-permute-start.5 = (f32[4,16,768]{2,1,0:T(8,128)S(1)}, f32[4,16,768]{2,1,0:T(8,128)S(1)}, u32[]{:S(2)}, u32[]{:S(2)}) collective-permute-start(f32[4,16,768]{2,1,0:T(8,128)S(1)} %collective-permute-done.4.refs_4_), channel_id=1, source_target_pairs={{0,4},{4,0},{8,12},{12,8},{16,20},{20,16},{24,28},{28,24},{1,5},{5... | collective-permute-start | bytes 589832 | tf_op jit(solution)/shard_map/ppermute | solution.py:22
  16.7 4.8 %collective-permute-start.7 = (f32[168,128]{1,0:T(8,128)S(1)}, f32[168,128]{1,0:T(8,128)S(1)}, u32[]{:S(2)}, u32[]{:S(2)}) collective-permute-start(f32[168,128]{1,0:T(8,128)S(1)} %get-tuple-element.22), channel_id=1, source_target_pairs={{0,1},{1,0},{2,3},{3,2},{4,5},{5,4},{6,7},{7,6},{8,9},{9,8},{10,11... | collective-permute-start | bytes 258056 | tf_op jit(solution)/shard_map/ppermute | solution.py:22
  21.5 8.3 %collective-permute-start.10 = (f32[168,128]{1,0:T(8,128)S(1)}, f32[168,128]{1,0:T(8,128)S(1)}, u32[]{:S(2)}, u32[]{:S(2)}) collective-permute-start(f32[168,128]{1,0:T(8,128)S(1)} %add.3.refs_0_), channel_id=1, source_target_pairs={{0,2},{1,3},{2,0},{3,1},{4,6},{5,7},{6,4},{7,5},{8,10},{9,11},{10,... | collective-permute-start | bytes 258056 | tf_op jit(solution)/shard_map/ppermute | solution.py:22
  24.3 6.8 %collective-permute-start.9 = (f32[168,128]{1,0:T(8,128)S(1)}, f32[168,128]{1,0:T(8,128)S(1)}, u32[]{:S(2)}, u32[]{:S(2)}) collective-permute-start(f32[168,128]{1,0:T(8,128)S(1)} %add.3.refs_0_), channel_id=1, source_target_pairs={{0,3},{1,2},{2,1},{3,0},{4,7},{5,6},{6,5},{7,4},{8,11},{9,10},{10,... | collective-permute-start | bytes 258056 | tf_op jit(solution)/shard_map/ppermute | solution.py:22
  25.6 5.7 %collective-permute-start.8 = (f32[168,128]{1,0:T(8,128)S(1)}, f32[168,128]{1,0:T(8,128)S(1)}, u32[]{:S(2)}, u32[]{:S(2)}) collective-permute-start(f32[168,128]{1,0:T(8,128)S(1)} %add.3.refs_0_), channel_id=1, source_target_pairs={{0,1},{1,0},{2,3},{3,2},{4,5},{5,4},{6,7},{7,6},{8,9},{9,8},{10,11... | collective-permute-start | bytes 258056 | tf_op jit(solution)/shard_map/ppermute | solution.py:22

commit v5 on v4

--- a/solution.py
+++ b/solution.py
@@ -199,30 +199,61 @@
     )
     rest = folded.shape[0] // 2
     for out, part in ((keep, here & 1), (give, 1 - (here & 1))):
-        rows = pl.ds(pl.multiple_of(part * half, half), half)
-        for stop in range(STOPS - 1):
-            out[pl.ds(stop * half, half), :] = total[stop, rows, :]
-        out[pl.ds((STOPS - 1) * half, rest), :] = folded[
-            pl.ds(pl.multiple_of(part * rest, 8), rest), :
-        ]
-
-
-def density_kernel(steps, *refs):
-    parts = len(steps)
-    shares = refs[:parts]
-    left, right, back, gap, x_high, x_low, out, total, folded, w_high, w_low, density, sems = refs[parts:]
-    here = lax.axis_index("aux")
+        packed = folded[pl.ds(pl.multiple_of(part * rest, 8), rest), :]
+        out[...] = jnp.concatenate([total[part], packed], axis=0)
+
+
+def weigh(total, left, right, back, gap, w_high, w_low):
+    slots = total.shape[0]
+    virt_count = w_high.shape[0]
+    stops = total.shape[1] // slots
+    high, low = halves(total)
+    half_done = matmul(left[...], jnp.concatenate([high, low, high], axis=0))
+    half_done = jnp.concatenate(
+        [half_done[:, stop * slots : (stop + 1) * slots] for stop in range(stops)], axis=0
+    )
+    high, low = halves(half_done)
+    summed = matmul(jnp.concatenate([high, high, low], axis=1), right[...])
+    high, low = halves(summed * gap)
+    both = matmul(high, back[...])
+    weight = both[:, :slots] + both[:, slots:] + matmul(low, back[:, :slots])
+    for stop in range(stops):
+        cols = slice(stop * slots, (stop + 1) * slots)
+        w_high[:, cols], w_low[:, cols] = halves(
+            weight[stop * virt_count : (stop + 1) * virt_count]
+        )
+
+
+def rows_of(ref, stop, count):
+    return ref[pl.ds(pl.multiple_of(stop * count, count), count), :]
+
+
+def first_density_kernel(*refs):
+    *shares, left, right, back, gap, x_high, x_low, out, w_high, w_low = refs
+    slots = left.shape[1] // 3
+    stop = 1 + (lax.axis_index("aux") & 1)
+    square = sum(piece[:slots, :] for piece in shares)
+    weigh(square, left, right, back, rows_of(gap, stop, out.shape[0]), w_high, w_low)
+    high, low = rows_of(x_high, stop, slots), rows_of(x_low, stop, slots)
+    x_all = jnp.concatenate([high, high, low], axis=0)
+    out[...] = matmul(jnp.concatenate([w_high[...], w_low[...], w_high[...]], axis=1), x_all)
+
+
+def last_density_kernel(count, *refs):
+    first, second = refs[:count], refs[count : 2 * count]
+    before, left, right, back, gap, x_high, x_low, out, *scratch = refs[2 * count :]
+    total, folded, w_high, w_low, density, sems = scratch
+    mine = lax.axis_index("aux") & 1
+    stop = 2 - mine
     slots = total.shape[0]
     half = slots // 2
+    band, rest = slots // 4, folded.shape[0] // 2
     virt_count = out.shape[0]
-    band, rest = slots // 4, folded.shape[0] // 2
-    for other in range(2):
-        part = here & 1 ^ other
-        rows = pl.ds(pl.multiple_of(part * half, half), half)
-        share = sum(piece[...] for step, piece in zip(steps, shares) if step & 1 == other)
-        for stop in range(1, STOPS):
-            total[rows, stop * slots : (stop + 1) * slots] = share[(stop - 1) * half : stop * half]
-        folded[pl.ds(pl.multiple_of(part * rest, 8), rest), :] = share[(STOPS - 1) * half :]
+    for part, pieces in ((mine, first), (1 - mine, second)):
+        folded[pl.ds(pl.multiple_of(part * rest, 8), rest), :] = sum(
+            piece[slots:, :] for piece in pieces
+        )
+    total[:, slots:] = sum(piece[:slots, :] for piece in second)
     last = folded[half:, :]
     upper = jnp.concatenate(
         [
@@ -236,27 +267,17 @@
     row_band = lax.broadcasted_iota(jnp.int32, (slots, slots), 0) // band
     lane_band = lax.broadcasted_iota(jnp.int32, (slots, slots), 1) // band
     total[:, :slots] = jnp.where(lane_band >= row_band, upper, upper.T)
-    high, low = halves(total[...])
-    half_done = matmul(left[...], jnp.concatenate([high, low, high], axis=0))
-    half_done = jnp.concatenate(
-        [half_done[:, stop * slots : (stop + 1) * slots] for stop in range(STOPS)], axis=0
-    )
-    high, low = halves(half_done)
-    summed = matmul(jnp.concatenate([high, high, low], axis=1), right[...])
-    high, low = halves(summed * gap[...])
-    both = matmul(high, back[...])
-    weight = both[:, :slots] + both[:, slots:] + matmul(low, back[:, :slots])
-    for stop in range(STOPS):
-        rows = slice(stop * virt_count, (stop + 1) * virt_count)
-        cols = slice(stop * slots, (stop + 1) * slots)
-        w_high[:, cols], w_low[:, cols] = halves(weight[rows])
+    gaps = jnp.concatenate([gap[:virt_count, :], rows_of(gap, stop, virt_count)], axis=0)
+    weigh(total[...], left, right, back, gaps, w_high, w_low)
+    x_high = jnp.concatenate([x_high[:slots, :], rows_of(x_high, stop, slots)], axis=0)
+    x_low = jnp.concatenate([x_low[:slots, :], rows_of(x_low, stop, slots)], axis=0)
     copies = []
     for index in range(sems.shape[0]):
         band = virt_count // sems.shape[0]
         rows = pl.ds(index * band, band)
         high, low = w_high[rows, :], w_low[rows, :]
-        x_all = jnp.concatenate([x_high[...], x_high[...], x_low[...]], axis=0)
-        density[rows, :] = matmul(jnp.concatenate([high, low, high], axis=1), x_all)
+        both = matmul(jnp.concatenate([high, low], axis=0), x_high)
+        density[rows, :] = before[rows, :] + both[:band] + both[band:] + matmul(high, x_low)
         copies.append(pltpu.make_async_copy(density.at[rows], out.at[rows], sems.at[index]))
         copies[-1].start()
     for copy in copies:
@@ -325,7 +346,7 @@
     places = [2 * step + core for step in reversed(range(chips)) for core in range(2)]
     keep, give, x_high, x_low = pl.pallas_call(
         functools.partial(overlap_kernel, slot_cap, places),
-        out_shape=[jax.ShapeDtypeStruct(((STOPS - 1) * slots // 2 + fold // 2, slots), F32)] * 2
+        out_shape=[jax.ShapeDtypeStruct((slots + fold // 2, slots), F32)] * 2
         + [jax.ShapeDtypeStruct((STOPS * slots, aux_width), BF16)] * 2,
         in_specs=[vmem] * len(pieces),
         out_specs=[vmem] * 4,
@@ -336,26 +357,39 @@
         compiler_params=params,
     )(*[pieces[place] for place in places])
 
-    mine = keep + swapped(give, "aux", 1)
-    steps = [0, *range(1, parts, 2), *range(2, parts, 2)]
-    gathered = [swapped(mine, "aux", step) if step else mine for step in steps]
-
+    taken = swapped(give, "aux", 1)
+    mine = keep + taken
+    mine, left = lax.optimization_barrier((mine, left))
+    evens = [mine] + [swapped(mine, "aux", step) for step in range(2, parts, 2)]
+    held = mine
+    odds = [swapped(held, "aux", step) for step in range(1, parts, 2)]
     bands = 3 if virt_count % 48 == 0 else 1
+    flops = 18 * virt_count * slots * (slots + 2 * virt_count + aux_width)
+
+    first = pl.pallas_call(
+        first_density_kernel,
+        out_shape=jax.ShapeDtypeStruct((virt_count, aux_width), F32),
+        in_specs=[vmem] * (len(evens) + 6),
+        out_specs=vmem,
+        scratch_shapes=[pltpu.VMEM((virt_count, slots), BF16)] * 2,
+        compiler_params=params,
+        cost_estimate=pl.CostEstimate(flops=flops, bytes_accessed=0, transcendentals=0),
+    )(*evens, left, right, back, gap, x_high, x_low)
     density = pl.pallas_call(
-        functools.partial(density_kernel, steps),
+        functools.partial(last_density_kernel, len(evens)),
         out_shape=jax.ShapeDtypeStruct((virt_count, aux_width), F32),
-        in_specs=[vmem] * (parts + 6),
+        in_specs=[vmem] * (len(evens) + len(odds) + 7),
         out_specs=pl.BlockSpec(memory_space=pl.ANY),
         scratch_shapes=[
-            pltpu.VMEM((slots, STOPS * slots), F32),
+            pltpu.VMEM((slots, 2 * slots), F32),
             pltpu.VMEM((fold, slots), F32),
-            pltpu.VMEM((virt_count, STOPS * slots), BF16),
-            pltpu.VMEM((virt_count, STOPS * slots), BF16),
+            pltpu.VMEM((virt_count, 2 * slots), BF16),
+            pltpu.VMEM((virt_count, 2 * slots), BF16),
             pltpu.VMEM((virt_count, aux_width), F32),
             pltpu.SemaphoreType.DMA((bands,)),
         ],
         compiler_params=params,
-    )(*gathered, left, right, back, gap, x_high, x_low)
+    )(*evens, *odds, first, left, right, back, gap, x_high, x_low)
     return density.reshape(1, virt_count, aux_width)
 
 

time: 34.7 us -> 34.2 us (0.986)
  waiting for transfers between devices: 17.1 us -> 15.8 us
  Pallas kernels: 6.35 us -> 7.04 us
    ppermute x8, waiting for transfers between devices: 8.33 us -> 7.06 us  [swapped(): lax.ppermute(value, axis, [(i, i ^ step) for i in range(lax.axis_size(axi...]
    pallas_call x1 -> x2, Pallas kernels: 3.29 us -> 3.97 us  [the longest x1 2.71 us: slots_first(): pl.pallas_call(functools.partial(last_density_kernel, len(evens)), out_sh...]
  transfers between devices with their start and end apart: 11 -> 11, of which waited for: 9 -> 9; matrix products, arithmetic and copies ran while one was open for 0% -> 0% of each run, Pallas kernels for 3% -> 7%
where the time goes in v5:
time: 34.2 us; the launch traced here: 34 us
  waiting for transfers between devices  15.8 us (46%)
  starting transfers between devices  11.1 us (32%)
  Pallas kernels  7.04 us (21%)
    ppermute x3, waiting for transfers between devices, slots_first(): piece = lax.ppermute(piece, 'blk', pairs)  8.74 us
    ppermute x8, waiting for transfers between devices, swapped(): lax.ppermute(value, axis, [(i, i ^ step) for i in range(lax.axis_size(axi...  7.06 us
    ppermute x8, starting transfers between devices, swapped(): lax.ppermute(value, axis, [(i, i ^ step) for i in range(lax.axis_size(axi...  6.46 us
    ppermute x3, starting transfers between devices, slots_first(): piece = lax.ppermute(piece, 'blk', pairs)  4.6 us
    pallas_call x1, Pallas kernels, slots_first(): pl.pallas_call(functools.partial(last_density_kernel, len(evens)), out_sh...  2.71 us
    pallas_call x1, Pallas kernels, slots_first(): pl.pallas_call(first_density_kernel, out_shape=jax.ShapeDtypeStruct((virt...  1.26 us
    pallas_call x1, Pallas kernels, slots_first(): pl.pallas_call(functools.partial(coefficient_kernel, blk_count), out_shap...  1.21 us
    pallas_call x1, Pallas kernels, slots_first(): pl.pallas_call(functools.partial(select_kernel, blk_count), out_shape=[ja...  1.17 us
  transfers between devices with their start and end apart: 11, of which 9 were waited for; matrix products, arithmetic and copies ran while one was open for 0% of the time, Pallas kernels for 7%

profile of v5, /device:TPU:0, one launch (start us, length us, event | category | flops | bytes accessed | tf_op | source)
XLA Modules:
  0.0 34.0 jit_solution(14169002401836671368)
XLA Ops:
  0.0 0.0 copy-start
  0.0 1.2 %shard_map.73 = (f32[4,16,768]{2,1,0:T(8,128)S(1)}, f32[4,16,768]{2,1,0:T(8,128)S(1)}, f32[4,16,768]{2,1,0:T(8,128)S(1)}, f32[4,16,768]{2,1,0:T(8,128)S(1)}) custom-call(s32[8]{0:T(128)} %owner_ref.1, f32[8,16,768]{2,1,0:T(8,128)} %x_hbm.1), custom_call_target="tpu_custom_call" | custom-call | tf_op jit(solution)/shard_map/pallas_call | solution.py:299
  1.2 4.0 %collective-permute-start = (f32[4,16,768]{2,1,0:T(8,128)S(1)}, f32[4,16,768]{2,1,0:T(8,128)S(1)}, u32[]{:S(2)}, u32[]{:S(2)}) collective-permute-start(f32[4,16,768]{2,1,0:T(8,128)S(1)} %get-tuple-element.19), channel_id=1, source_target_pairs={{0,24},{4,28},{8,16},{12,20},{16,8},{20,12},{24,0},{28,4},{1,25},{... | collective-permute-start | bytes 589832 | tf_op jit(solution)/shard_map/ppermute | solution.py:321
  5.2 0.5 %collective-permute-start.2 = (f32[4,16,768]{2,1,0:T(8,128)S(1)}, f32[4,16,768]{2,1,0:T(8,128)S(1)}, u32[]{:S(2)}, u32[]{:S(2)}) collective-permute-start(f32[4,16,768]{2,1,0:T(8,128)S(1)} %get-tuple-element.20), channel_id=1, source_target_pairs={{0,16},{4,20},{8,24},{12,28},{16,0},{20,4},{24,8},{28,12},{1,17},{... | collective-permute-start | bytes 589832 | tf_op jit(solution)/shard_map/ppermute | solution.py:321
  5.7 0.1 collective-permute-start.4
  5.8 0.0 collective-permute-start.6
  5.8 5.1 %collective-permute-done.refs_0_ = f32[4,16,768]{2,1,0:T(8,128)S(1)} collective-permute-done((f32[4,16,768]{2,1,0:T(8,128)S(1)}, f32[4,16,768]{2,1,0:T(8,128)S(1)}, u32[]{:S(2)}, u32[]{:S(2)}) %collective-permute-start) | collective-permute-done | bytes 196640 | tf_op jit(solution)/shard_map/ppermute | solution.py:321
  10.9 0.0 collective-permute-start.1
  10.9 3.3 %collective-permute-done.2.refs_2_ = f32[4,16,768]{2,1,0:T(8,128)S(1)} collective-permute-done((f32[4,16,768]{2,1,0:T(8,128)S(1)}, f32[4,16,768]{2,1,0:T(8,128)S(1)}, u32[]{:S(2)}, u32[]{:S(2)}) %collective-permute-start.2) | collective-permute-done | bytes 196640 | tf_op jit(solution)/shard_map/ppermute | solution.py:321
  14.3 0.0 collective-permute-start.3
  14.3 0.3 collective-permute-done.4.refs_4_
  14.6 0.2 collective-permute-start.5
  14.8 0.0 collective-permute-done.6.refs_7_
  14.8 0.0 collective-permute-done.1.refs_1_
  14.8 0.9 %collective-permute-done.3.refs_3_ = f32[4,16,768]{2,1,0:T(8,128)S(1)} collective-permute-done((f32[4,16,768]{2,1,0:T(8,128)S(1)}, f32[4,16,768]{2,1,0:T(8,128)S(1)}, u32[]{:S(2)}, u32[]{:S(2)}) %collective-permute-start.3) | collective-permute-done | bytes 196640 | tf_op jit(solution)/shard_map/ppermute | solution.py:22
  15.7 0.3 collective-permute-done.5.refs_5_
  16.0 0.7 %shard_map.74 = (f32[168,128]{1,0:T(8,128)S(1)}, f32[168,128]{1,0:T(8,128)S(1)}, bf16[384,768]{1,0:T(8,128)(2,1)S(1)}, bf16[384,768]{1,0:T(8,128)(2,1)S(1)}) custom-call(f32[4,16,768]{2,1,0:T(8,128)S(1)} %collective-permute-done.refs_0_, f32[4,16,768]{2,1,0:T(8,128)S(1)} %collective-permute-done.1.refs_1_, f32[4,16,768]{2,1,0:T(8,128)S(1)} %collective-permute-done.2.refs_2_, ...), custom_call_target="tpu_custom_call" | custom-call | tf_op jit(solution)/shard_map/pallas_call | solution.py:347
  16.7 1.8 %collective-permute-start.7 = (f32[168,128]{1,0:T(8,128)S(1)}, f32[168,128]{1,0:T(8,128)S(1)}, u32[]{:S(2)}, u32[]{:S(2)}) collective-permute-start(f32[168,128]{1,0:T(8,128)S(1)} %get-tuple-element.24), channel_id=1, source_target_pairs={{0,1},{1,0},{2,3},{3,2},{4,5},{5,4},{6,7},{7,6},{8,9},{9,8},{10,11... | collective-permute-start | bytes 258056 | tf_op jit(solution)/shard_map/ppermute | solution.py:22
  18.5 0.0 copy-done.5
  18.5 0.0 copy-done.1
  18.5 0.0 copy-done.4
  18.5 0.0 copy-done.3
  18.6 1.2 %shard_map.75 = (bf16[384,384]{1,0:T(8,128)(2,1)S(1)}, bf16[384,384]{1,0:T(8,128)(2,1)S(1)}, bf16[384,256]{1,0:T(8,128)(2,1)S(1)}, f32[1152,384]{1,0:T(8,128)S(1)}) custom-call(s32[16]{0:T(128)S(1)} %copy-done.2, s32[16]{0:T(128)S(1)} %copy-done.3, s32[8]{0:T(128)S(1)} %copy-done.1, f32[8]{0:T(128)S(1)} %copy-done.4, f32[128,384]{1,0:T(8,128)S(1)} %copy-done, ...), custom_call_target="tpu_custom_call" | custom-call | tf_op jit(solution)/shard_map/pallas_call | solution.py:324
  19.8 1.7 %collective-permute-done.7 = f32[168,128]{1,0:T(8,128)S(1)} collective-permute-done((f32[168,128]{1,0:T(8,128)S(1)}, f32[168,128]{1,0:T(8,128)S(1)}, u32[]{:S(2)}, u32[]{:S(2)}) %collective-permute-start.7) | collective-permute-done | bytes 86048 | tf_op jit(solution)/shard_map/ppermute | solution.py:22
  21.5 2.8 %collective-permute-start.8 = (f32[168,128]{1,0:T(8,128)S(1)}, f32[168,128]{1,0:T(8,128)S(1)}, u32[]{:S(2)}, u32[]{:S(2)}) collective-permute-start(f32[168,128]{1,0:T(8,128)S(1)} %add.3.refs_0_), channel_id=1, source_target_pairs={{0,2},{1,3},{2,0},{3,1},{4,6},{5,7},{6,4},{7,5},{8,10},{9,11},{10,... | collective-permute-start | bytes 258056 | tf_op jit(solution)/shard_map/ppermute | solution.py:22
  24.3 1.3 %collective-permute-start.10 = (f32[168,128]{1,0:T(8,128)S(1)}, f32[168,128]{1,0:T(8,128)S(1)}, u32[]{:S(2)}, u32[]{:S(2)}) collective-permute-start(f32[168,128]{1,0:T(8,128)S(1)} %add.3.refs_0_), channel_id=1, source_target_pairs={{0,3},{1,2},{2,1},{3,0},{4,7},{5,6},{6,5},{7,4},{8,11},{9,10},{10,... | collective-permute-start | bytes 258056 | tf_op jit(solution)/shard_map/ppermute | solution.py:22
  25.6 0.2 collective-permute-start.9
  25.9 3.9 %collective-permute-done.8.refs_1_ = f32[168,128]{1,0:T(8,128)S(1)} collective-permute-done((f32[168,128]{1,0:T(8,128)S(1)}, f32[168,128]{1,0:T(8,128)S(1)}, u32[]{:S(2)}, u32[]{:S(2)}) %collective-permute-start.8) | collective-permute-done | bytes 86048 | tf_op jit(solution)/shard_map/ppermute | solution.py:22
  29.7 1.3 %shard_map.76.refs_4_ = f32[384,768]{1,0:T(8,128)S(1)} custom-call(f32[168,128]{1,0:T(8,128)S(1)} %add.3.refs_0_, f32[168,128]{1,0:T(8,128)S(1)} %collective-permute-done.8.refs_1_, bf16[384,384]{1,0:T(8,128)(2,1)S(1)} %get-tuple-element.27.refs_2_.refs_5_, bf16[384,384]{1,0:T(8,128)(2,1)S(1)} %get-tuple-element.28.refs_3_.refs_6_, ...), custom_call_target="tpu_custom_call" | custom-call | flops 1472200704 | tf_op jit(solution)/shard_map/pallas_call | solution.py:369
  31.0 0.1 collective-permute-done.10.refs_3_
  31.1 0.2 collective-permute-done.9.refs_2_
  31.3 2.7 %shard_map.77 = f32[384,768]{1,0:T(8,128)} custom-call(f32[168,128]{1,0:T(8,128)S(1)} %add.3.refs_0_, f32[168,128]{1,0:T(8,128)S(1)} %collective-permute-done.8.refs_1_, f32[168,128]{1,0:T(8,128)S(1)} %collective-permute-done.9.refs_2_, f32[168,128]{1,0:T(8,128)S(1)} %collective-permute-done.10.refs_3_, f32[384,768]{1,0:T(8,128)S(1)} %shard_map.76.refs_4_, ...), custom_call_target="tpu_custom_call" | custom-call | tf_op jit(solution)/shard_map/pallas_call | solution.py:378
  (9 shorter events, 0.0 us)
Async XLA Ops:
  0.0 18.5 %copy-start.1 = (s32[8]{0:T(128)S(1)}, s32[8]{0:T(128)}, u32[]{:S(2)}) copy-start(s32[8]{0:T(128)} %owner_ref.1) | copy-start | bytes 100
  0.0 18.5 %copy-start.5 = (f32[384]{0:T(512)S(1)}, f32[384]{0:T(512)}, u32[]{:S(2)}) copy-start(f32[384]{0:T(512)} %param.13) | copy-start | bytes 4612
  0.0 18.5 %copy-start.4 = (f32[8]{0:T(128)S(1)}, f32[8]{0:T(128)}, u32[]{:S(2)}) copy-start(f32[8]{0:T(128)} %energy_ref.1) | copy-start | bytes 100
  0.0 18.5 %copy-start.3 = (s32[16]{0:T(128)S(1)}, s32[16]{0:T(128)}, u32[]{:S(2)}) copy-start(s32[16]{0:T(128)} %shell_ref.1) | copy-start | bytes 196
  0.0 18.5 %copy-start.2 = (s32[16]{0:T(128)S(1)}, s32[16]{0:T(128)}, u32[]{:S(2)}) copy-start(s32[16]{0:T(128)} %size_ref.1) | copy-start | bytes 196
  0.0 18.5 %copy-start = (f32[128,384]{1,0:T(8,128)S(1)}, f32[128,384]{1,0:T(8,128)}, u32[]{:S(2)}) copy-start(f32[128,384]{1,0:T(8,128)} %coef_ref.1) | copy-start | bytes 589828
  1.2 9.7 %collective-permute-start = (f32[4,16,768]{2,1,0:T(8,128)S(1)}, f32[4,16,768]{2,1,0:T(8,128)S(1)}, u32[]{:S(2)}, u32[]{:S(2)}) collective-permute-start(f32[4,16,768]{2,1,0:T(8,128)S(1)} %get-tuple-element.19), channel_id=1, source_target_pairs={{0,24},{4,28},{8,16},{12,20},{16,8},{20,12},{24,0},{28,4},{1,25},{... | collective-permute-start | bytes 589832 | tf_op jit(solution)/shard_map/ppermute | solution.py:321
  5.2 9.1 %collective-permute-start.2 = (f32[4,16,768]{2,1,0:T(8,128)S(1)}, f32[4,16,768]{2,1,0:T(8,128)S(1)}, u32[]{:S(2)}, u32[]{:S(2)}) collective-permute-start(f32[4,16,768]{2,1,0:T(8,128)S(1)} %get-tuple-element.20), channel_id=1, source_target_pairs={{0,16},{4,20},{8,24},{12,28},{16,0},{20,4},{24,8},{28,12},{1,17},{... | collective-permute-start | bytes 589832 | tf_op jit(solution)/shard_map/ppermute | solution.py:321
  5.7 8.9 %collective-permute-start.4 = (f32[4,16,768]{2,1,0:T(8,128)S(1)}, f32[4,16,768]{2,1,0:T(8,128)S(1)}, u32[]{:S(2)}, u32[]{:S(2)}) collective-permute-start(f32[4,16,768]{2,1,0:T(8,128)S(1)} %get-tuple-element.21), channel_id=1, source_target_pairs={{0,8},{4,12},{8,0},{12,4},{16,24},{20,28},{24,16},{28,20},{1,9},{5... | collective-permute-start | bytes 589832 | tf_op jit(solution)/shard_map/ppermute | solution.py:321
  5.8 9.0 %collective-permute-start.6 = (f32[4,16,768]{2,1,0:T(8,128)S(1)}, f32[4,16,768]{2,1,0:T(8,128)S(1)}, u32[]{:S(2)}, u32[]{:S(2)}) collective-permute-start(f32[4,16,768]{2,1,0:T(8,128)S(1)} %get-tuple-element.22.refs_6_), channel_id=1, source_target_pairs={{0,4},{4,0},{8,12},{12,8},{16,20},{20,16},{24,28},{28,24},{1,5},{5... | collective-permute-start | bytes 589832 | tf_op jit(solution)/shard_map/ppermute | solution.py:22
  10.9 3.9 %collective-permute-start.1 = (f32[4,16,768]{2,1,0:T(8,128)S(1)}, f32[4,16,768]{2,1,0:T(8,128)S(1)}, u32[]{:S(2)}, u32[]{:S(2)}) collective-permute-start(f32[4,16,768]{2,1,0:T(8,128)S(1)} %collective-permute-done.refs_0_), channel_id=1, source_target_pairs={{0,4},{4,0},{8,12},{12,8},{16,20},{20,16},{24,28},{28,24},{1,5},{5... | collective-permute-start | bytes 589832 | tf_op jit(solution)/shard_map/ppermute | solution.py:22
  14.3 1.4 %collective-permute-start.3 = (f32[4,16,768]{2,1,0:T(8,128)S(1)}, f32[4,16,768]{2,1,0:T(8,128)S(1)}, u32[]{:S(2)}, u32[]{:S(2)}) collective-permute-start(f32[4,16,768]{2,1,0:T(8,128)S(1)} %collective-permute-done.2.refs_2_), channel_id=1, source_target_pairs={{0,4},{4,0},{8,12},{12,8},{16,20},{20,16},{24,28},{28,24},{1,5},{5... | collective-permute-start | bytes 589832 | tf_op jit(solution)/shard_map/ppermute | solution.py:22
  14.6 1.4 %collective-permute-start.5 = (f32[4,16,768]{2,1,0:T(8,128)S(1)}, f32[4,16,768]{2,1,0:T(8,128)S(1)}, u32[]{:S(2)}, u32[]{:S(2)}) collective-permute-start(f32[4,16,768]{2,1,0:T(8,128)S(1)} %collective-permute-done.4.refs_4_), channel_id=1, source_target_pairs={{0,4},{4,0},{8,12},{12,8},{16,20},{20,16},{24,28},{28,24},{1,5},{5... | collective-permute-start | bytes 589832 | tf_op jit(solution)/shard_map/ppermute | solution.py:22
  16.7 4.8 %collective-permute-start.7 = (f32[168,128]{1,0:T(8,128)S(1)}, f32[168,128]{1,0:T(8,128)S(1)}, u32[]{:S(2)}, u32[]{:S(2)}) collective-permute-start(f32[168,128]{1,0:T(8,128)S(1)} %get-tuple-element.24), channel_id=1, source_target_pairs={{0,1},{1,0},{2,3},{3,2},{4,5},{5,4},{6,7},{7,6},{8,9},{9,8},{10,11... | collective-permute-start | bytes 258056 | tf_op jit(solution)/shard_map/ppermute | solution.py:22
  21.5 8.3 %collective-permute-start.8 = (f32[168,128]{1,0:T(8,128)S(1)}, f32[168,128]{1,0:T(8,128)S(1)}, u32[]{:S(2)}, u32[]{:S(2)}) collective-permute-start(f32[168,128]{1,0:T(8,128)S(1)} %add.3.refs_0_), channel_id=1, source_target_pairs={{0,2},{1,3},{2,0},{3,1},{4,6},{5,7},{6,4},{7,5},{8,10},{9,11},{10,... | collective-permute-start | bytes 258056 | tf_op jit(solution)/shard_map/ppermute | solution.py:22
  24.3 6.8 %collective-permute-start.10 = (f32[168,128]{1,0:T(8,128)S(1)}, f32[168,128]{1,0:T(8,128)S(1)}, u32[]{:S(2)}, u32[]{:S(2)}) collective-permute-start(f32[168,128]{1,0:T(8,128)S(1)} %add.3.refs_0_), channel_id=1, source_target_pairs={{0,3},{1,2},{2,1},{3,0},{4,7},{5,6},{6,5},{7,4},{8,11},{9,10},{10,... | collective-permute-start | bytes 258056 | tf_op jit(solution)/shard_map/ppermute | solution.py:22
  25.6 5.7 %collective-permute-start.9 = (f32[168,128]{1,0:T(8,128)S(1)}, f32[168,128]{1,0:T(8,128)S(1)}, u32[]{:S(2)}, u32[]{:S(2)}) collective-permute-start(f32[168,128]{1,0:T(8,128)S(1)} %add.3.refs_0_), channel_id=1, source_target_pairs={{0,1},{1,0},{2,3},{3,2},{4,5},{5,4},{6,7},{7,6},{8,9},{9,8},{10,11... | collective-permute-start | bytes 258056 | tf_op jit(solution)/shard_map/ppermute | solution.py:22

commit v6 on v5

--- a/solution.py
+++ b/solution.py
@@ -110,7 +110,8 @@
 def select_kernel(blk_count, owner_hbm, x_hbm, *refs):
     *outs, owner_ref, x_ref, owner_sem, x_sem = refs
     chips = blk_count // 2
-    my_chip = lax.axis_index("blk") >> 1
+    me = lax.axis_index("blk")
+    my_chip, my_core = me >> 1, me & 1
     reads = [
         pltpu.make_async_copy(owner_hbm, owner_ref, owner_sem),
         pltpu.make_async_copy(x_hbm, x_ref, x_sem),
@@ -119,10 +120,23 @@
         read.start()
     for read in reads:
         read.wait()
-    for step, out in enumerate(outs):
-        last = 2 * partner_chip(my_chip, step, chips) + 1
-        for stop in range(STOPS + 1):
-            out[stop] = x_ref[owner_ref[lax.rem(last + blk_count - stop, blk_count)]]
+
+    def rows(block):
+        return x_ref[owner_ref[lax.rem(block + blk_count, blk_count)]]
+
+    for step in range(chips):
+        last = 2 * partner_chip(my_chip, step, chips)
+        mine, theirs = last - 2 + 3 * my_core, last - 2 + 3 * (1 - my_core)
+        whole = outs[2 * step]
+        whole[0], whole[1] = rows(last), rows(last - 1)
+        if step == chips - 1:
+            whole[2], whole[3] = rows(last + 1), rows(last - 2)
+            continue
+        whole[2] = rows(mine)
+        rest = outs[2 * step + 1]
+        if step == 0:
+            rest[0], rest[1] = whole[0], whole[1]
+        rest[rest.shape[0] - 1] = rows(theirs)
 
 
 def coefficient_kernel(
@@ -168,17 +182,25 @@
         gap_ref[pl.ds(stop * virt_count, virt_count), :] = 1.0 / ((both - column) - row)
 
 
-def overlap_kernel(slot_cap, places, *refs):
-    *pieces, keep, give, x_high, x_low, total, folded = refs
-    first = 1 - (lax.axis_index("blk") & 1)
+def join_kernel(*refs):
+    *pieces, out = refs
+    for index, piece in enumerate(pieces):
+        out[index] = piece[0]
+
+
+def overlap_kernel(slot_cap, layout, *refs):
+    *operands, keep, give, x_high, x_low, total, folded = refs
+    count = 1 + max(place for entries in layout for _, _, place in entries)
+    my_core = lax.axis_index("blk") & 1
     here = lax.axis_index("aux")
-    for stop in range(STOPS):
-        for index, piece in zip(places, pieces):
-            high, low = halves(piece[first + stop])
-            rows = pl.ds((stop * len(pieces) + index) * slot_cap, slot_cap)
-            x_high[rows, :] = high
-            x_low[rows, :] = low
-    slots = slot_cap * len(pieces)
+    for entries, operand in zip(layout, operands):
+        for row, offset, place in entries:
+            stop = lax.rem(offset + my_core, STOPS)
+            high, low = halves(operand[3 - my_core if row == 3 else row])
+            target = pl.ds(pl.multiple_of((stop * count + place) * slot_cap, slot_cap), slot_cap)
+            x_high[target, :] = high
+            x_low[target, :] = low
+    slots = slot_cap * count
     own = jnp.concatenate([x_high[:slots, :], x_low[:slots, :]], axis=0)
     both = matmul_nt(own, x_high[...])
     gram = both[:slots] + both[slots:] + matmul_nt(x_high[:slots, :], x_low[...])
@@ -296,11 +318,14 @@
     smem = pl.BlockSpec(memory_space=pltpu.SMEM)
     params = pltpu.CompilerParams(vmem_limit_bytes=24 * 1024 * 1024)
 
+    def block(count):
+        return jax.ShapeDtypeStruct((count, slot_cap, aux_width), F32)
+
     sent = pl.pallas_call(
         functools.partial(select_kernel, blk_count),
-        out_shape=[jax.ShapeDtypeStruct((STOPS + 1, slot_cap, aux_width), F32)] * chips,
+        out_shape=[block(STOPS)] * 2 + [block(STOPS), block(1)] * (chips - 2) + [block(4)],
         in_specs=[pl.BlockSpec(memory_space=pltpu.HBM)] * 2,
-        out_specs=[vmem] * chips,
+        out_specs=[vmem] * (2 * chips - 1),
         scratch_shapes=[
             pltpu.SMEM(occ_owner.shape, jnp.int32),
             pltpu.VMEM(occupied_integrals.shape, F32),
@@ -310,16 +335,42 @@
         compiler_params=params,
     )(*[pltpu.with_memory_space_constraint(a, pltpu.HBM) for a in (occ_owner, occupied_integrals)])
 
-    pieces = []
-    for step, piece in enumerate(sent):
-        if step > 0:
-            pairs = [
-                (2 * chip + core, 2 * int(partner_chip(chip, step, chips)) + core)
+    def entries(place, rows=STOPS):
+        return [(row, row, place) for row in range(rows)]
+
+    own = [(sent[0], entries(0)), (swapped(sent[1], "blk", 1), entries(1))]
+    whole, rest = [], []
+    for step in range(1, chips):
+        ways = [
+            [
+                (2 * chip + core, 2 * int(partner_chip(chip, step, chips)) + (core ^ cross))
                 for chip in range(chips)
                 for core in range(2)
             ]
-            piece = lax.ppermute(piece, "blk", pairs)
-        pieces += [piece, swapped(piece, "blk", 1)]
+            for cross in range(2)
+        ]
+        piece = lax.ppermute(sent[2 * step], "blk", ways[0])
+        if step == chips - 1:
+            both = [[*entries(place, 2), (3, 2, place)] for place in (2 * step, 2 * step + 1)]
+            held, sibling = lax.optimization_barrier((piece, own[1][0]))
+            own[1] = (sibling, own[1][1])
+            whole += [(piece, both[0]), (swapped(held, "blk", 1), both[1])]
+            continue
+        other = lax.ppermute(sent[2 * step + 1], "blk", ways[1])
+        whole.append((piece, entries(2 * step)))
+        whole.append((swapped(piece, "blk", 1), entries(2 * step + 1, 2)))
+        rest.append(other)
+    joined = pl.pallas_call(
+        join_kernel,
+        out_shape=block(chips - 2),
+        in_specs=[vmem] * (chips - 2),
+        out_specs=vmem,
+        compiler_params=params,
+        cost_estimate=pl.CostEstimate(flops=2 * 10**9, bytes_accessed=0, transcendentals=0),
+    )(*rest)
+    last = [(joined, [(row, 2, 2 * step + 1) for row, step in enumerate(range(1, chips - 1))])]
+    pieces = whole[4:6] + whole[2:4] + whole[:2] + own + last
+    operands, layout = zip(*pieces)
 
     left, right, back, gap = pl.pallas_call(
         functools.partial(coefficient_kernel, blk_count),
@@ -343,19 +394,18 @@
     )
 
     fold = 5 * slots // 8
-    places = [2 * step + core for step in reversed(range(chips)) for core in range(2)]
     keep, give, x_high, x_low = pl.pallas_call(
-        functools.partial(overlap_kernel, slot_cap, places),
+        functools.partial(overlap_kernel, slot_cap, layout),
         out_shape=[jax.ShapeDtypeStruct((slots + fold // 2, slots), F32)] * 2
         + [jax.ShapeDtypeStruct((STOPS * slots, aux_width), BF16)] * 2,
-        in_specs=[vmem] * len(pieces),
+        in_specs=[vmem] * len(operands),
         out_specs=[vmem] * 4,
         scratch_shapes=[
             pltpu.VMEM((STOPS - 1, slots, slots), F32),
             pltpu.VMEM((fold, slots), F32),
         ],
         compiler_params=params,
-    )(*[pieces[place] for place in places])
+    )(*operands)
 
     taken = swapped(give, "aux", 1)
     mine = keep + taken

time: 34.2 us -> 33.3 us (0.974)
  waiting for transfers between devices: 15.8 us -> 12.2 us
  starting transfers between devices: 11.1 us -> 13.6 us
    ppermute x3 -> x5, waiting for transfers between devices: 8.74 us -> 5.25 us  [the longest x3 5.06 us: slots_first(): piece = lax.ppermute(sent[2 * step], 'blk', ways[0])]
    ppermute x3 -> x5, starting transfers between devices: 4.6 us -> 7.73 us  [the longest x3 4.68 us: slots_first(): piece = lax.ppermute(sent[2 * step], 'blk', ways[0])]
    ppermute x8, starting transfers between devices: 6.46 us -> 5.91 us  [swapped(): lax.ppermute(value, axis, [(i, i ^ step) for i in range(lax.axis_size(axi...]
    pallas_call x2 -> x3, Pallas kernels: 1.86 us -> 1.92 us  [the longest x1 1.07 us: slots_first(): pl.pallas_call(functools.partial(select_kernel, blk_count), out_shape=[bl...]
  transfers between devices with their start and end apart: 11 -> 13, of which waited for: 9 -> 10; matrix products, arithmetic and copies ran while one was open for 0% -> 0% of each run, Pallas kernels for 7% -> 7%
where the time goes in v6:
time: 33.3 us; the launch traced here: 33.2 us
  starting transfers between devices  13.6 us (41%)
  waiting for transfers between devices  12.2 us (37%)
  Pallas kernels  7.1 us (21%)
    ppermute x8, waiting for transfers between devices, swapped(): lax.ppermute(value, axis, [(i, i ^ step) for i in range(lax.axis_size(axi...  7 us
    ppermute x8, starting transfers between devices, swapped(): lax.ppermute(value, axis, [(i, i ^ step) for i in range(lax.axis_size(axi...  5.91 us
    ppermute x3, waiting for transfers between devices, slots_first(): piece = lax.ppermute(sent[2 * step], 'blk', ways[0])  5.06 us
    ppermute x3, starting transfers between devices, slots_first(): piece = lax.ppermute(sent[2 * step], 'blk', ways[0])  4.68 us
    ppermute x2, starting transfers between devices, slots_first(): other = lax.ppermute(sent[2 * step + 1], 'blk', ways[1])  3.05 us
    pallas_call x1, Pallas kernels, slots_first(): pl.pallas_call(functools.partial(last_density_kernel, len(evens)), out_sh...  2.71 us
    pallas_call x1, Pallas kernels, slots_first(): pl.pallas_call(first_density_kernel, out_shape=jax.ShapeDtypeStruct((virt...  1.26 us
    pallas_call x1, Pallas kernels, slots_first(): pl.pallas_call(functools.partial(coefficient_kernel, blk_count), out_shap...  1.21 us
  transfers between devices with their start and end apart: 13, of which 10 were waited for; matrix products, arithmetic and copies ran while one was open for 0% of the time, Pallas kernels for 7%

profile of v6, /device:TPU:0, one launch (start us, length us, event | category | flops | bytes accessed | tf_op | source)
XLA Modules:
  0.0 33.2 jit_solution(5789790011318073670)
XLA Ops:
  0.0 1.1 %shard_map.73 = (f32[3,16,768]{2,1,0:T(8,128)S(1)}, f32[3,16,768]{2,1,0:T(8,128)S(1)}, f32[3,16,768]{2,1,0:T(8,128)S(1)}, f32[1,16,768]{2,1,0:T(8,128)S(1)}, f32...) custom-call(s32[8]{0:T(128)} %owner_ref.1, f32[8,16,768]{2,1,0:T(8,128)} %x_hbm.1), custom_call_target="tpu_custom_call" | custom-call | tf_op jit(solution)/shard_map/pallas_call | solution.py:324
  1.1 4.0 %collective-permute-start = (f32[4,16,768]{2,1,0:T(8,128)S(1)}, f32[4,16,768]{2,1,0:T(8,128)S(1)}, u32[]{:S(2)}, u32[]{:S(2)}) collective-permute-start(f32[4,16,768]{2,1,0:T(8,128)S(1)} %get-tuple-element.24), channel_id=1, source_target_pairs={{0,24},{4,28},{8,16},{12,20},{16,8},{20,12},{24,0},{28,4},{1,25},{... | collective-permute-start | bytes 589832 | tf_op jit(solution)/shard_map/ppermute | solution.py:352
  5.0 0.0 collective-permute-start.1
  5.0 0.5 %collective-permute-start.3 = (f32[3,16,768]{2,1,0:T(8,128)S(1)}, f32[3,16,768]{2,1,0:T(8,128)S(1)}, u32[]{:S(2)}, u32[]{:S(2)}) collective-permute-start(f32[3,16,768]{2,1,0:T(8,128)S(1)} %get-tuple-element.27), channel_id=1, source_target_pairs={{0,16},{4,20},{8,24},{12,28},{16,0},{20,4},{24,8},{28,12},{1,17},{... | collective-permute-start | bytes 442376 | tf_op jit(solution)/shard_map/ppermute | solution.py:352
  5.5 0.2 collective-permute-start.5
  5.8 1.4 %collective-permute-start.7 = (f32[1,16,768]{2,1,0:T(8,128)S(1)}, f32[1,16,768]{2,1,0:T(8,128)S(1)}, u32[]{:S(2)}, u32[]{:S(2)}) collective-permute-start(f32[1,16,768]{2,1,0:T(8,128)S(1)} %get-tuple-element.31), channel_id=1, source_target_pairs={{0,12},{4,8},{8,4},{12,0},{16,28},{20,24},{24,20},{28,16},{1,13},{... | collective-permute-start | bytes 147464 | tf_op jit(solution)/shard_map/ppermute | solution.py:359
  7.1 1.7 %collective-permute-start.8 = (f32[1,16,768]{2,1,0:T(8,128)S(1)}, f32[1,16,768]{2,1,0:T(8,128)S(1)}, u32[]{:S(2)}, u32[]{:S(2)}) collective-permute-start(f32[1,16,768]{2,1,0:T(8,128)S(1)} %get-tuple-element.32), channel_id=1, source_target_pairs={{0,20},{4,16},{8,28},{12,24},{16,4},{20,0},{24,12},{28,8},{1,21},{... | collective-permute-start | bytes 147464 | tf_op jit(solution)/shard_map/ppermute | solution.py:359
  8.8 1.7 %collective-permute-done.refs_0_ = f32[4,16,768]{2,1,0:T(8,128)S(1)} collective-permute-done((f32[4,16,768]{2,1,0:T(8,128)S(1)}, f32[4,16,768]{2,1,0:T(8,128)S(1)}, u32[]{:S(2)}, u32[]{:S(2)}) %collective-permute-start) | collective-permute-done | bytes 196640 | tf_op jit(solution)/shard_map/ppermute | solution.py:352
  10.5 2.7 %collective-permute-done.3.refs_2_ = f32[3,16,768]{2,1,0:T(8,128)S(1)} collective-permute-done((f32[3,16,768]{2,1,0:T(8,128)S(1)}, f32[3,16,768]{2,1,0:T(8,128)S(1)}, u32[]{:S(2)}, u32[]{:S(2)}) %collective-permute-start.3) | collective-permute-done | bytes 147488 | tf_op jit(solution)/shard_map/ppermute | solution.py:352
  13.1 0.0 collective-permute-start.4
  13.2 0.7 %collective-permute-done.5.refs_4_ = f32[3,16,768]{2,1,0:T(8,128)S(1)} collective-permute-done((f32[3,16,768]{2,1,0:T(8,128)S(1)}, f32[3,16,768]{2,1,0:T(8,128)S(1)}, u32[]{:S(2)}, u32[]{:S(2)}) %collective-permute-start.5) | collective-permute-done | bytes 147488 | tf_op jit(solution)/shard_map/ppermute | solution.py:352
  13.9 0.2 collective-permute-done.8.refs_1_
  14.1 0.0 copy-start.5
  14.1 0.0 copy-start
  14.1 0.0 copy-start.1
  14.2 0.0 copy-start.2
  14.2 0.0 copy-start.3
  14.2 0.0 copy-start.4
  14.2 0.3 collective-permute-done.4.refs_3_
  14.5 0.8 %collective-permute-done.6.refs_5_ = f32[3,16,768]{2,1,0:T(8,128)S(1)} collective-permute-done((f32[3,16,768]{2,1,0:T(8,128)S(1)}, f32[3,16,768]{2,1,0:T(8,128)S(1)}, u32[]{:S(2)}, u32[]{:S(2)}) %collective-permute-start.6) | collective-permute-done | bytes 147488 | tf_op jit(solution)/shard_map/ppermute | solution.py:22
  15.3 0.8 %shard_map.75 = (f32[168,128]{1,0:T(8,128)S(1)}, f32[168,128]{1,0:T(8,128)S(1)}, bf16[384,768]{1,0:T(8,128)(2,1)S(1)}, bf16[384,768]{1,0:T(8,128)(2,1)S(1)}) custom-call(f32[4,16,768]{2,1,0:T(8,128)S(1)} %collective-permute-done.refs_0_, f32[4,16,768]{2,1,0:T(8,128)S(1)} %collective-permute-done.2.refs_1_, f32[3,16,768]{2,1,0:T(8,128)S(1)} %collective-permute-done.3.refs_2_, ...), custom_call_target="tpu_custom_call" | custom-call | tf_op jit(solution)/shard_map/pallas_call | solution.py:397
  16.1 1.6 %collective-permute-start.9 = (f32[168,128]{1,0:T(8,128)S(1)}, f32[168,128]{1,0:T(8,128)S(1)}, u32[]{:S(2)}, u32[]{:S(2)}) collective-permute-start(f32[168,128]{1,0:T(8,128)S(1)} %get-tuple-element.34), channel_id=1, source_target_pairs={{0,1},{1,0},{2,3},{3,2},{4,5},{5,4},{6,7},{7,6},{8,9},{9,8},{10,11... | collective-permute-start | bytes 258056 | tf_op jit(solution)/shard_map/ppermute | solution.py:22
  17.8 1.2 %shard_map.76 = (bf16[384,384]{1,0:T(8,128)(2,1)S(1)}, bf16[384,384]{1,0:T(8,128)(2,1)S(1)}, bf16[384,256]{1,0:T(8,128)(2,1)S(1)}, f32[1152,384]{1,0:T(8,128)S(1)}) custom-call(s32[16]{0:T(128)S(1)} %copy-done.2, s32[16]{0:T(128)S(1)} %copy-done.3, s32[8]{0:T(128)S(1)} %copy-done.1, f32[8]{0:T(128)S(1)} %copy-done.4, f32[128,384]{1,0:T(8,128)S(1)} %copy-done, ...), custom_call_target="tpu_custom_call" | custom-call | tf_op jit(solution)/shard_map/pallas_call | solution.py:375
  19.0 1.7 %collective-permute-done.9 = f32[168,128]{1,0:T(8,128)S(1)} collective-permute-done((f32[168,128]{1,0:T(8,128)S(1)}, f32[168,128]{1,0:T(8,128)S(1)}, u32[]{:S(2)}, u32[]{:S(2)}) %collective-permute-start.9) | collective-permute-done | bytes 86048 | tf_op jit(solution)/shard_map/ppermute | solution.py:22
  20.8 2.7 %collective-permute-start.10 = (f32[168,128]{1,0:T(8,128)S(1)}, f32[168,128]{1,0:T(8,128)S(1)}, u32[]{:S(2)}, u32[]{:S(2)}) collective-permute-start(f32[168,128]{1,0:T(8,128)S(1)} %add.3.refs_0_), channel_id=1, source_target_pairs={{0,2},{1,3},{2,0},{3,1},{4,6},{5,7},{6,4},{7,5},{8,10},{9,11},{10,... | collective-permute-start | bytes 258056 | tf_op jit(solution)/shard_map/ppermute | solution.py:22
  23.4 1.4 %collective-permute-start.12 = (f32[168,128]{1,0:T(8,128)S(1)}, f32[168,128]{1,0:T(8,128)S(1)}, u32[]{:S(2)}, u32[]{:S(2)}) collective-permute-start(f32[168,128]{1,0:T(8,128)S(1)} %add.3.refs_0_), channel_id=1, source_target_pairs={{0,3},{1,2},{2,1},{3,0},{4,7},{5,6},{6,5},{7,4},{8,11},{9,10},{10,... | collective-permute-start | bytes 258056 | tf_op jit(solution)/shard_map/ppermute | solution.py:22
  24.8 0.2 collective-permute-start.11
  25.0 3.8 %collective-permute-done.10.refs_1_ = f32[168,128]{1,0:T(8,128)S(1)} collective-permute-done((f32[168,128]{1,0:T(8,128)S(1)}, f32[168,128]{1,0:T(8,128)S(1)}, u32[]{:S(2)}, u32[]{:S(2)}) %collective-permute-start.10) | collective-permute-done | bytes 86048 | tf_op jit(solution)/shard_map/ppermute | solution.py:22
  28.8 1.3 %shard_map.77.refs_4_ = f32[384,768]{1,0:T(8,128)S(1)} custom-call(f32[168,128]{1,0:T(8,128)S(1)} %add.3.refs_0_, f32[168,128]{1,0:T(8,128)S(1)} %collective-permute-done.10.refs_1_, bf16[384,384]{1,0:T(8,128)(2,1)S(1)} %get-tuple-element.37.refs_2_.refs_5_, bf16[384,384]{1,0:T(8,128)(2,1)S(1)} %get-tuple-element.38.refs_3_.refs_6_, ...), custom_call_target="tpu_custom_call" | custom-call | flops 1472200704 | tf_op jit(solution)/shard_map/pallas_call | solution.py:419
  30.1 0.1 collective-permute-done.12.refs_3_
  30.2 0.2 collective-permute-done.11.refs_2_
  30.4 2.7 %shard_map.78 = f32[384,768]{1,0:T(8,128)} custom-call(f32[168,128]{1,0:T(8,128)S(1)} %add.3.refs_0_, f32[168,128]{1,0:T(8,128)S(1)} %collective-permute-done.10.refs_1_, f32[168,128]{1,0:T(8,128)S(1)} %collective-permute-done.11.refs_2_, f32[168,128]{1,0:T(8,128)S(1)} %collective-permute-done.12.refs_3_, f32[384,768]{1,0:T(8,128)S(1)} %shard_map.77.refs_4_, ...), custom_call_target="tpu_custom_call" | custom-call | tf_op jit(solution)/shard_map/pallas_call | solution.py:428
  (14 shorter events, 0.0 us)
Async XLA Ops:
  1.1 9.4 %collective-permute-start = (f32[4,16,768]{2,1,0:T(8,128)S(1)}, f32[4,16,768]{2,1,0:T(8,128)S(1)}, u32[]{:S(2)}, u32[]{:S(2)}) collective-permute-start(f32[4,16,768]{2,1,0:T(8,128)S(1)} %get-tuple-element.24), channel_id=1, source_target_pairs={{0,24},{4,28},{8,16},{12,20},{16,8},{20,12},{24,0},{28,4},{1,25},{... | collective-permute-start | bytes 589832 | tf_op jit(solution)/shard_map/ppermute | solution.py:352
  5.0 2.1 %collective-permute-start.1 = (f32[3,16,768]{2,1,0:T(8,128)S(1)}, f32[3,16,768]{2,1,0:T(8,128)S(1)}, u32[]{:S(2)}, u32[]{:S(2)}) collective-permute-start(f32[3,16,768]{2,1,0:T(8,128)S(1)} %get-tuple-element.25), channel_id=1, source_target_pairs={{0,4},{4,0},{8,12},{12,8},{16,20},{20,16},{24,28},{28,24},{1,5},{5... | collective-permute-start | bytes 442376 | tf_op jit(solution)/shard_map/ppermute | solution.py:22
  5.0 8.1 %collective-permute-start.3 = (f32[3,16,768]{2,1,0:T(8,128)S(1)}, f32[3,16,768]{2,1,0:T(8,128)S(1)}, u32[]{:S(2)}, u32[]{:S(2)}) collective-permute-start(f32[3,16,768]{2,1,0:T(8,128)S(1)} %get-tuple-element.27), channel_id=1, source_target_pairs={{0,16},{4,20},{8,24},{12,28},{16,0},{20,4},{24,8},{28,12},{1,17},{... | collective-permute-start | bytes 442376 | tf_op jit(solution)/shard_map/ppermute | solution.py:352
  5.5 8.4 %collective-permute-start.5 = (f32[3,16,768]{2,1,0:T(8,128)S(1)}, f32[3,16,768]{2,1,0:T(8,128)S(1)}, u32[]{:S(2)}, u32[]{:S(2)}) collective-permute-start(f32[3,16,768]{2,1,0:T(8,128)S(1)} %get-tuple-element.28), channel_id=1, source_target_pairs={{0,8},{4,12},{8,0},{12,4},{16,24},{20,28},{24,16},{28,20},{1,9},{5... | collective-permute-start | bytes 442376 | tf_op jit(solution)/shard_map/ppermute | solution.py:352
  5.8 8.2 %collective-permute-start.7 = (f32[1,16,768]{2,1,0:T(8,128)S(1)}, f32[1,16,768]{2,1,0:T(8,128)S(1)}, u32[]{:S(2)}, u32[]{:S(2)}) collective-permute-start(f32[1,16,768]{2,1,0:T(8,128)S(1)} %get-tuple-element.31), channel_id=1, source_target_pairs={{0,12},{4,8},{8,4},{12,0},{16,28},{20,24},{24,20},{28,16},{1,13},{... | collective-permute-start | bytes 147464 | tf_op jit(solution)/shard_map/ppermute | solution.py:359
  7.1 7.0 %collective-permute-start.8 = (f32[1,16,768]{2,1,0:T(8,128)S(1)}, f32[1,16,768]{2,1,0:T(8,128)S(1)}, u32[]{:S(2)}, u32[]{:S(2)}) collective-permute-start(f32[1,16,768]{2,1,0:T(8,128)S(1)} %get-tuple-element.32), channel_id=1, source_target_pairs={{0,20},{4,16},{8,28},{12,24},{16,4},{20,0},{24,12},{28,8},{1,21},{... | collective-permute-start | bytes 147464 | tf_op jit(solution)/shard_map/ppermute | solution.py:359
  10.5 4.8 %collective-permute-start.2 = (f32[4,16,768]{2,1,0:T(8,128)S(1)}, f32[4,16,768]{2,1,0:T(8,128)S(1)}, u32[]{:S(2)}, u32[]{:S(2)}) collective-permute-start(f32[4,16,768]{2,1,0:T(8,128)S(1)} %collective-permute-done.refs_0_), channel_id=1, source_target_pairs={{0,4},{4,0},{8,12},{12,8},{16,20},{20,16},{24,28},{28,24},{1,5},{5... | collective-permute-start | bytes 589832 | tf_op jit(solution)/shard_map/ppermute | solution.py:22
  13.1 1.4 %collective-permute-start.4 = (f32[3,16,768]{2,1,0:T(8,128)S(1)}, f32[3,16,768]{2,1,0:T(8,128)S(1)}, u32[]{:S(2)}, u32[]{:S(2)}) collective-permute-start(f32[3,16,768]{2,1,0:T(8,128)S(1)} %collective-permute-done.3.refs_2_), channel_id=1, source_target_pairs={{0,4},{4,0},{8,12},{12,8},{16,20},{20,16},{24,28},{28,24},{1,5},{5... | collective-permute-start | bytes 442376 | tf_op jit(solution)/shard_map/ppermute | solution.py:22
  13.9 1.4 %collective-permute-start.6 = (f32[3,16,768]{2,1,0:T(8,128)S(1)}, f32[3,16,768]{2,1,0:T(8,128)S(1)}, u32[]{:S(2)}, u32[]{:S(2)}) collective-permute-start(f32[3,16,768]{2,1,0:T(8,128)S(1)} %collective-permute-done.5.refs_4_), channel_id=1, source_target_pairs={{0,4},{4,0},{8,12},{12,8},{16,20},{20,16},{24,28},{28,24},{1,5},{5... | collective-permute-start | bytes 442376 | tf_op jit(solution)/shard_map/ppermute | solution.py:22
  14.1 3.7 %copy-start.5 = (f32[384]{0:T(512)S(1)}, f32[384]{0:T(512)}, u32[]{:S(2)}) copy-start(f32[384]{0:T(512)} %param.13) | copy-start | bytes 4612
  14.1 3.6 %copy-start = (f32[128,384]{1,0:T(8,128)S(1)}, f32[128,384]{1,0:T(8,128)}, u32[]{:S(2)}) copy-start(f32[128,384]{1,0:T(8,128)} %coef_ref.1) | copy-start | bytes 589828
  14.1 3.6 %copy-start.1 = (s32[8]{0:T(128)S(1)}, s32[8]{0:T(128)}, u32[]{:S(2)}) copy-start(s32[8]{0:T(128)} %owner_ref.1) | copy-start | bytes 100
  14.2 3.6 %copy-start.2 = (s32[16]{0:T(128)S(1)}, s32[16]{0:T(128)}, u32[]{:S(2)}) copy-start(s32[16]{0:T(128)} %size_ref.1) | copy-start | bytes 196
  14.2 3.6 %copy-start.3 = (s32[16]{0:T(128)S(1)}, s32[16]{0:T(128)}, u32[]{:S(2)}) copy-start(s32[16]{0:T(128)} %shell_ref.1) | copy-start | bytes 196
  14.2 3.6 %copy-start.4 = (f32[8]{0:T(128)S(1)}, f32[8]{0:T(128)}, u32[]{:S(2)}) copy-start(f32[8]{0:T(128)} %energy_ref.1) | copy-start | bytes 100
  16.1 4.6 %collective-permute-start.9 = (f32[168,128]{1,0:T(8,128)S(1)}, f32[168,128]{1,0:T(8,128)S(1)}, u32[]{:S(2)}, u32[]{:S(2)}) collective-permute-start(f32[168,128]{1,0:T(8,128)S(1)} %get-tuple-element.34), channel_id=1, source_target_pairs={{0,1},{1,0},{2,3},{3,2},{4,5},{5,4},{6,7},{7,6},{8,9},{9,8},{10,11... | collective-permute-start | bytes 258056 | tf_op jit(solution)/shard_map/ppermute | solution.py:22
  20.8 8.1 %collective-permute-start.10 = (f32[168,128]{1,0:T(8,128)S(1)}, f32[168,128]{1,0:T(8,128)S(1)}, u32[]{:S(2)}, u32[]{:S(2)}) collective-permute-start(f32[168,128]{1,0:T(8,128)S(1)} %add.3.refs_0_), channel_id=1, source_target_pairs={{0,2},{1,3},{2,0},{3,1},{4,6},{5,7},{6,4},{7,5},{8,10},{9,11},{10,... | collective-permute-start | bytes 258056 | tf_op jit(solution)/shard_map/ppermute | solution.py:22
  23.4 6.8 %collective-permute-start.12 = (f32[168,128]{1,0:T(8,128)S(1)}, f32[168,128]{1,0:T(8,128)S(1)}, u32[]{:S(2)}, u32[]{:S(2)}) collective-permute-start(f32[168,128]{1,0:T(8,128)S(1)} %add.3.refs_0_), channel_id=1, source_target_pairs={{0,3},{1,2},{2,1},{3,0},{4,7},{5,6},{6,5},{7,4},{8,11},{9,10},{10,... | collective-permute-start | bytes 258056 | tf_op jit(solution)/shard_map/ppermute | solution.py:22
  24.8 5.6 %collective-permute-start.11 = (f32[168,128]{1,0:T(8,128)S(1)}, f32[168,128]{1,0:T(8,128)S(1)}, u32[]{:S(2)}, u32[]{:S(2)}) collective-permute-start(f32[168,128]{1,0:T(8,128)S(1)} %add.3.refs_0_), channel_id=1, source_target_pairs={{0,1},{1,0},{2,3},{3,2},{4,5},{5,4},{6,7},{7,6},{8,9},{9,8},{10,11... | collective-permute-start | bytes 258056 | tf_op jit(solution)/shard_map/ppermute | solution.py:22

commit v7 on v6

--- a/solution.py
+++ b/solution.py
@@ -369,7 +369,8 @@
         cost_estimate=pl.CostEstimate(flops=2 * 10**9, bytes_accessed=0, transcendentals=0),
     )(*rest)
     last = [(joined, [(row, 2, 2 * step + 1) for row, step in enumerate(range(1, chips - 1))])]
-    pieces = whole[4:6] + whole[2:4] + whole[:2] + own + last
+    farthest_first = [whole[2 * step - 2 + one] for step in range(chips - 1, 0, -1) for one in (0, 1)]
+    pieces = farthest_first + own + last
     operands, layout = zip(*pieces)
 
     left, right, back, gap = pl.pallas_call(
@@ -446,7 +447,7 @@
 def per_device(occupied_integrals, virtual_coefficients, *rest):
     blk_count = lax.axis_size("blk")
     slots, virt_count = virtual_coefficients.shape
-    paired = blk_count % 2 == 0 and blk_count == occupied_integrals.shape[0]
+    paired = blk_count % 2 == 0 and blk_count > 4 and blk_count == occupied_integrals.shape[0]
     parts = lax.axis_size("aux")
     shared = parts > 1 and parts & (parts - 1) == 0 and slots % 128 == 0 and slots <= virt_count
     run = slots_first if paired and shared else transformed_first

time: 33.3 us -> 33.3 us (level)
  no operation moved by 1% of the time
where the time goes in v7:
time: 33.3 us; the launch traced here: 33.2 us
  starting transfers between devices  13.6 us (41%)
  waiting for transfers between devices  12.2 us (37%)
  Pallas kernels  7.1 us (21%)
    ppermute x8, waiting for transfers between devices, swapped(): lax.ppermute(value, axis, [(i, i ^ step) for i in range(lax.axis_size(axi...  7 us
    ppermute x8, starting transfers between devices, swapped(): lax.ppermute(value, axis, [(i, i ^ step) for i in range(lax.axis_size(axi...  5.91 us
    ppermute x3, waiting for transfers between devices, slots_first(): piece = lax.ppermute(sent[2 * step], 'blk', ways[0])  5.06 us
    ppermute x3, starting transfers between devices, slots_first(): piece = lax.ppermute(sent[2 * step], 'blk', ways[0])  4.68 us
    ppermute x2, starting transfers between devices, slots_first(): other = lax.ppermute(sent[2 * step + 1], 'blk', ways[1])  3.05 us
    pallas_call x1, Pallas kernels, slots_first(): pl.pallas_call(functools.partial(last_density_kernel, len(evens)), out_sh...  2.71 us
    pallas_call x1, Pallas kernels, slots_first(): pl.pallas_call(first_density_kernel, out_shape=jax.ShapeDtypeStruct((virt...  1.26 us
    pallas_call x1, Pallas kernels, slots_first(): pl.pallas_call(functools.partial(coefficient_kernel, blk_count), out_shap...  1.21 us
  transfers between devices with their start and end apart: 13, of which 10 were waited for; matrix products, arithmetic and copies ran while one was open for 0% of the time, Pallas kernels for 7%

profile of v7, /device:TPU:0, one launch (start us, length us, event | category | flops | bytes accessed | tf_op | source)
XLA Modules:
  0.0 33.2 jit_solution(5789790011318073670)
XLA Ops:
  0.0 1.1 %shard_map.73 = (f32[3,16,768]{2,1,0:T(8,128)S(1)}, f32[3,16,768]{2,1,0:T(8,128)S(1)}, f32[3,16,768]{2,1,0:T(8,128)S(1)}, f32[1,16,768]{2,1,0:T(8,128)S(1)}, f32...) custom-call(s32[8]{0:T(128)} %owner_ref.1, f32[8,16,768]{2,1,0:T(8,128)} %x_hbm.1), custom_call_target="tpu_custom_call" | custom-call | tf_op jit(solution)/shard_map/pallas_call | solution.py:324
  1.1 4.0 %collective-permute-start = (f32[4,16,768]{2,1,0:T(8,128)S(1)}, f32[4,16,768]{2,1,0:T(8,128)S(1)}, u32[]{:S(2)}, u32[]{:S(2)}) collective-permute-start(f32[4,16,768]{2,1,0:T(8,128)S(1)} %get-tuple-element.24), channel_id=1, source_target_pairs={{0,24},{4,28},{8,16},{12,20},{16,8},{20,12},{24,0},{28,4},{1,25},{... | collective-permute-start | bytes 589832 | tf_op jit(solution)/shard_map/ppermute | solution.py:352
  5.0 0.0 collective-permute-start.1
  5.0 0.5 %collective-permute-start.3 = (f32[3,16,768]{2,1,0:T(8,128)S(1)}, f32[3,16,768]{2,1,0:T(8,128)S(1)}, u32[]{:S(2)}, u32[]{:S(2)}) collective-permute-start(f32[3,16,768]{2,1,0:T(8,128)S(1)} %get-tuple-element.27), channel_id=1, source_target_pairs={{0,16},{4,20},{8,24},{12,28},{16,0},{20,4},{24,8},{28,12},{1,17},{... | collective-permute-start | bytes 442376 | tf_op jit(solution)/shard_map/ppermute | solution.py:352
  5.5 0.2 collective-permute-start.5
  5.8 1.4 %collective-permute-start.7 = (f32[1,16,768]{2,1,0:T(8,128)S(1)}, f32[1,16,768]{2,1,0:T(8,128)S(1)}, u32[]{:S(2)}, u32[]{:S(2)}) collective-permute-start(f32[1,16,768]{2,1,0:T(8,128)S(1)} %get-tuple-element.31), channel_id=1, source_target_pairs={{0,12},{4,8},{8,4},{12,0},{16,28},{20,24},{24,20},{28,16},{1,13},{... | collective-permute-start | bytes 147464 | tf_op jit(solution)/shard_map/ppermute | solution.py:359
  7.1 1.7 %collective-permute-start.8 = (f32[1,16,768]{2,1,0:T(8,128)S(1)}, f32[1,16,768]{2,1,0:T(8,128)S(1)}, u32[]{:S(2)}, u32[]{:S(2)}) collective-permute-start(f32[1,16,768]{2,1,0:T(8,128)S(1)} %get-tuple-element.32), channel_id=1, source_target_pairs={{0,20},{4,16},{8,28},{12,24},{16,4},{20,0},{24,12},{28,8},{1,21},{... | collective-permute-start | bytes 147464 | tf_op jit(solution)/shard_map/ppermute | solution.py:359
  8.8 1.7 %collective-permute-done.refs_0_ = f32[4,16,768]{2,1,0:T(8,128)S(1)} collective-permute-done((f32[4,16,768]{2,1,0:T(8,128)S(1)}, f32[4,16,768]{2,1,0:T(8,128)S(1)}, u32[]{:S(2)}, u32[]{:S(2)}) %collective-permute-start) | collective-permute-done | bytes 196640 | tf_op jit(solution)/shard_map/ppermute | solution.py:352
  10.5 2.7 %collective-permute-done.3.refs_2_ = f32[3,16,768]{2,1,0:T(8,128)S(1)} collective-permute-done((f32[3,16,768]{2,1,0:T(8,128)S(1)}, f32[3,16,768]{2,1,0:T(8,128)S(1)}, u32[]{:S(2)}, u32[]{:S(2)}) %collective-permute-start.3) | collective-permute-done | bytes 147488 | tf_op jit(solution)/shard_map/ppermute | solution.py:352
  13.1 0.0 collective-permute-start.4
  13.2 0.7 %collective-permute-done.5.refs_4_ = f32[3,16,768]{2,1,0:T(8,128)S(1)} collective-permute-done((f32[3,16,768]{2,1,0:T(8,128)S(1)}, f32[3,16,768]{2,1,0:T(8,128)S(1)}, u32[]{:S(2)}, u32[]{:S(2)}) %collective-permute-start.5) | collective-permute-done | bytes 147488 | tf_op jit(solution)/shard_map/ppermute | solution.py:352
  13.9 0.2 collective-permute-done.8.refs_1_
  14.1 0.0 copy-start.5
  14.1 0.0 copy-start
  14.1 0.0 copy-start.1
  14.2 0.0 copy-start.2
  14.2 0.0 copy-start.3
  14.2 0.0 copy-start.4
  14.2 0.3 collective-permute-done.4.refs_3_
  14.5 0.8 %collective-permute-done.6.refs_5_ = f32[3,16,768]{2,1,0:T(8,128)S(1)} collective-permute-done((f32[3,16,768]{2,1,0:T(8,128)S(1)}, f32[3,16,768]{2,1,0:T(8,128)S(1)}, u32[]{:S(2)}, u32[]{:S(2)}) %collective-permute-start.6) | collective-permute-done | bytes 147488 | tf_op jit(solution)/shard_map/ppermute | solution.py:22
  15.3 0.8 %shard_map.75 = (f32[168,128]{1,0:T(8,128)S(1)}, f32[168,128]{1,0:T(8,128)S(1)}, bf16[384,768]{1,0:T(8,128)(2,1)S(1)}, bf16[384,768]{1,0:T(8,128)(2,1)S(1)}) custom-call(f32[4,16,768]{2,1,0:T(8,128)S(1)} %collective-permute-done.refs_0_, f32[4,16,768]{2,1,0:T(8,128)S(1)} %collective-permute-done.2.refs_1_, f32[3,16,768]{2,1,0:T(8,128)S(1)} %collective-permute-done.3.refs_2_, ...), custom_call_target="tpu_custom_call" | custom-call | tf_op jit(solution)/shard_map/pallas_call | solution.py:398
  16.1 1.6 %collective-permute-start.9 = (f32[168,128]{1,0:T(8,128)S(1)}, f32[168,128]{1,0:T(8,128)S(1)}, u32[]{:S(2)}, u32[]{:S(2)}) collective-permute-start(f32[168,128]{1,0:T(8,128)S(1)} %get-tuple-element.34), channel_id=1, source_target_pairs={{0,1},{1,0},{2,3},{3,2},{4,5},{5,4},{6,7},{7,6},{8,9},{9,8},{10,11... | collective-permute-start | bytes 258056 | tf_op jit(solution)/shard_map/ppermute | solution.py:22
  17.8 1.2 %shard_map.76 = (bf16[384,384]{1,0:T(8,128)(2,1)S(1)}, bf16[384,384]{1,0:T(8,128)(2,1)S(1)}, bf16[384,256]{1,0:T(8,128)(2,1)S(1)}, f32[1152,384]{1,0:T(8,128)S(1)}) custom-call(s32[16]{0:T(128)S(1)} %copy-done.2, s32[16]{0:T(128)S(1)} %copy-done.3, s32[8]{0:T(128)S(1)} %copy-done.1, f32[8]{0:T(128)S(1)} %copy-done.4, f32[128,384]{1,0:T(8,128)S(1)} %copy-done, ...), custom_call_target="tpu_custom_call" | custom-call | tf_op jit(solution)/shard_map/pallas_call | solution.py:376
  19.0 1.7 %collective-permute-done.9 = f32[168,128]{1,0:T(8,128)S(1)} collective-permute-done((f32[168,128]{1,0:T(8,128)S(1)}, f32[168,128]{1,0:T(8,128)S(1)}, u32[]{:S(2)}, u32[]{:S(2)}) %collective-permute-start.9) | collective-permute-done | bytes 86048 | tf_op jit(solution)/shard_map/ppermute | solution.py:22
  20.8 2.7 %collective-permute-start.10 = (f32[168,128]{1,0:T(8,128)S(1)}, f32[168,128]{1,0:T(8,128)S(1)}, u32[]{:S(2)}, u32[]{:S(2)}) collective-permute-start(f32[168,128]{1,0:T(8,128)S(1)} %add.3.refs_0_), channel_id=1, source_target_pairs={{0,2},{1,3},{2,0},{3,1},{4,6},{5,7},{6,4},{7,5},{8,10},{9,11},{10,... | collective-permute-start | bytes 258056 | tf_op jit(solution)/shard_map/ppermute | solution.py:22
  23.4 1.4 %collective-permute-start.12 = (f32[168,128]{1,0:T(8,128)S(1)}, f32[168,128]{1,0:T(8,128)S(1)}, u32[]{:S(2)}, u32[]{:S(2)}) collective-permute-start(f32[168,128]{1,0:T(8,128)S(1)} %add.3.refs_0_), channel_id=1, source_target_pairs={{0,3},{1,2},{2,1},{3,0},{4,7},{5,6},{6,5},{7,4},{8,11},{9,10},{10,... | collective-permute-start | bytes 258056 | tf_op jit(solution)/shard_map/ppermute | solution.py:22
  24.8 0.2 collective-permute-start.11
  25.0 3.8 %collective-permute-done.10.refs_1_ = f32[168,128]{1,0:T(8,128)S(1)} collective-permute-done((f32[168,128]{1,0:T(8,128)S(1)}, f32[168,128]{1,0:T(8,128)S(1)}, u32[]{:S(2)}, u32[]{:S(2)}) %collective-permute-start.10) | collective-permute-done | bytes 86048 | tf_op jit(solution)/shard_map/ppermute | solution.py:22
  28.8 1.3 %shard_map.77.refs_4_ = f32[384,768]{1,0:T(8,128)S(1)} custom-call(f32[168,128]{1,0:T(8,128)S(1)} %add.3.refs_0_, f32[168,128]{1,0:T(8,128)S(1)} %collective-permute-done.10.refs_1_, bf16[384,384]{1,0:T(8,128)(2,1)S(1)} %get-tuple-element.37.refs_2_.refs_5_, bf16[384,384]{1,0:T(8,128)(2,1)S(1)} %get-tuple-element.38.refs_3_.refs_6_, ...), custom_call_target="tpu_custom_call" | custom-call | flops 1472200704 | tf_op jit(solution)/shard_map/pallas_call | solution.py:420
  30.1 0.1 collective-permute-done.12.refs_3_
  30.2 0.2 collective-permute-done.11.refs_2_
  30.4 2.7 %shard_map.78 = f32[384,768]{1,0:T(8,128)} custom-call(f32[168,128]{1,0:T(8,128)S(1)} %add.3.refs_0_, f32[168,128]{1,0:T(8,128)S(1)} %collective-permute-done.10.refs_1_, f32[168,128]{1,0:T(8,128)S(1)} %collective-permute-done.11.refs_2_, f32[168,128]{1,0:T(8,128)S(1)} %collective-permute-done.12.refs_3_, f32[384,768]{1,0:T(8,128)S(1)} %shard_map.77.refs_4_, ...), custom_call_target="tpu_custom_call" | custom-call | tf_op jit(solution)/shard_map/pallas_call | solution.py:429
  (14 shorter events, 0.0 us)
Async XLA Ops:
  1.1 9.4 %collective-permute-start = (f32[4,16,768]{2,1,0:T(8,128)S(1)}, f32[4,16,768]{2,1,0:T(8,128)S(1)}, u32[]{:S(2)}, u32[]{:S(2)}) collective-permute-start(f32[4,16,768]{2,1,0:T(8,128)S(1)} %get-tuple-element.24), channel_id=1, source_target_pairs={{0,24},{4,28},{8,16},{12,20},{16,8},{20,12},{24,0},{28,4},{1,25},{... | collective-permute-start | bytes 589832 | tf_op jit(solution)/shard_map/ppermute | solution.py:352
  5.0 2.1 %collective-permute-start.1 = (f32[3,16,768]{2,1,0:T(8,128)S(1)}, f32[3,16,768]{2,1,0:T(8,128)S(1)}, u32[]{:S(2)}, u32[]{:S(2)}) collective-permute-start(f32[3,16,768]{2,1,0:T(8,128)S(1)} %get-tuple-element.25), channel_id=1, source_target_pairs={{0,4},{4,0},{8,12},{12,8},{16,20},{20,16},{24,28},{28,24},{1,5},{5... | collective-permute-start | bytes 442376 | tf_op jit(solution)/shard_map/ppermute | solution.py:22
  5.0 8.1 %collective-permute-start.3 = (f32[3,16,768]{2,1,0:T(8,128)S(1)}, f32[3,16,768]{2,1,0:T(8,128)S(1)}, u32[]{:S(2)}, u32[]{:S(2)}) collective-permute-start(f32[3,16,768]{2,1,0:T(8,128)S(1)} %get-tuple-element.27), channel_id=1, source_target_pairs={{0,16},{4,20},{8,24},{12,28},{16,0},{20,4},{24,8},{28,12},{1,17},{... | collective-permute-start | bytes 442376 | tf_op jit(solution)/shard_map/ppermute | solution.py:352
  5.5 8.4 %collective-permute-start.5 = (f32[3,16,768]{2,1,0:T(8,128)S(1)}, f32[3,16,768]{2,1,0:T(8,128)S(1)}, u32[]{:S(2)}, u32[]{:S(2)}) collective-permute-start(f32[3,16,768]{2,1,0:T(8,128)S(1)} %get-tuple-element.28), channel_id=1, source_target_pairs={{0,8},{4,12},{8,0},{12,4},{16,24},{20,28},{24,16},{28,20},{1,9},{5... | collective-permute-start | bytes 442376 | tf_op jit(solution)/shard_map/ppermute | solution.py:352
  5.8 8.2 %collective-permute-start.7 = (f32[1,16,768]{2,1,0:T(8,128)S(1)}, f32[1,16,768]{2,1,0:T(8,128)S(1)}, u32[]{:S(2)}, u32[]{:S(2)}) collective-permute-start(f32[1,16,768]{2,1,0:T(8,128)S(1)} %get-tuple-element.31), channel_id=1, source_target_pairs={{0,12},{4,8},{8,4},{12,0},{16,28},{20,24},{24,20},{28,16},{1,13},{... | collective-permute-start | bytes 147464 | tf_op jit(solution)/shard_map/ppermute | solution.py:359
  7.1 7.0 %collective-permute-start.8 = (f32[1,16,768]{2,1,0:T(8,128)S(1)}, f32[1,16,768]{2,1,0:T(8,128)S(1)}, u32[]{:S(2)}, u32[]{:S(2)}) collective-permute-start(f32[1,16,768]{2,1,0:T(8,128)S(1)} %get-tuple-element.32), channel_id=1, source_target_pairs={{0,20},{4,16},{8,28},{12,24},{16,4},{20,0},{24,12},{28,8},{1,21},{... | collective-permute-start | bytes 147464 | tf_op jit(solution)/shard_map/ppermute | solution.py:359
  10.5 4.8 %collective-permute-start.2 = (f32[4,16,768]{2,1,0:T(8,128)S(1)}, f32[4,16,768]{2,1,0:T(8,128)S(1)}, u32[]{:S(2)}, u32[]{:S(2)}) collective-permute-start(f32[4,16,768]{2,1,0:T(8,128)S(1)} %collective-permute-done.refs_0_), channel_id=1, source_target_pairs={{0,4},{4,0},{8,12},{12,8},{16,20},{20,16},{24,28},{28,24},{1,5},{5... | collective-permute-start | bytes 589832 | tf_op jit(solution)/shard_map/ppermute | solution.py:22
  13.1 1.4 %collective-permute-start.4 = (f32[3,16,768]{2,1,0:T(8,128)S(1)}, f32[3,16,768]{2,1,0:T(8,128)S(1)}, u32[]{:S(2)}, u32[]{:S(2)}) collective-permute-start(f32[3,16,768]{2,1,0:T(8,128)S(1)} %collective-permute-done.3.refs_2_), channel_id=1, source_target_pairs={{0,4},{4,0},{8,12},{12,8},{16,20},{20,16},{24,28},{28,24},{1,5},{5... | collective-permute-start | bytes 442376 | tf_op jit(solution)/shard_map/ppermute | solution.py:22
  13.9 1.4 %collective-permute-start.6 = (f32[3,16,768]{2,1,0:T(8,128)S(1)}, f32[3,16,768]{2,1,0:T(8,128)S(1)}, u32[]{:S(2)}, u32[]{:S(2)}) collective-permute-start(f32[3,16,768]{2,1,0:T(8,128)S(1)} %collective-permute-done.5.refs_4_), channel_id=1, source_target_pairs={{0,4},{4,0},{8,12},{12,8},{16,20},{20,16},{24,28},{28,24},{1,5},{5... | collective-permute-start | bytes 442376 | tf_op jit(solution)/shard_map/ppermute | solution.py:22
  14.1 3.7 %copy-start.5 = (f32[384]{0:T(512)S(1)}, f32[384]{0:T(512)}, u32[]{:S(2)}) copy-start(f32[384]{0:T(512)} %param.13) | copy-start | bytes 4612
  14.1 3.6 %copy-start = (f32[128,384]{1,0:T(8,128)S(1)}, f32[128,384]{1,0:T(8,128)}, u32[]{:S(2)}) copy-start(f32[128,384]{1,0:T(8,128)} %coef_ref.1) | copy-start | bytes 589828
  14.1 3.6 %copy-start.1 = (s32[8]{0:T(128)S(1)}, s32[8]{0:T(128)}, u32[]{:S(2)}) copy-start(s32[8]{0:T(128)} %owner_ref.1) | copy-start | bytes 100
  14.2 3.6 %copy-start.2 = (s32[16]{0:T(128)S(1)}, s32[16]{0:T(128)}, u32[]{:S(2)}) copy-start(s32[16]{0:T(128)} %size_ref.1) | copy-start | bytes 196
  14.2 3.6 %copy-start.3 = (s32[16]{0:T(128)S(1)}, s32[16]{0:T(128)}, u32[]{:S(2)}) copy-start(s32[16]{0:T(128)} %shell_ref.1) | copy-start | bytes 196
  14.2 3.6 %copy-start.4 = (f32[8]{0:T(128)S(1)}, f32[8]{0:T(128)}, u32[]{:S(2)}) copy-start(f32[8]{0:T(128)} %energy_ref.1) | copy-start | bytes 100
  16.1 4.6 %collective-permute-start.9 = (f32[168,128]{1,0:T(8,128)S(1)}, f32[168,128]{1,0:T(8,128)S(1)}, u32[]{:S(2)}, u32[]{:S(2)}) collective-permute-start(f32[168,128]{1,0:T(8,128)S(1)} %get-tuple-element.34), channel_id=1, source_target_pairs={{0,1},{1,0},{2,3},{3,2},{4,5},{5,4},{6,7},{7,6},{8,9},{9,8},{10,11... | collective-permute-start | bytes 258056 | tf_op jit(solution)/shard_map/ppermute | solution.py:22
  20.8 8.1 %collective-permute-start.10 = (f32[168,128]{1,0:T(8,128)S(1)}, f32[168,128]{1,0:T(8,128)S(1)}, u32[]{:S(2)}, u32[]{:S(2)}) collective-permute-start(f32[168,128]{1,0:T(8,128)S(1)} %add.3.refs_0_), channel_id=1, source_target_pairs={{0,2},{1,3},{2,0},{3,1},{4,6},{5,7},{6,4},{7,5},{8,10},{9,11},{10,... | collective-permute-start | bytes 258056 | tf_op jit(solution)/shard_map/ppermute | solution.py:22
  23.4 6.8 %collective-permute-start.12 = (f32[168,128]{1,0:T(8,128)S(1)}, f32[168,128]{1,0:T(8,128)S(1)}, u32[]{:S(2)}, u32[]{:S(2)}) collective-permute-start(f32[168,128]{1,0:T(8,128)S(1)} %add.3.refs_0_), channel_id=1, source_target_pairs={{0,3},{1,2},{2,1},{3,0},{4,7},{5,6},{6,5},{7,4},{8,11},{9,10},{10,... | collective-permute-start | bytes 258056 | tf_op jit(solution)/shard_map/ppermute | solution.py:22
  24.8 5.6 %collective-permute-start.11 = (f32[168,128]{1,0:T(8,128)S(1)}, f32[168,128]{1,0:T(8,128)S(1)}, u32[]{:S(2)}, u32[]{:S(2)}) collective-permute-start(f32[168,128]{1,0:T(8,128)S(1)} %add.3.refs_0_), channel_id=1, source_target_pairs={{0,1},{1,0},{2,3},{3,2},{4,5},{5,4},{6,7},{7,6},{8,9},{9,8},{10,11... | collective-permute-start | bytes 258056 | tf_op jit(solution)/shard_map/ppermute | solution.py:22
